TPU v7x, 256 devices: a whole 4x4x8 slice. The times are simulated.
256 devices in a mesh: mp: 4 (over y), seq: 16 (over x, z_lo, core), dp: 4 (over z_hi).
Axes of the slice: x: 4, y: 4, z: 8 (z_hi: 4, z_lo: 2; z = z_hi * 2 + z_lo), core: 2. Of those that a mesh axis runs over, the one named last changes fastest.
Arguments:
- gen_features: bfloat16 [4, 2048, 3072], P('dp', 'seq'), may hold values from -6 to 6
- gen_gain: bfloat16 [3072], replicated, may hold values from 0.5 to 1.5
- gen_weight: bfloat16 [3072, 64], replicated, may hold values from -0.109375 to 0.109375
- flow_noise: bfloat16 [4, 2048, 64], P('dp', 'seq'), may hold values from -133 to 133
- time_steps: int32 [4], P('dp'), may hold values from 0 to 999
- embed_weight: bfloat16 [2, 64, 3072], replicated, may hold values from -0.75 to 0.75
- norm_gain: bfloat16 [2, 3072], replicated, may hold values from 0.5 to 1.5
- qkv_weight: bfloat16 [2, 3072, 3, 2048], P(None, None, None, 'seq'), may hold values from -0.109375 to 0.109375
- qk_gain: bfloat16 [2, 2, 128], replicated, may hold values from 0.5 to 1.5
- out_weight: bfloat16 [2, 2048, 64], replicated, may hold values from -0.125 to 0.125
Outputs:
- dmd_grad: float32 [4, 2048, 64], P('dp', 'seq')
- gen_grad: float32 [3072, 64], P('seq')
All inputs are finite; a program needn't handle non-finite values.
Results may differ from a plain program's by a relative error of at most 0.0065.
Values may be sent and summed in bfloat16 or wider, within the bound.
No kernel may reach another device: no remote copies, remote signals or barrier semaphores. Data moves between devices by JAX's collectives and lax.ppermute only.
A program may use at most 128 MiB of HBM per device.

v0:
```python
import math

import jax
import jax.numpy as jnp
from jax import lax
from jax.sharding import PartitionSpec as P

STEPS = 1000


def rms_scale(values, gain):
    mean_square = jnp.mean(values * values, axis=-1, keepdims=True)
    return values * lax.rsqrt(mean_square + 1e-06) * gain.astype(jnp.float32)


def time_embedding(step_value, width):
    half_width = width // 2
    ranks = jnp.arange(half_width).astype(jnp.float32) / half_width
    frequency = jnp.exp(-math.log(10000.0) * ranks)
    phases = step_value * frequency
    return jnp.concatenate([jnp.cos(phases), jnp.sin(phases)])


def head_norm(projected, gain, heads_here, head_dim):
    shaped = projected.reshape(projected.shape[0], heads_here, head_dim)
    return (
        rms_scale(shaped, gain)
        .astype(jnp.bfloat16)
        .reshape(projected.shape[0], heads_here * head_dim)
    )


def attend(query_rows, key_rows, value_rows, heads_here, head_dim):
    query_count = query_rows.shape[0]
    block_rows = 512
    key_heads = key_rows.reshape(key_rows.shape[0], heads_here, head_dim)
    value_heads = value_rows.reshape(value_rows.shape[0], heads_here, head_dim)
    divisor = math.sqrt(head_dim)

    def one_block(query_block):
        query_heads = query_block.reshape(block_rows, heads_here, head_dim)
        scores = (
            jnp.einsum("qhd,khd->hqk", query_heads, key_heads, preferred_element_type=jnp.float32)
            / divisor
        )
        weights = jnp.exp(scores)
        shares = (weights / jnp.sum(weights, axis=2, keepdims=True)).astype(jnp.bfloat16)
        mixed = jnp.einsum("hqk,khd->qhd", shares, value_heads, preferred_element_type=jnp.float32)
        return mixed.astype(jnp.bfloat16).reshape(block_rows, heads_here * head_dim)

    blocks = query_rows.reshape(query_count // block_rows, block_rows, heads_here * head_dim)
    return lax.map(one_block, blocks).reshape(query_count, heads_here * head_dim)


def per_device(
    gen_features,
    gen_gain,
    gen_weight,
    flow_noise,
    time_steps,
    embed_weight,
    norm_gain,
    qkv_weight,
    qk_gain,
    out_weight,
):
    seq_count = lax.axis_size("seq")
    slot_index = lax.axis_index("mp")
    model_index = slot_index % 2
    half_index = slot_index // 2
    features = gen_features[0]
    tok_rows = features.shape[0]
    half_rows = tok_rows // 2
    width = features.shape[1]
    channels = gen_weight.shape[1]
    features_f = features.astype(jnp.float32)
    inv_rms = lax.rsqrt(jnp.sum(features_f * features_f, axis=1) / width + 1e-06)
    scaled = (features_f * gen_gain.astype(jnp.float32)).astype(jnp.bfloat16)
    clean = jnp.dot(scaled, gen_weight, preferred_element_type=jnp.float32) * inv_rms[:, None]
    step_value = time_steps[0].astype(jnp.float32)
    level = (step_value + 1.0) / (STEPS + 1.0)
    noisy = (1.0 - level) * clean + level * flow_noise[0].astype(jnp.float32)
    noisy_bf = noisy.astype(jnp.bfloat16)
    every_noisy = lax.all_gather(noisy_bf, "seq", axis=0, tiled=True)
    embed_sel = lax.dynamic_index_in_dim(embed_weight, model_index, 0, keepdims=False)
    norm_sel = lax.dynamic_index_in_dim(norm_gain, model_index, 0, keepdims=False)
    qkv_sel = lax.dynamic_index_in_dim(qkv_weight, model_index, 0, keepdims=False)
    gain_sel = lax.dynamic_index_in_dim(qk_gain, model_index, 0, keepdims=False)
    out_sel = lax.dynamic_index_in_dim(out_weight, model_index, 0, keepdims=False)
    head_dim = gain_sel.shape[1]
    local_width = qkv_sel.shape[2]
    heads_here = local_width // head_dim
    temb = time_embedding(step_value, width)
    hidden = jnp.dot(every_noisy, embed_sel, preferred_element_type=jnp.float32) + temb
    normed = rms_scale(hidden, norm_sel).astype(jnp.bfloat16)
    pair_weight = qkv_sel[:, 1:].reshape(width, 2 * local_width)
    pair_proj = jnp.dot(normed, pair_weight, preferred_element_type=jnp.float32).reshape(
        normed.shape[0], 2, local_width
    )
    key_rows = head_norm(pair_proj[:, 0], gain_sel[1], heads_here, head_dim)
    value_rows = pair_proj[:, 1].astype(jnp.bfloat16)
    grouped = normed.reshape((seq_count, tok_rows) + normed.shape[1:])
    picked = lax.dynamic_slice_in_dim(grouped, half_index * half_rows, half_rows, 1)
    query_proj = jnp.dot(
        picked.reshape((seq_count * half_rows,) + normed.shape[1:]),
        qkv_sel[:, 0],
        preferred_element_type=jnp.float32,
    )
    query_rows = head_norm(query_proj, gain_sel[0], heads_here, head_dim)
    attended = attend(query_rows, key_rows, value_rows, heads_here, head_dim)
    token_heads = lax.all_to_all(attended, "seq", split_axis=0, concat_axis=1, tiled=True)
    velocity = jnp.dot(token_heads, out_sel, preferred_element_type=jnp.float32)
    own_noisy = lax.dynamic_slice_in_dim(noisy, half_index * half_rows, half_rows, 0)
    predicted = own_noisy - level * velocity
    every_pred = lax.all_gather(predicted[None], "mp", axis=0, tiled=True)
    real_pred = every_pred[0::2].reshape(tok_rows, channels)
    fake_pred = every_pred[1::2].reshape(tok_rows, channels)
    gap = fake_pred - real_pred
    direction = (gap * inv_rms[:, None]).astype(jnp.bfloat16)
    spread = jnp.sum(jnp.abs(clean - real_pred))
    cell_count = tok_rows * seq_count * channels
    partial_value = jnp.dot(scaled.T, direction, preferred_element_type=jnp.float32)
    total, spread_all = lax.psum((partial_value, spread), "seq")
    weight = spread_all / cell_count + 1e-05
    summed = lax.psum(total / weight, "dp")
    rows_here = summed.shape[0] // seq_count
    grad_rows = lax.dynamic_slice_in_dim(summed, lax.axis_index("seq") * rows_here, rows_here, 0)
    return ((gap / weight)[None], grad_rows)


def solution(mesh):
    placed = (
        P("dp", "seq", None),
        P(),
        P(),
        P("dp", "seq", None),
        P("dp"),
        P(),
        P(),
        P(None, None, None, "seq"),
        P(),
        P(),
    )
    return jax.shard_map(
        per_device,
        mesh=mesh,
        in_specs=placed,
        out_specs=(P("dp", "seq", None), P("seq", None)),
        check_vma=False,
    )
```

profile of v0, /device:TPU:32, one launch (start us, length us, event | category | flops | bytes accessed | tf_op | source)
XLA Modules:
  0.0 322.2 jit_solution(3444769131018072422)
XLA Ops:
  8.0 0.7 convert_element_type.80
  8.7 1.4 fusion.17
  10.1 1.7 fusion.39
  11.8 18.8 %all_gather.6 = bf16[2048,64]{0,1:T(8,128)(2,1)S(1)} all-gather(bf16[128,64]{0,1:T(8,128)(2,1)S(1)} %get-tuple-element.60), channel_id=1, replica_groups=mesh['mp'=4,'seq'=16,'dp'=4] {'seq'}, dimensions={0}, use_global_device_ids=true | all-gather | bytes 278528 | tf_op jit(solution)/shard_map/all_gather | solution.py:84
  30.6 10.1 %multiply_reduce_fusion = (f32[2048]{0:T(1024)S(1)}, f32[2048,3072]{1,0:T(8,128)}) fusion(f32[3072]{0:T(1024)S(1)} %pad_maximum_fusion, bf16[2048,64]{0,1:T(8,128)(2,1)S(1)} %all_gather.6, bf16[2,64,3072]{2,1,0:T(8,128)(2,1)S(1)} %copy-done, s32[]{:T(128)S(6)} %select_n.33), kind=kOutput, calls=%fused_computation.15 | convolution fusion | flops 824178688 | bytes 25841668 | tf_op jit(solution)/shard_map/dot_general | solution.py:94
  40.7 0.2 dynamic-slice_bitcast_fusion
  40.9 1.5 copy-done.3
  42.5 1.6 copy.25
  44.1 10.6 %multiply_convert_fusion = bf16[2048,3072]{1,0:T(8,128)(2,1)S(1)} fusion(f32[2048,3072]{1,0:T(8,128)} %get-tuple-element.72, f32[3072]{0:T(1024)S(1)} %bitcast.112, f32[2048]{0:T(1024)S(1)} %add_rsqrt_fusion.1, f32[3072]{0:T(1024)S(1)} %pad_maximum_fusion), kind=kLoop, calls=%fused_computation.14 | loop fusion | flops 25165824 | bytes 37781504 | tf_op jit(solution)/shard_map/convert_element_type | solution.py:95
  54.7 3.5 %fusion.12 = f32[2048,2,128]{0,2,1:T(8,128)S(1)} fusion(bf16[2048,3072]{1,0:T(8,128)(2,1)S(1)} %multiply_convert_fusion, bf16[3072,2,128]{0,2,1:T(8,128)(2,1)S(1)} %copy-done.5), kind=kOutput, calls=%fused_computation.16 | convolution fusion | flops 3221225472 | bytes 16252928 | tf_op jit(solution)/shard_map/dot_general | solution.py:97
  58.1 1.1 copy-done.2
  59.6 0.3 copy.26
  59.9 3.2 %constant_dynamic-slice_fusion.1 = bf16[16,64,3072]{2,1,0:T(8,128)(2,1)S(1)} fusion(bf16[16,128,3072]{2,1,0:T(8,128)(2,1)} %bitcast.106, s32[]{:T(128)S(6)} %select_n.31), kind=kLoop, calls=%fused_computation.63 | loop fusion | bytes 12582916 | tf_op jit(solution)/shard_map/dynamic_slice | solution.py:103
  63.1 3.0 multiply_reduce_fusion.2
  66.1 0.3 copy.27
  66.4 0.2 multiply_convert_fusion.2
  66.6 4.7 %while.10 = (s32[]{:T(128)}, bf16[2,512,128]{2,1,0:T(8,128)(2,1)}, bf16[2,512,128]{2,1,0:T(8,128)(2,1)S(1)}, bf16[2048,1,128]{2,0,1:T(8,128)(2,1)S(1)}, bf16[2048,1,128]{2,0,1:T(8,128)(2,1)S(1)}, /*index=5*/s32[]{:T(128)}) while((s32[]{:T(128)}, bf16[2,512,128]{2,1,0:T(8,128)(2,1)}, bf16[2,512,128]{2,1,0:T(8,128)(2,1)S(1)}, ...), condition=%wide.region_6.7_spmd, body=%wide.region_4.6_spmd.sunk | while | flops 542178816 | bytes 9704009 | solution.py:52
  66.7 0.8 fusion.50
  67.5 1.5 fusion.51
  69.0 0.8 fusion.50
  69.8 1.5 fusion.51
  71.4 12.8 %all_to_all.19 = bf16[16,64,128]{2,1,0:T(8,128)(2,1)S(1)} all-to-all(bf16[16,64,128]{2,1,0:T(8,128)(2,1)} %bitcast.23), channel_id=1, replica_groups=mesh['mp'=4,'seq'=16,'dp'=4] {'seq'}, dimensions={0} | all-to-all | bytes 524288 | tf_op jit(solution)/shard_map/all_to_all | solution.py:111
  84.2 0.2 fusion.20
  84.5 12.5 %all-gather = f32[256,64]{1,0:T(8,128)S(1)} all-gather(f32[64,64]{1,0:T(8,128)S(1)} %copy.30), channel_id=2, replica_groups=mesh['mp'=4,'seq'=16,'dp'=4] {'mp'}, dimensions={0}, use_global_device_ids=true | all-gather | bytes 81920 | tf_op jit(solution)/shard_map/all_gather | solution.py:115
  97.2 0.6 abs_reduce_fusion
  97.9 24.8 %psum.21 = f32[]{:T(128)} all-reduce(f32[]{:T(128)} %abs_reduce_fusion), channel_id=1, replica_groups=mesh['mp'=4,'seq'=16,'dp'=4] {'seq'}, use_global_device_ids=true, to_apply=%region_8.9 | all-reduce | flops 1 | bytes 8 | tf_op jit(solution)/shard_map/psum | solution.py:123
  123.6 1.2 fusion.22
  124.8 122.9 %all-reduce.3.cloned.1.call-done = f32[3072,64]{0,1:T(8,128)} async-done(((f32[3072,64]{0,1:T(8,128)}), f32[3072,64]{0,1:T(8,128)}) %all-reduce.3.cloned.1.call-update) | async-done | bytes 786448 | tf_op jit(solution)/shard_map/psum | solution.py:123
  247.8 2.1 broadcast_divide_fusion
  249.9 0.7 div.89
  250.6 63.1 %all-reduce.5.cloned.1.call-done = f32[3072,64]{0,1:T(8,128)} async-done(((f32[3072,64]{0,1:T(8,128)}), f32[3072,64]{0,1:T(8,128)}) %all-reduce.5.cloned.1.call-update) | async-done | bytes 786448 | tf_op jit(solution)/shard_map/psum | solution.py:125
  313.7 1.6 constant_dynamic-slice_fusion.2
  (47 shorter events, 1.3 us)
Async XLA Ops:
  7.2 23.4 %copy-start = (bf16[2,64,3072]{2,1,0:T(8,128)(2,1)S(1)}, bf16[2,64,3072]{2,1,0:T(8,128)(2,1)}, u32[]{:S(2)}) copy-start(bf16[2,64,3072]{2,1,0:T(8,128)(2,1)} %param.17) | copy-start | bytes 2359300
  7.2 240.6 %all-reduce.3.cloned.1.call-start = ((), (), s32[]{:S(2)}) async-start(), calls=%async_computation.1 | async-start | bytes 1572864 | tf_op jit(solution)/shard_map/psum | solution.py:123
  11.8 28.9 %slice-start = ((s8[4718592]{0:T(1024)(128)(4,1)}), s8[524288]{0:T(1024)(128)(4,1)S(1)}, s32[]{:S(2)}) async-start(s8[4718592]{0:T(1024)(128)(4,1)} %bitcast.109), calls=%async_computation.3 | async-start | bytes 1048576
  30.6 10.1 %copy-start.7 = (bf16[2,3072]{1,0:T(2,128)(2,1)S(1)}, bf16[2,3072]{1,0:T(2,128)(2,1)}, u32[]{:S(2)}) copy-start(bf16[2,3072]{1,0:T(2,128)(2,1)} %param.18) | copy-start | bytes 36868
  30.6 10.1 %slice-start.1 = ((s8[4718592]{0:T(1024)(128)(4,1)}), s8[4194304]{0:T(1024)(128)(4,1)S(1)}, s32[]{:S(2)}) async-start(s8[4718592]{0:T(1024)(128)(4,1)} %bitcast.109), calls=%async_computation.4 | async-start | bytes 8388608
  40.9 1.5 copy-start.3
  44.1 10.6 %copy-start.5 = (bf16[3072,2,128]{0,2,1:T(8,128)(2,1)S(1)}, bf16[3072,2,128]{0,2,1:T(8,128)(2,1)}, u32[]{:S(2)}) copy-start(bf16[3072,2,128]{0,2,1:T(8,128)(2,1)} %copy.25) | copy-start | bytes 4718596
  54.6 4.6 %copy-start.2 = (bf16[2048,3072]{1,0:T(8,128)(2,1)}, bf16[2048,3072]{1,0:T(8,128)(2,1)S(1)}, u32[]{:S(2)}) copy-start(bf16[2048,3072]{1,0:T(8,128)(2,1)S(1)} %multiply_convert_fusion) | copy-start | bytes 37748740
  54.7 4.7 %copy-start.8 = (bf16[2,2,128]{2,1,0:T(2,128)(2,1)S(1)}, bf16[2,2,128]{2,1,0:T(2,128)(2,1)}, u32[]{:S(2)}) copy-start(bf16[2,2,128]{2,1,0:T(2,128)(2,1)} %param.20) | copy-start | bytes 3076
  66.6 17.5 %copy-start.6 = (bf16[2,2048,64]{1,2,0:T(8,128)(2,1)S(1)}, bf16[2,2048,64]{1,2,0:T(8,128)(2,1)}, u32[]{:S(2)}) copy-start(bf16[2,2048,64]{1,2,0:T(8,128)(2,1)} %param.21) | copy-start | bytes 1572868
  66.6 56.9 %copy-start.4 = (bf16[1,128,3072]{2,1,0:T(8,128)(2,1)S(1)}, bf16[1,128,3072]{2,1,0:T(8,128)(2,1)}, u32[]{:S(2)}) copy-start(bf16[1,128,3072]{2,1,0:T(8,128)(2,1)} %param.12) | copy-start | bytes 2359300
  71.4 244.0 %copy-start.1 = (bf16[2,64,3072]{2,1,0:T(8,128)(2,1)S(1)}, bf16[2,64,3072]{2,1,0:T(8,128)(2,1)}, u32[]{:S(2)}) copy-start(bf16[2,64,3072]{2,1,0:T(8,128)(2,1)} %param.17) | copy-start | bytes 2359300
  124.8 188.9 %all-reduce.5.cloned.1.call-start = ((), (), s32[]{:S(2)}) async-start(), calls=%async_computation.2 | async-start | bytes 1572864 | tf_op jit(solution)/shard_map/psum | solution.py:125
Sparse Core Ops, SparseCore 0:
  124.9 122.8 all-reduce.2
  250.7 63.0 all-reduce.4
where the time goes:
time: 324 us; the launch traced here: 322 us
  waiting for transfers between devices  186 us (57%)
  blocking collectives  68.9 us (21%)
  matrix products  24.3 us (8%)
  other arithmetic  15.9 us (5%)
  between operations  15.7 us (5%)
  local copies, waits for them, and re-layouts  11.2 us (3%)
    psum x1, waiting for transfers between devices, per_device(): total, spread_all = lax.psum((partial_value, spread), 'seq')  123 us
    psum x1, waiting for transfers between devices, per_device(): summed = lax.psum(total / weight, 'dp')  63.1 us
    psum x1, blocking collectives, per_device(): total, spread_all = lax.psum((partial_value, spread), 'seq')  24.8 us
    all_gather x1, blocking collectives, per_device(): every_noisy = lax.all_gather(noisy_bf, 'seq', axis=0, tiled=True)  18.8 us
    all_to_all x1, blocking collectives, per_device(): lax.all_to_all(attended, 'seq', split_axis=0, concat_axis=1, tiled=True)  12.8 us
    all_gather x1, blocking collectives, per_device(): every_pred = lax.all_gather(predicted[None], 'mp', axis=0, tiled=True)  12.5 us
    convert_element_type x1, other arithmetic, per_device(): normed = rms_scale(hidden, norm_sel).astype(jnp.bfloat16)  10.6 us
    dot_general x1, matrix products, per_device(): jnp.dot(every_noisy, embed_sel, preferred_element_type=jnp.float32) + temb  10.1 us
  transfers between devices with their start and end apart: 2, of which 2 were waited for; matrix products, arithmetic and copies ran while one was open for 0% of the time, Pallas kernels for 0%

commit v1 on v0

v1 whole, which is shorter than its diff:
```python
import math

import jax
import jax.numpy as jnp
from jax import lax
from jax.experimental import pallas as pl
from jax.experimental.pallas import tpu as pltpu
from jax.sharding import PartitionSpec as P

F32 = jnp.float32
BF16 = jnp.bfloat16
STEPS = 1000
NN = (((1,), (0,)), ((), ()))
NT = (((1,), (1,)), ((), ()))
TN = (((0,), (0,)), ((), ()))
VMEM = pl.BlockSpec(memory_space=pltpu.VMEM)
SMEM = pl.BlockSpec(memory_space=pltpu.SMEM)
VMEM_BYTES = 48 * 1024 * 1024


def dot(left, right, dims=NN):
    return lax.dot_general(left, right, dims, preferred_element_type=F32)


def split_two(values):
    high = values.astype(BF16)
    low = (values - high.astype(F32)).astype(BF16)
    return high, low


def level_of(steps_ref):
    return (steps_ref[0].astype(F32) + 1.0) * (1.0 / (STEPS + 1.0))


def time_embedding(step_value, width):
    half_width = width // 2
    ranks = jnp.arange(half_width).astype(F32) / half_width
    frequency = jnp.exp(-math.log(10000.0) * ranks)
    phases = step_value * frequency
    return jnp.concatenate([jnp.cos(phases), jnp.sin(phases)])


def scaled_and_rms(features, gain):
    features_f = features.astype(F32)
    mean_square = jnp.sum(features_f * features_f, axis=1, keepdims=True) / features.shape[1]
    return (features_f * gain).astype(BF16), lax.rsqrt(mean_square + 1e-06)


def latents_kernel(steps_ref, features_ref, gain_ref, weight_ref, noise_ref, send_ref, clean_ref, noisy_ref):
    level = level_of(steps_ref)
    slot = lax.axis_index("mp")
    tokens = features_ref.shape[0]
    part = tokens // 4
    rows = [features_ref[pl.ds(pl.multiple_of(((slot + i) % 4) * part, part), part), :] for i in range(4)]
    scaled, inv_rms = scaled_and_rms(jnp.concatenate(rows, axis=0), gain_ref[...].astype(F32))
    inv_row = jnp.broadcast_to(inv_rms, (tokens, tokens)).T[0:1]
    clean = dot(weight_ref[...], scaled, NT) * inv_row
    noise = pltpu.roll(noise_ref[...].astype(F32), (tokens - slot * part) % tokens, 1)
    noisy = (1.0 - level) * clean + level * noise
    rounded = noisy.astype(BF16)
    for target in range(send_ref.shape[0]):
        send_ref[target] = rounded
    clean_ref[...] = clean
    noisy_ref[...] = noisy


def own_kernel(features_ref, gain_ref, clean_ref, noisy_ref, scaled_ref, own_ref, inv_ref):
    tokens = features_ref.shape[0]
    part = tokens // 4
    slot = lax.axis_index("mp")
    rows = features_ref[pl.ds(pl.multiple_of(slot * part, part), part), :]
    scaled, inv_rms = scaled_and_rms(rows, gain_ref[...].astype(F32))
    scaled_ref[...] = scaled
    inv_ref[...] = jnp.broadcast_to(inv_rms, inv_ref.shape)
    both = jnp.concatenate([clean_ref[...], noisy_ref[...]], axis=0).T
    own_ref[...] = both[0:part]


def fold_kernel(temb_ref, embed_ref, gain_ref, qkv_ref, qk_ref, out_ref, fold_ref, scale_ref, square_ref, acc, gram):
    step = pl.program_id(0)
    chunk = embed_ref.shape[2]

    @pl.when(step == 0)
    def _():
        acc[...] = jnp.zeros_like(acc)
        gram[...] = jnp.zeros_like(gram)
        square_ref[...] = jnp.zeros_like(square_ref)

    temb = temb_ref[...]
    squares = jnp.sum(temb * temb, axis=1, keepdims=True)
    square_ref[...] += jnp.broadcast_to(squares, square_ref.shape)
    spot = lax.broadcasted_iota(jnp.int32, (16, chunk), 0)
    temb_one = temb.astype(BF16).astype(F32)
    temb_two = (temb - temb_one).astype(BF16).astype(F32)
    temb_three = temb - temb_one - temb_two
    temb_rows = jnp.where(spot == 0, temb_one, jnp.where(spot == 1, temb_two, jnp.where(spot == 2, temb_three, 0.0))).astype(BF16)
    for m in range(2):
        gain = gain_ref[m : m + 1, :].astype(F32)
        table = embed_ref[m]
        high, low = split_two(table.astype(F32) * gain)
        biased = temb * gain
        bias_high = biased.astype(BF16).astype(F32)
        bias_rows = jnp.where(spot == 0, bias_high, jnp.where(spot == 1, biased - bias_high, 0.0)).astype(BF16)
        rows = jnp.concatenate([high, low, bias_rows], axis=0)
        for i in range(3):
            acc[m, i] += dot(rows, qkv_ref[m, i])
        pads = jnp.zeros((48, chunk), BF16)
        gram[m] += dot(table, jnp.concatenate([table, temb_rows, pads], axis=0), NT)

    @pl.when(step == pl.num_programs(0) - 1)
    def _():
        head = lax.axis_index("seq")
        lane = lax.broadcasted_iota(jnp.int32, (64, 128), 1)
        row = lax.broadcasted_iota(jnp.int32, (64, 128), 0)

        def stacked(m, i):
            whole = acc[m, i]
            table = whole[0:64] + whole[64:128]
            bias = whole[128:129] + whole[129:130]
            return jnp.concatenate([table, jnp.where(row == 0, bias, 0.0)], axis=0)

        for m in range(2):
            value_high, value_low = split_two(stacked(m, 2))
            out_rows = out_ref[m, :, pl.ds(pl.multiple_of(head * 128, 128), 128)]
            mixed = dot(out_rows, value_high, NT) + dot(out_rows, value_low, NT)
            inner = gram[m]
            linear = inner[:, 64:65] + inner[:, 65:66] + inner[:, 66:67]
            inner = jnp.where(lane < 64, inner, jnp.where(lane == 64, 2.0 * linear, 0.0))
            whole = jnp.concatenate([stacked(m, 1).T, mixed, inner, stacked(m, 0).T], axis=0)
            high, low = split_two(whole)
            fold_ref[m] = jnp.concatenate([high, low], axis=1)
            gains = qk_ref[m, 0:1, :].astype(F32) * qk_ref[m, 1:2, :].astype(F32)
            gains = gains * (math.log2(math.e) / math.sqrt(128.0))
            scale_ref[m] = jnp.broadcast_to(gains, (128, 128)).T


def attention_kernel(latent_ref, fold_ref, scale_ref, square_ref, send_ref, latents, queries):
    blocks = latent_ref.shape[0]
    keys = blocks * 128
    count = blocks * 32
    latents[...] = jnp.ones_like(latents)
    queries[...] = jnp.ones_like(queries)
    for s in range(blocks):
        block = latent_ref[s]
        latents[0:64, s * 128 : (s + 1) * 128] = block
        latents[128:192, s * 128 : (s + 1) * 128] = block
    for g in range(blocks // 4):
        pieces = jnp.concatenate([latent_ref[4 * g + i][:, 0:32] for i in range(4)], axis=1)
        queries[0:64, g * 128 : (g + 1) * 128] = pieces
        queries[128:192, g * 128 : (g + 1) * 128] = pieces
    squares = square_ref[0:1, 0:1]

    def hidden_square(inner, rows):
        return (jnp.sum(inner * rows.astype(F32), axis=0, keepdims=True) + squares) / 3072.0 + 1e-06

    mixed = []
    for m in range(2):
        projected = dot(fold_ref[m, 0:256], latents[...])
        hidden = hidden_square(projected[192:256], latents[0:64])
        key = projected[0:128]
        key_scale = lax.rsqrt(jnp.mean(key * key, axis=0, keepdims=True) + 1e-06 * hidden)
        key = (key * key_scale).astype(BF16)
        value = (projected[128:192] * lax.rsqrt(hidden)).astype(BF16)
        value = jnp.concatenate([value, jnp.ones((16, keys), BF16)], axis=0)
        projected = dot(fold_ref[m, 192:384], queries[...])
        hidden = hidden_square(projected[0:64], queries[0:64])
        query = projected[64:192]
        query_scale = lax.rsqrt(jnp.mean(query * query, axis=0, keepdims=True) + 1e-06 * hidden)
        query = query * query_scale * jnp.concatenate([scale_ref[m]] * (count // 128), axis=1)
        query = query.astype(BF16).T
        total = jnp.zeros((80, count), F32)
        for c in range(keys // 512):
            span = slice(c * 512, (c + 1) * 512)
            shares = jnp.exp2(dot(query, key[:, span])).astype(BF16)
            total += dot(value[:, span], shares, NT)
        mixed.append(total[0:64] / total[64:65])
    whole = jnp.concatenate(mixed, axis=0).T.astype(BF16)
    send_ref[...] = whole.reshape(send_ref.shape)


def spread_rows(total, width):
    spot = lax.broadcasted_iota(jnp.int32, (16, width), 0)
    high = total.astype(BF16).astype(F32)
    return jnp.where(spot == 0, high, jnp.where(spot == 1, total - high, 0.0)).astype(BF16)


def gap_kernel(steps_ref, velocity_ref, scaled_ref, own_ref, inv_ref, send_ref, gap_ref):
    level = level_of(steps_ref)
    velocity = jnp.sum(velocity_ref[...].astype(F32), axis=0)
    own = own_ref[...]
    teacher = velocity[:, 0:64]
    gap = level * (teacher - velocity[:, 64:128])
    distance = jnp.abs(own[:, 0:64] - (own[:, 64:128] - level * teacher))
    spread = jnp.sum(jnp.sum(distance, axis=1, keepdims=True), axis=0, keepdims=True)
    direction = (gap * inv_ref[:, 0:64]).astype(BF16)
    high = gap.astype(BF16)
    gap_ref[...] = jnp.concatenate([high, (gap - high.astype(F32)).astype(BF16)], axis=1)
    grad = dot(direction, scaled_ref[...], TN)
    tail = spread_rows(jnp.broadcast_to(spread, (1, 128)), 128)
    left = lax.broadcasted_iota(jnp.int32, (32, 128), 1) < 64
    for j in range(send_ref.shape[0] // 2):
        first = grad[:, j * 384 : j * 384 + 128]
        middle = grad[:, j * 384 + 128 : j * 384 + 256]
        last = grad[:, j * 384 + 256 : j * 384 + 384]
        turned = pltpu.roll(middle, 64, 1)
        even = jnp.where(left, middle[0:32], turned[32:64])
        odd = jnp.where(left, turned[0:32], middle[32:64])
        send_ref[2 * j] = jnp.concatenate([first.astype(BF16), even.astype(BF16), tail], axis=0)
        send_ref[2 * j + 1] = jnp.concatenate([last.astype(BF16), odd.astype(BF16), tail], axis=0)


def total_kernel(grad_ref, gap_ref, send_ref):
    total = jnp.sum(grad_ref[...].astype(F32), axis=0)
    tail = spread_rows(total[96:97] + total[97:98], 128)
    whole = jnp.concatenate([total[0:96].astype(BF16), tail, gap_ref[...]], axis=0)
    for target in range(send_ref.shape[0]):
        send_ref[target] = whole


def result_kernel(all_ref, gap_ref, grad_ref):
    weights = []
    total = jnp.zeros((96, 128), F32)
    for d in range(4):
        parts = jnp.sum(jnp.stack([all_ref[4 * m + d, 0:112].astype(F32) for m in range(4)]), axis=0)
        inverse = 1.0 / ((parts[96:97] + parts[97:98]) / 131072.0 + 1e-05)
        total += parts[0:96] * inverse
        weights.append(inverse)
    sample = lax.axis_index("dp")
    inverse = weights[0]
    for d in range(1, 4):
        inverse = jnp.where(sample == d, weights[d], inverse)
    gaps = []
    for m in range(4):
        pair = all_ref[4 * m + sample, 112:144].astype(F32)
        gaps.append(pair + pltpu.roll(pair, 64, 1))
    gap_ref[...] = (jnp.concatenate(gaps, axis=0) * inverse).T[0:64]
    whole = total[0:64]
    low = total[64:96]
    half = jnp.concatenate([low, pltpu.roll(low, 64, 1)], axis=0)
    odd = lax.axis_index("seq") % 2 == 1

    @pl.when(odd)
    def _():
        grad_ref[:, 0:64] = half[:, 0:64]
        grad_ref[:, 64:192] = whole

    @pl.when(jnp.logical_not(odd))
    def _():
        grad_ref[:, 0:128] = whole
        grad_ref[:, 128:192] = half[:, 0:64]


def call(kernel, outs, in_specs, name, flops=0, moved=0, **more):
    return pl.pallas_call(
        kernel,
        out_shape=outs,
        in_specs=in_specs,
        out_specs=more.pop("out_specs", jax.tree.map(lambda _: VMEM, outs)),
        compiler_params=pltpu.CompilerParams(vmem_limit_bytes=VMEM_BYTES),
        cost_estimate=pl.CostEstimate(flops=flops, bytes_accessed=moved, transcendentals=0),
        name=name,
        **more,
    )


def per_device(
    gen_features,
    gen_gain,
    gen_weight,
    flow_noise,
    time_steps,
    embed_weight,
    norm_gain,
    qkv_weight,
    qk_gain,
    out_weight,
):
    shape = jax.ShapeDtypeStruct
    seq_count = lax.axis_size("seq")
    group = lax.axis_size("mp") * lax.axis_size("dp")
    features = gen_features[0]
    tokens, width = features.shape
    part = tokens // 4
    gain_row = gen_gain[None]
    send, clean, noisy = call(
        latents_kernel,
        (shape((seq_count, 64, tokens), BF16), shape((64, tokens), F32), shape((64, tokens), F32)),
        [SMEM, VMEM, VMEM, VMEM, VMEM],
        "latents",
        flops=2 * tokens * width * 64,
        moved=2 * tokens * width,
    )(time_steps, features, gain_row, gen_weight.T, flow_noise[0].T)
    every_latent = lax.all_to_all(send, "seq", 0, 0)

    scaled, own, inv = call(
        own_kernel,
        (shape((part, width), BF16), shape((part, 128), F32), shape((part, 128), F32)),
        [VMEM] * 4,
        "own",
        flops=part * width * 4,
        moved=2 * tokens * width,
    )(features, gain_row, clean, noisy)
    temb = time_embedding(time_steps[0].astype(F32), width)[None]
    chunk = 512
    fold, scale, square = call(
        fold_kernel,
        (shape((2, 384, 256), BF16), shape((2, 128, 128), F32), shape((8, 128), F32)),
        [
            pl.BlockSpec((1, chunk), lambda k: (0, k)),
            pl.BlockSpec((2, 64, chunk), lambda k: (0, 0, k)),
            pl.BlockSpec((2, chunk), lambda k: (0, k)),
            pl.BlockSpec((2, 3, chunk, 128), lambda k: (0, 0, k, 0)),
            pl.BlockSpec((2, 2, 128), lambda k: (0, 0, 0)),
            pl.BlockSpec((2, 64, 2048), lambda k: (0, 0, 0)),
        ],
        "fold",
        flops=2 * 2 * width * 384 * 256,
        moved=2 * 2 * width * 384,
        out_specs=(
            pl.BlockSpec((2, 384, 256), lambda k: (0, 0, 0)),
            pl.BlockSpec((2, 128, 128), lambda k: (0, 0, 0)),
            pl.BlockSpec((8, 128), lambda k: (0, 0)),
        ),
        grid=(width // chunk,),
        scratch_shapes=[pltpu.VMEM((2, 3, 144, 128), F32), pltpu.VMEM((2, 64, 128), F32)],
    )(
        temb,
        embed_weight,
        norm_gain,
        qkv_weight.transpose(0, 2, 1, 3),
        qk_gain,
        out_weight.transpose(0, 2, 1),
    )
    keys = seq_count * tokens
    send = call(
        attention_kernel,
        shape((seq_count, part, 128), BF16),
        [VMEM] * 4,
        "attention",
        flops=2 * 2 * keys * (keys // 4) * 256,
        moved=2 * keys * 64,
        scratch_shapes=[pltpu.VMEM((256, keys), BF16), pltpu.VMEM((256, keys // 4), BF16)],
    )(every_latent, fold, scale, square)
    velocities = lax.all_to_all(send, "seq", 0, 0)
    send, gap = call(
        gap_kernel,
        (shape((seq_count, 112, 128), BF16), shape((part, 128), BF16)),
        [SMEM] + [VMEM] * 4,
        "gap",
        flops=2 * part * width * 64,
        moved=2 * part * width,
    )(time_steps, velocities, scaled, own, inv)
    partials = lax.all_to_all(send, "seq", 0, 0)
    send = call(
        total_kernel,
        shape((group, 144, 128), BF16),
        [VMEM] * 2,
        "total",
        flops=seq_count * 112 * 128,
        moved=2 * seq_count * 112 * 128,
    )(partials, gap)
    every_total = lax.all_to_all(send, ("mp", "dp"), 0, 0)
    dmd, grad = call(
        result_kernel,
        (shape((64, tokens), F32), shape((64, width // seq_count), F32)),
        [VMEM],
        "result",
        flops=group * 112 * 128,
        moved=2 * group * 144 * 128,
    )(every_total)
    return dmd.T[None], grad.T


def solution(mesh):
    placed = (
        P("dp", "seq", None),
        P(),
        P(),
        P("dp", "seq", None),
        P("dp"),
        P(),
        P(),
        P(None, None, None, "seq"),
        P(),
        P(),
    )
    return jax.shard_map(
        per_device,
        mesh=mesh,
        in_specs=placed,
        out_specs=(P("dp", "seq", None), P("seq", None)),
        check_vma=False,
    )
```

time: 324 us -> 82.2 us (0.25)
  waiting for transfers between devices: 186 us -> 5.07 us
  blocking collectives: 68.9 us -> 43.4 us
  matrix products: 24.3 us -> 0 us
  other arithmetic: 15.9 us -> 0.06 us
  between operations: 15.7 us -> 1.35 us
  Pallas kernels: 0 us -> 13 us
  starting transfers between devices: 0.08 us -> 11.5 us
  local copies, waits for them, and re-layouts: 11.2 us -> 7.1 us
    psum x2 -> x0, waiting for transfers between devices: 186 us -> none  [the longest x1 123 us: per_device(): total, spread_all = lax.psum((partial_value, spread), 'seq')]
    all_gather x2 -> x0, blocking collectives: 31.3 us -> none  [the longest x1 18.8 us: per_device(): every_noisy = lax.all_gather(noisy_bf, 'seq', axis=0, tiled=True)]
    all_to_all x1 -> x2, blocking collectives: 12.8 us -> 43.4 us  [the longest x1 30.4 us: per_device(): every_total = lax.all_to_all(send, ('mp', 'dp'), 0, 0)]
    psum x1 -> x0, blocking collectives: 24.8 us -> none  [per_device(): total, spread_all = lax.psum((partial_value, spread), 'seq')]
    dot_general x10 -> x0, matrix products: 24.3 us -> none  [the longest x1 10.1 us: per_device(): jnp.dot(every_noisy, embed_sel, preferred_element_type=jnp.float32) + temb]
    pallas_call x0 -> x7, Pallas kernels: none -> 13 us  [the longest x1 5.77 us: per_device(): call(fold_kernel, (shape((2, 384, 256), BF16), shape((2, 128, 128), F32),...]
    convert_element_type x5 -> x0, other arithmetic: 11.6 us -> none  [the longest x1 10.6 us: per_device(): normed = rms_scale(hidden, norm_sel).astype(jnp.bfloat16)]
    all_to_all x0 -> x2, starting transfers between devices: none -> 11.5 us  [the longest x1 5.77 us: per_device(): every_latent = lax.all_to_all(send, 'seq', 0, 0)]
  transfers between devices with their start and end apart: 2 -> 2, of which waited for: 2 -> 1; matrix products, arithmetic and copies ran while one was open for 0% -> 0% of each run, Pallas kernels for 0% -> 7%
where the time goes in v1:
time: 82.2 us; the launch traced here: 81.5 us
  blocking collectives  43.4 us (53%)
  Pallas kernels  13 us (16%)
  starting transfers between devices  11.5 us (14%)
  local copies, waits for them, and re-layouts  7.1 us (9%)
  waiting for transfers between devices  5.07 us (6%)
  between operations  1.35 us (2%)
    all_to_all x1, blocking collectives, per_device(): every_total = lax.all_to_all(send, ('mp', 'dp'), 0, 0)  30.4 us
    all_to_all x1, blocking collectives, per_device(): partials = lax.all_to_all(send, 'seq', 0, 0)  13.1 us
    unnamed x16, local copies, waits for them, and re-layouts  6.4 us
    all_to_all x1, starting transfers between devices, per_device(): every_latent = lax.all_to_all(send, 'seq', 0, 0)  5.77 us
    pallas_call x1, Pallas kernels, per_device(): call(fold_kernel, (shape((2, 384, 256), BF16), shape((2, 128, 128), F32),...  5.77 us
    all_to_all x1, starting transfers between devices, per_device(): velocities = lax.all_to_all(send, 'seq', 0, 0)  5.71 us
    all_to_all x1, waiting for transfers between devices, per_device(): velocities = lax.all_to_all(send, 'seq', 0, 0)  5.06 us
    pallas_call x1, Pallas kernels, per_device(): call(attention_kernel, shape((seq_count, part, 128), BF16), [VMEM] * 4, '...  4.59 us
  transfers between devices with their start and end apart: 2, of which 1 were waited for; matrix products, arithmetic and copies ran while one was open for 0% of the time, Pallas kernels for 7%

profile of v1, /device:TPU:32, one launch (start us, length us, event | category | flops | bytes accessed | tf_op | source)
XLA Modules:
  0.0 81.5 jit_solution(7861701503152536571)
XLA Ops:
  1.3 0.7 broadcast_in_dim.9.gain_ref
  2.0 0.0 copy-start
  2.0 1.1 %copy-done = bf16[1,128,3072]{2,1,0:T(8,128)(2,1)S(1)} copy-done((bf16[1,128,3072]{2,1,0:T(8,128)(2,1)S(1)}, bf16[1,128,3072]{2,1,0:T(8,128)(2,1)}, u32[]{:S(2)}) %copy-start) | copy-done | bytes 786456
  3.1 0.0 copy-start.4
  3.1 1.0 %copy-done.4 = bf16[3072,64]{0,1:T(8,128)(2,1)S(1)} copy-done((bf16[3072,64]{0,1:T(8,128)(2,1)S(1)}, bf16[3072,64]{0,1:T(8,128)(2,1)}, u32[]{:S(2)}) %copy-start.4) | copy-done | bytes 393240
  4.1 0.0 copy-start.5
  4.1 0.7 copy-done.5
  4.8 1.1 %latents.1 = (bf16[16,64,128]{2,1,0:T(8,128)(2,1)}, f32[64,128]{1,0:T(8,128)S(1)}, f32[64,128]{1,0:T(8,128)S(1)}) custom-call(s32[1]{0:T(128)S(6)} %copy.12.steps_ref, bf16[128,3072]{1,0:T(8,128)(2,1)S(1)} %bitcast.13, bf16[1,3072]{1,0:T(2,128)(2,1)S(1)} %broadcast_in_dim.9.gain_ref, bf16[64,3072]{1,0:T(8,128)(2,1)S(1)} %bitcast.16, bf16[64,128]{1,0:T(8,128)(2,1)S(1)} %bitcast.18), custom_call_target="tpu_custom_call" | custom-call | flops 50331648 | bytes 786432 | tf_op jit(solution)/shard_map/latents/pallas_call | solution.py:285
  5.9 5.8 %all-to-all-start = ((bf16[16,64,128]{2,1,0:T(8,128)(2,1)}), bf16[16,64,128]{2,1,0:T(8,128)(2,1)S(1)}, u32[]{:S(2)}, u32[]{:S(2)}) async-start(bf16[16,64,128]{2,1,0:T(8,128)(2,1)} %get-tuple-element.15), calls=%async_computation | async-start | bytes 524288 | tf_op jit(solution)/shard_map/all_to_all | solution.py:293
  11.7 0.1 fusion
  11.8 0.0 copy-start.2
  11.8 1.1 %copy-done.2 = bf16[2,64,3072]{2,1,0:T(8,128)(2,1)S(1)} copy-done((bf16[2,64,3072]{2,1,0:T(8,128)(2,1)S(1)}, bf16[2,64,3072]{2,1,0:T(8,128)(2,1)}, u32[]{:S(2)}) %copy-start.2) | copy-done | bytes 786456
  12.9 0.0 copy-start.3
  12.9 1.0 %copy-done.3 = bf16[2,2048,64]{1,2,0:T(8,128)(2,1)S(1)} copy-done((bf16[2,2048,64]{1,2,0:T(8,128)(2,1)S(1)}, bf16[2,2048,64]{1,2,0:T(8,128)(2,1)}, u32[]{:S(2)}) %copy-start.3) | copy-done | bytes 524312
  14.0 0.0 copy-start.6
  14.0 0.7 copy-done.6
  14.7 0.0 copy-start.7
  14.7 0.7 copy-done.7
  15.4 0.0 copy-start.1
  15.4 5.8 %fold.1 = (bf16[2,384,256]{2,1,0:T(8,128)(2,1)S(1)}, f32[2,128,128]{2,1,0:T(8,128)S(1)}, f32[8,128]{1,0:T(8,128)S(1)}) custom-call(f32[1,3072]{1,0:T(1,128)S(1)} %bitcast.17, bf16[2,64,3072]{2,1,0:T(8,128)(2,1)S(1)} %copy-done.2, bf16[2,3072]{1,0:T(2,128)(2,1)S(1)} %copy-done.6, bf16[2,3,3072,128]{3,2,1,0:T(8,128)(2,1)} %bitcast.19, ...), custom_call_target="tpu_custom_call" | custom-call | flops 1207959552 | bytes 4718592 | tf_op jit(solution)/shard_map/fold/pallas_call | solution.py:305
  21.1 0.0 all-to-all-done.latent_ref
  21.1 4.6 %attention.1 = bf16[16,32,128]{2,1,0:T(8,128)(2,1)} custom-call(bf16[16,64,128]{2,1,0:T(8,128)(2,1)S(1)} %all-to-all-done.latent_ref, bf16[2,384,256]{2,1,0:T(8,128)(2,1)S(1)} %get-tuple-element.16.fold_ref, f32[2,128,128]{2,1,0:T(8,128)S(1)} %get-tuple-element.17.scale_ref, f32[8,128]{1,0:T(8,128)S(1)} %get-tuple-element.18.square_ref), custom_call_target="tpu_custom_call" | custom-call | flops 1073741824 | bytes 262144 | tf_op jit(solution)/shard_map/attention/pallas_call | solution.py:335
  25.7 5.7 %all-to-all-start.1 = ((bf16[16,32,128]{2,1,0:T(8,128)(2,1)}), bf16[16,32,128]{2,1,0:T(8,128)(2,1)S(1)}, u32[]{:S(2)}, u32[]{:S(2)}) async-start(bf16[16,32,128]{2,1,0:T(8,128)(2,1)} %attention.1), calls=%async_computation.1 | async-start | bytes 262144 | tf_op jit(solution)/shard_map/all_to_all | solution.py:344
  31.4 0.0 copy-done.1
  31.5 0.2 own.1
  31.6 5.1 %all-to-all-done.1.velocity_ref = bf16[16,32,128]{2,1,0:T(8,128)(2,1)S(1)} async-done(((bf16[16,32,128]{2,1,0:T(8,128)(2,1)}), bf16[16,32,128]{2,1,0:T(8,128)(2,1)S(1)}, u32[]{:S(2)}, u32[]{:S(2)}) %all-to-all-start.1) | async-done | bytes 131104 | tf_op jit(solution)/shard_map/all_to_all | solution.py:344
  36.7 0.5 gap.1
  37.1 13.1 %all_to_all.20.grad_ref = bf16[16,112,128]{2,1,0:T(8,128)(2,1)S(1)} all-to-all(bf16[16,112,128]{2,1,0:T(8,128)(2,1)S(1)} %get-tuple-element.24), channel_id=1, replica_groups=mesh['mp'=4,'seq'=16,'dp'=4] {'seq'}, dimensions={0} | all-to-all | bytes 917504 | tf_op jit(solution)/shard_map/all_to_all | solution.py:353
  50.2 0.1 total.1
  50.3 30.4 %all_to_all.21.all_ref = bf16[16,144,128]{2,1,0:T(8,128)(2,1)S(1)} all-to-all(bf16[16,144,128]{2,1,0:T(8,128)(2,1)S(1)} %total.1), channel_id=1, replica_groups=mesh['mp'=4,'seq'=16,'dp'=4] {'mp','dp'}, dimensions={0} | all-to-all | bytes 1179648 | tf_op jit(solution)/shard_map/all_to_all | solution.py:362
  80.6 0.8 %result.1 = (f32[64,128]{1,0:T(8,128)}, f32[64,192]{1,0:T(8,128)}) custom-call(bf16[16,144,128]{2,1,0:T(8,128)(2,1)S(1)} %all_to_all.21.all_ref), custom_call_target="tpu_custom_call" | custom-call | flops 229376 | bytes 589824 | tf_op jit(solution)/shard_map/result/pallas_call | solution.py:363
  (1 shorter events, 0.0 us)
Async XLA Ops:
  2.0 1.1 %copy-start = (bf16[1,128,3072]{2,1,0:T(8,128)(2,1)S(1)}, bf16[1,128,3072]{2,1,0:T(8,128)(2,1)}, u32[]{:S(2)}) copy-start(bf16[1,128,3072]{2,1,0:T(8,128)(2,1)} %param.10) | copy-start | bytes 2359300
  3.1 1.0 %copy-start.4 = (bf16[3072,64]{0,1:T(8,128)(2,1)S(1)}, bf16[3072,64]{0,1:T(8,128)(2,1)}, u32[]{:S(2)}) copy-start(bf16[3072,64]{0,1:T(8,128)(2,1)} %param.12) | copy-start | bytes 1179652
  4.1 0.7 copy-start.5
  5.9 15.2 %all-to-all-start = ((bf16[16,64,128]{2,1,0:T(8,128)(2,1)}), bf16[16,64,128]{2,1,0:T(8,128)(2,1)S(1)}, u32[]{:S(2)}, u32[]{:S(2)}) async-start(bf16[16,64,128]{2,1,0:T(8,128)(2,1)} %get-tuple-element.15), calls=%async_computation | async-start | bytes 524288 | tf_op jit(solution)/shard_map/all_to_all | solution.py:293
  11.8 1.1 %copy-start.2 = (bf16[2,64,3072]{2,1,0:T(8,128)(2,1)S(1)}, bf16[2,64,3072]{2,1,0:T(8,128)(2,1)}, u32[]{:S(2)}) copy-start(bf16[2,64,3072]{2,1,0:T(8,128)(2,1)} %embed_ref.1) | copy-start | bytes 2359300
  12.9 1.0 %copy-start.3 = (bf16[2,2048,64]{1,2,0:T(8,128)(2,1)S(1)}, bf16[2,2048,64]{1,2,0:T(8,128)(2,1)}, u32[]{:S(2)}) copy-start(bf16[2,2048,64]{1,2,0:T(8,128)(2,1)} %param.19) | copy-start | bytes 1572868
  14.0 0.7 copy-start.6
  14.7 0.7 copy-start.7
  15.4 16.1 %copy-start.1 = (bf16[1,128,3072]{2,1,0:T(8,128)(2,1)S(1)}, bf16[1,128,3072]{2,1,0:T(8,128)(2,1)}, u32[]{:S(2)}) copy-start(bf16[1,128,3072]{2,1,0:T(8,128)(2,1)} %param.10) | copy-start | bytes 2359300
  25.7 10.9 %all-to-all-start.1 = ((bf16[16,32,128]{2,1,0:T(8,128)(2,1)}), bf16[16,32,128]{2,1,0:T(8,128)(2,1)S(1)}, u32[]{:S(2)}, u32[]{:S(2)}) async-start(bf16[16,32,128]{2,1,0:T(8,128)(2,1)} %attention.1), calls=%async_computation.1 | async-start | bytes 262144 | tf_op jit(solution)/shard_map/all_to_all | solution.py:344

commit v2 on v1

v2 whole, which is shorter than its diff:
```python
import math

import jax
import jax.numpy as jnp
from jax import lax
from jax.experimental import pallas as pl
from jax.experimental.pallas import tpu as pltpu
from jax.sharding import PartitionSpec as P

F32 = jnp.float32
BF16 = jnp.bfloat16
STEPS = 1000
NN = (((1,), (0,)), ((), ()))
NT = (((1,), (1,)), ((), ()))
TN = (((0,), (0,)), ((), ()))
VMEM = pl.BlockSpec(memory_space=pltpu.VMEM)
SMEM = pl.BlockSpec(memory_space=pltpu.SMEM)
HBM = pl.BlockSpec(memory_space=pltpu.HBM)
VMEM_BYTES = 48 * 1024 * 1024


def dot(left, right, dims=NN):
    return lax.dot_general(left, right, dims, preferred_element_type=F32)


def split_two(values):
    high = values.astype(BF16)
    low = (values - high.astype(F32)).astype(BF16)
    return high, low


def level_of(steps_ref):
    return (steps_ref[0].astype(F32) + 1.0) * (1.0 / (STEPS + 1.0))


def time_embedding(step_value, width):
    half_width = width // 2
    ranks = jnp.arange(half_width).astype(F32) / half_width
    frequency = jnp.exp(-math.log(10000.0) * ranks)
    phases = step_value * frequency
    return jnp.concatenate([jnp.cos(phases), jnp.sin(phases)])


def scaled_and_rms(features, gain):
    features_f = features.astype(F32)
    mean_square = jnp.sum(features_f * features_f, axis=1, keepdims=True) / features.shape[1]
    return (features_f * gain).astype(BF16), lax.rsqrt(mean_square + 1e-06)


def latents_kernel(steps_ref, features_hbm, gain_hbm, weight_hbm, noise_hbm, send_ref, features, gain, weight, noise, sems):
    slot = lax.axis_index("mp")
    tokens, width = features.shape
    part = tokens // 4
    copies = [
        pltpu.make_async_copy(gain_hbm, gain, sems.at[4]),
        pltpu.make_async_copy(weight_hbm, weight, sems.at[5]),
        pltpu.make_async_copy(noise_hbm, noise, sems.at[6]),
    ]
    quarters = []
    for i in range(4):
        start = pl.multiple_of(((slot + i) % 4) * part, part)
        rows = features.at[pl.ds(i * part, part), :]
        quarters.append(pltpu.make_async_copy(features_hbm.at[pl.ds(start, part), :], rows, sems.at[i]))
    for copy in copies[:1] + quarters + copies[1:]:
        copy.start()
    level = level_of(steps_ref)
    copies[0].wait()
    gain_row = gain[...].astype(F32).reshape(1, width)
    scaled, inverse = [], []
    for i in range(4):
        quarters[i].wait()
        one, inv_rms = scaled_and_rms(features[i * part : (i + 1) * part, :], gain_row)
        scaled.append(one)
        inverse.append(inv_rms)
    inv_row = jnp.broadcast_to(jnp.concatenate(inverse, axis=0), (tokens, tokens)).T[0:1]
    copies[1].wait()
    clean = dot(weight[...], jnp.concatenate(scaled, axis=0), NT) * inv_row
    copies[2].wait()
    noise_here = pltpu.roll(noise[...].astype(F32), (tokens - slot * part) % tokens, 1)
    rounded = ((1.0 - level) * clean + level * noise_here).astype(BF16)
    for target in range(send_ref.shape[0]):
        send_ref[target] = rounded


def own_kernel(steps_ref, features_hbm, gain_hbm, weight_hbm, noise_hbm, picked_ref, own_ref, inv_ref, features, gain, weight, noise, turned, sems):
    slot = lax.axis_index("mp")
    width = features.shape[1]
    pairs = ((gain_hbm, gain), (features_hbm, features), (weight_hbm, weight), (noise_hbm, noise))
    copies = [pltpu.make_async_copy(source, target, sems.at[i]) for i, (source, target) in enumerate(pairs)]
    for copy in copies:
        copy.start()
    for copy in copies:
        copy.wait()
    level = level_of(steps_ref)
    scaled, inv_rms = scaled_and_rms(features[...], gain[...].astype(F32).reshape(1, width))
    inv_ref[...] = jnp.broadcast_to(inv_rms, inv_ref.shape)
    clean = dot(scaled, weight[...], NT) * inv_rms
    noise_rows = noise[...].astype(F32).T
    own_ref[...] = jnp.concatenate([clean, (1.0 - level) * clean + level * noise_rows], axis=1)
    turned[...] = scaled.T
    for s in range(16):
        start = pl.multiple_of(s * 192 + slot * 48, 16)
        picked_ref[s * 48 : (s + 1) * 48, :] = turned[pl.ds(start, 48), :]


def fold_kernel(temb_ref, embed_hbm, gain_hbm, qkv_hbm, qk_hbm, out_hbm, fold_ref, scale_ref, square_ref, embed, gain, qkv, qk, out, sems):
    head = lax.axis_index("seq")
    width = embed.shape[2]
    parts = 3
    chunk = width // parts
    columns = pl.ds(pl.multiple_of(head * 128, 128), 128)
    pairs = ((embed_hbm, embed), (gain_hbm, gain), (qk_hbm, qk), (out_hbm.at[:, :, columns], out))
    copies = [pltpu.make_async_copy(source, target, sems.at[i]) for i, (source, target) in enumerate(pairs)]
    pieces = []
    for k in range(parts):
        span = pl.ds(k * chunk, chunk)
        pieces.append(pltpu.make_async_copy(qkv_hbm.at[:, :, span, :], qkv.at[:, :, span, :], sems.at[4 + k]))
    for copy in copies + pieces:
        copy.start()
    temb = temb_ref[...]
    squares = jnp.sum(temb * temb, axis=1, keepdims=True)
    square_ref[...] = jnp.broadcast_to(squares, square_ref.shape)
    spot = lax.broadcasted_iota(jnp.int32, (16, width), 0)
    temb_one = temb.astype(BF16).astype(F32)
    temb_two = (temb - temb_one).astype(BF16).astype(F32)
    temb_three = temb - temb_one - temb_two
    temb_rows = jnp.where(spot == 0, temb_one, jnp.where(spot == 1, temb_two, jnp.where(spot == 2, temb_three, 0.0))).astype(BF16)
    for copy in copies:
        copy.wait()
    rows, gram = [], []
    pads = jnp.zeros((48, width), BF16)
    for m in range(2):
        gain_row = gain[m : m + 1, :].astype(F32)
        table = embed[m]
        high, low = split_two(table.astype(F32) * gain_row)
        biased = temb * gain_row
        bias_high = biased.astype(BF16).astype(F32)
        bias_rows = jnp.where(spot == 0, bias_high, jnp.where(spot == 1, biased - bias_high, 0.0)).astype(BF16)
        rows.append(jnp.concatenate([high, low, bias_rows], axis=0))
        gram.append(dot(table, jnp.concatenate([table, temb_rows, pads], axis=0), NT))
    acc = [None, None]
    for k in range(parts):
        pieces[k].wait()
        span = slice(k * chunk, (k + 1) * chunk)
        for m in range(2):
            table = jnp.concatenate([qkv[m, i, span, :] for i in range(3)], axis=1)
            one = dot(rows[m][:, span], table)
            acc[m] = one if acc[m] is None else acc[m] + one
    lane = lax.broadcasted_iota(jnp.int32, (64, 128), 1)
    row = lax.broadcasted_iota(jnp.int32, (64, 128), 0)

    def stacked(m, i):
        whole = acc[m][:, i * 128 : (i + 1) * 128]
        table = whole[0:64] + whole[64:128]
        bias = whole[128:129] + whole[129:130]
        return jnp.concatenate([table, jnp.where(row == 0, bias, 0.0)], axis=0)

    for m in range(2):
        value_high, value_low = split_two(stacked(m, 2))
        mixed = dot(out[m], value_high, NT) + dot(out[m], value_low, NT)
        inner = gram[m]
        linear = inner[:, 64:65] + inner[:, 65:66] + inner[:, 66:67]
        inner = jnp.where(lane < 64, inner, jnp.where(lane == 64, 2.0 * linear, 0.0))
        whole = jnp.concatenate([stacked(m, 1).T, mixed, inner, stacked(m, 0).T], axis=0)
        high, low = split_two(whole)
        fold_ref[m] = jnp.concatenate([high, low], axis=1)
        gains = qk[m, 0:1, :].astype(F32) * qk[m, 1:2, :].astype(F32)
        gains = gains * (math.log2(math.e) / math.sqrt(128.0))
        scale_ref[m] = jnp.broadcast_to(gains, (128, 128)).T


def attention_kernel(latent_ref, fold_ref, scale_ref, square_ref, send_ref, latents, queries):
    blocks = latent_ref.shape[0]
    keys = blocks * 128
    count = blocks * 32
    latents[...] = jnp.ones_like(latents)
    queries[...] = jnp.ones_like(queries)
    for s in range(blocks):
        block = latent_ref[s]
        latents[0:64, s * 128 : (s + 1) * 128] = block
        latents[128:192, s * 128 : (s + 1) * 128] = block
    for g in range(blocks // 4):
        pieces = jnp.concatenate([latent_ref[4 * g + i][:, 0:32] for i in range(4)], axis=1)
        queries[0:64, g * 128 : (g + 1) * 128] = pieces
        queries[128:192, g * 128 : (g + 1) * 128] = pieces
    squares = square_ref[0:1, 0:1]

    def hidden_square(inner, rows):
        return (jnp.sum(inner * rows.astype(F32), axis=0, keepdims=True) + squares) / 3072.0 + 1e-06

    mixed = []
    for m in range(2):
        projected = dot(fold_ref[m, 0:256], latents[...])
        hidden = hidden_square(projected[192:256], latents[0:64])
        key = projected[0:128]
        key_scale = lax.rsqrt(jnp.mean(key * key, axis=0, keepdims=True) + 1e-06 * hidden)
        key = (key * key_scale).astype(BF16)
        value = (projected[128:192] * lax.rsqrt(hidden)).astype(BF16)
        value = jnp.concatenate([value, jnp.ones((16, keys), BF16)], axis=0)
        projected = dot(fold_ref[m, 192:384], queries[...])
        hidden = hidden_square(projected[0:64], queries[0:64])
        query = projected[64:192]
        query_scale = lax.rsqrt(jnp.mean(query * query, axis=0, keepdims=True) + 1e-06 * hidden)
        query = query * query_scale * jnp.concatenate([scale_ref[m]] * (count // 128), axis=1)
        query = query.astype(BF16).T
        total = jnp.zeros((80, count), F32)
        for c in range(keys // 512):
            span = slice(c * 512, (c + 1) * 512)
            shares = jnp.exp2(dot(query, key[:, span])).astype(BF16)
            total += dot(value[:, span], shares, NT)
        mixed.append(total[0:64] / total[64:65])
    whole = jnp.concatenate(mixed, axis=0).T.astype(BF16)
    for target in range(send_ref.shape[0]):
        s = target % blocks
        send_ref[target] = whole[s * 32 : (s + 1) * 32]


def gap_kernel(steps_ref, velocity_ref, picked_ref, own_ref, inv_ref, send_ref, gap_ref):
    level = level_of(steps_ref)
    blocks = send_ref.shape[0]
    velocity = [jnp.sum(velocity_ref[q * blocks : (q + 1) * blocks].astype(F32), axis=0) for q in range(4)]
    velocity = jnp.concatenate(velocity, axis=0)
    own = own_ref[...]
    teacher = velocity[:, 0:64]
    gap = level * (teacher - velocity[:, 64:128])
    gap_ref[...] = jnp.concatenate([gap, gap], axis=1)
    distance = jnp.abs(own[:, 0:64] - (own[:, 64:128] - level * teacher))
    spread = jnp.sum(jnp.sum(distance, axis=1, keepdims=True), axis=0, keepdims=True)
    direction = (gap * inv_ref[:, 0:64]).astype(BF16)
    grad = dot(picked_ref[...], jnp.concatenate([direction, direction], axis=1))
    spread = jnp.broadcast_to(spread, (8, 128))
    spot = lax.broadcasted_iota(jnp.int32, (8, 128), 0)
    high = spread.astype(BF16).astype(F32)
    tail = jnp.where(spot == 0, high, jnp.where(spot == 1, spread - high, 0.0))
    left = lax.broadcasted_iota(jnp.int32, (24, 128), 1) < 64
    for s in range(blocks):
        packed = jnp.where(left, grad[s * 48 : s * 48 + 24], grad[s * 48 + 24 : s * 48 + 48])
        send_ref[s] = jnp.concatenate([packed, tail], axis=0).astype(BF16)


def weight_inverse(total):
    return 1.0 / ((total[24:25] + total[25:26]) / 131072.0 + 1e-05)


def total_kernel(grad_ref, send_ref):
    total = jnp.sum(grad_ref[...].astype(F32), axis=0)
    whole = (total[0:24] * weight_inverse(total)).astype(BF16)
    for target in range(send_ref.shape[0]):
        send_ref[target] = whole


def dmd_kernel(grad_ref, gap_ref, dmd_ref):
    total = jnp.sum(grad_ref[...].astype(F32), axis=0)
    dmd_ref[...] = (gap_ref[...] * weight_inverse(total)).T[0:64]


def result_kernel(all_ref, grad_ref):
    rows = []
    for m in range(4):
        total = jnp.sum(all_ref[4 * m : 4 * m + 4].astype(F32), axis=0)
        rows += [total, pltpu.roll(total, 64, 1)]
    rows.append(jnp.zeros((64, 128), F32))
    grad_ref[...] = jnp.concatenate(rows, axis=0).T[0:64, 0:192]


def call(kernel, outs, in_specs, name, flops=0, moved=0, **more):
    return pl.pallas_call(
        kernel,
        out_shape=outs,
        in_specs=in_specs,
        out_specs=more.pop("out_specs", jax.tree.map(lambda _: VMEM, outs)),
        compiler_params=pltpu.CompilerParams(vmem_limit_bytes=VMEM_BYTES),
        cost_estimate=pl.CostEstimate(flops=flops, bytes_accessed=moved, transcendentals=0),
        name=name,
        **more,
    )


def per_device(
    gen_features,
    gen_gain,
    gen_weight,
    flow_noise,
    time_steps,
    embed_weight,
    norm_gain,
    qkv_weight,
    qk_gain,
    out_weight,
):
    shape = jax.ShapeDtypeStruct
    seq_count = lax.axis_size("seq")
    group = lax.axis_size("mp") * lax.axis_size("dp")
    features = gen_features[0]
    tokens, width = features.shape
    part = tokens // 4
    local = (time_steps, features, gen_gain, gen_weight.T, flow_noise[0].T)
    buffers = [
        pltpu.VMEM((tokens, width), BF16),
        pltpu.VMEM((width,), BF16),
        pltpu.VMEM((64, width), BF16),
        pltpu.VMEM((64, tokens), BF16),
    ]
    send = call(
        latents_kernel,
        shape((seq_count, 64, tokens), BF16),
        [SMEM] + [HBM] * 4,
        "latents",
        flops=2 * tokens * width * 64,
        moved=2 * tokens * width,
        scratch_shapes=buffers + [pltpu.SemaphoreType.DMA((7,))],
    )(*local)
    every_latent = lax.all_to_all(send, "seq", 0, 0)

    temb = time_embedding(time_steps[0].astype(F32), width)[None]
    fold, scale, square = call(
        fold_kernel,
        (shape((2, 384, 256), BF16), shape((2, 128, 128), F32), shape((8, 128), F32)),
        [VMEM] + [HBM] * 5,
        "fold",
        flops=2 * 2 * width * 384 * 256,
        moved=2 * 2 * width * 384,
        scratch_shapes=[
            pltpu.VMEM((2, 64, width), BF16),
            pltpu.VMEM((2, width), BF16),
            pltpu.VMEM((2, 3, width, 128), BF16),
            pltpu.VMEM((2, 2, 128), BF16),
            pltpu.VMEM((2, 64, 128), BF16),
            pltpu.SemaphoreType.DMA((7,)),
        ],
    )(
        temb,
        embed_weight,
        norm_gain,
        qkv_weight.transpose(0, 2, 1, 3),
        qk_gain,
        out_weight.transpose(0, 2, 1),
    )
    keys = seq_count * tokens
    send = call(
        attention_kernel,
        shape((4 * seq_count, part, 128), BF16),
        [VMEM] * 4,
        "attention",
        flops=2 * 2 * keys * (keys // 4) * 256,
        moved=2 * keys * 64,
        scratch_shapes=[pltpu.VMEM((256, keys), BF16), pltpu.VMEM((256, keys // 4), BF16)],
    )(every_latent, fold, scale, square)
    velocities = lax.all_to_all(send, ("mp", "seq"), 0, 0)
    picked, own, inv = call(
        own_kernel,
        (shape((width // 4, tokens), BF16), shape((tokens, 128), F32), shape((tokens, 128), F32)),
        [SMEM] + [HBM] * 4,
        "own",
        flops=2 * tokens * width * 64,
        moved=2 * tokens * width,
        scratch_shapes=buffers + [pltpu.VMEM((width, tokens), BF16), pltpu.SemaphoreType.DMA((4,))],
    )(*local)
    send, gap = call(
        gap_kernel,
        (shape((seq_count, 32, 128), BF16), shape((tokens, 128), F32)),
        [SMEM] + [VMEM] * 4,
        "gap",
        flops=2 * tokens * width * 16,
        moved=2 * 64 * 32 * 128,
    )(time_steps, velocities, picked, own, inv)
    partials = lax.all_to_all(send, "seq", 0, 0)
    send = call(
        total_kernel,
        shape((group, 24, 128), BF16),
        [VMEM],
        "total",
        flops=seq_count * 32 * 128,
        moved=2 * seq_count * 32 * 128,
    )(partials)
    every_total = lax.all_to_all(send, ("mp", "dp"), 0, 0)
    dmd = call(
        dmd_kernel,
        shape((64, tokens), F32),
        [VMEM] * 2,
        "dmd",
        flops=seq_count * 32 * 128,
        moved=2 * seq_count * 32 * 128,
    )(partials, gap)
    grad = call(
        result_kernel,
        shape((64, width // seq_count), F32),
        [VMEM],
        "result",
        flops=group * 24 * 128,
        moved=2 * group * 24 * 128,
    )(every_total)
    return dmd.T[None], grad.T


def solution(mesh):
    placed = (
        P("dp", "seq", None),
        P(),
        P(),
        P("dp", "seq", None),
        P("dp"),
        P(),
        P(),
        P(None, None, None, "seq"),
        P(),
        P(),
    )
    return jax.shard_map(
        per_device,
        mesh=mesh,
        in_specs=placed,
        out_specs=(P("dp", "seq", None), P("seq", None)),
        check_vma=False,
    )
```

time: 82.2 us -> 78.1 us (0.950)
  the two profiles are of different devices: /device:TPU:32 before, /device:TPU:1 now
where the time goes in v2:
time: 78.1 us; the launch traced here: 77.4 us
  starting transfers between devices  24.1 us (31%)
  waiting for transfers between devices  20.6 us (26%)
  Pallas kernels  15.1 us (19%)
  blocking collectives  9.1 us (12%)
  local copies, waits for them, and re-layouts  7.1 us (9%)
  between operations  1.41 us (2%)
    all_to_all x1, waiting for transfers between devices, per_device(): velocities = lax.all_to_all(send, ('mp', 'seq'), 0, 0)  11.8 us
    all_to_all x1, blocking collectives, per_device(): partials = lax.all_to_all(send, 'seq', 0, 0)  9.1 us
    all_to_all x1, starting transfers between devices, per_device(): velocities = lax.all_to_all(send, ('mp', 'seq'), 0, 0)  8.92 us
    all_to_all x1, waiting for transfers between devices, per_device(): every_total = lax.all_to_all(send, ('mp', 'dp'), 0, 0)  8.8 us
    all_to_all x1, starting transfers between devices, per_device(): every_total = lax.all_to_all(send, ('mp', 'dp'), 0, 0)  7.98 us
    all_to_all x1, starting transfers between devices, per_device(): every_latent = lax.all_to_all(send, 'seq', 0, 0)  7.18 us
    unnamed x24, local copies, waits for them, and re-layouts  7.1 us
    pallas_call x1, Pallas kernels, per_device(): call(attention_kernel, shape((4 * seq_count, part, 128), BF16), [VMEM] *...  4.75 us
  transfers between devices with their start and end apart: 3, of which 2 were waited for; matrix products, arithmetic and copies ran while one was open for 0% of the time, Pallas kernels for 7%

profile of v2, /device:TPU:1, one launch (start us, length us, event | category | flops | bytes accessed | tf_op | source)
XLA Modules:
  0.0 77.4 jit_solution(7700017316111244917)
XLA Ops:
  1.3 0.0 copy-start
  1.3 1.1 %copy-done = bf16[1,128,3072]{2,1,0:T(8,128)(2,1)S(1)} copy-done((bf16[1,128,3072]{2,1,0:T(8,128)(2,1)S(1)}, bf16[1,128,3072]{2,1,0:T(8,128)(2,1)}, u32[]{:S(2)}) %copy-start) | copy-done | bytes 786456
  2.4 0.0 copy-start.2
  2.4 1.0 %copy-done.2 = bf16[3072,64]{0,1:T(8,128)(2,1)S(1)} copy-done((bf16[3072,64]{0,1:T(8,128)(2,1)S(1)}, bf16[3072,64]{0,1:T(8,128)(2,1)}, u32[]{:S(2)}) %copy-start.2) | copy-done | bytes 393240
  3.4 0.0 copy-start.6
  3.4 0.7 copy-done.6
  4.1 0.7 copy-done.8
  4.8 3.2 %latents.1 = bf16[16,64,128]{2,1,0:T(8,128)(2,1)} custom-call(s32[1]{0:T(128)S(6)} %copy.12.steps_ref, bf16[128,3072]{1,0:T(8,128)(2,1)S(1)} %bitcast.13, bf16[3072]{0:T(1024)(128)(2,1)S(1)} %copy-done.8, bf16[64,3072]{1,0:T(8,128)(2,1)S(1)} %bitcast.15, bf16[64,128]{1,0:T(8,128)(2,1)S(1)} %bitcast.18), custom_call_target="tpu_custom_call" | custom-call | flops 50331648 | bytes 786432 | tf_op jit(solution)/shard_map/latents/pallas_call | solution.py:304
  8.0 7.2 %all-to-all-start = ((bf16[16,64,128]{2,1,0:T(8,128)(2,1)}), bf16[16,64,128]{2,1,0:T(8,128)(2,1)S(1)}, u32[]{:S(2)}, u32[]{:S(2)}) async-start(bf16[16,64,128]{2,1,0:T(8,128)(2,1)} %latents.1), calls=%async_computation | async-start | bytes 524288 | tf_op jit(solution)/shard_map/all_to_all | solution.py:313
  15.2 0.1 fusion
  15.3 0.0 copy-start.4
  15.3 1.1 %copy-done.4 = bf16[2,64,3072]{2,1,0:T(8,128)(2,1)S(1)} copy-done((bf16[2,64,3072]{2,1,0:T(8,128)(2,1)S(1)}, bf16[2,64,3072]{2,1,0:T(8,128)(2,1)}, u32[]{:S(2)}) %copy-start.4) | copy-done | bytes 786456
  16.4 1.0 %copy-done.5 = bf16[2,2048,64]{1,2,0:T(8,128)(2,1)S(1)} copy-done((bf16[2,2048,64]{1,2,0:T(8,128)(2,1)S(1)}, bf16[2,2048,64]{1,2,0:T(8,128)(2,1)}, u32[]{:S(2)}) %copy-start.5) | copy-done | bytes 524312
  17.5 0.7 copy-done.10
  18.2 0.7 copy-done.11
  18.9 3.5 %fold.1 = (bf16[2,384,256]{2,1,0:T(8,128)(2,1)S(1)}, f32[2,128,128]{2,1,0:T(8,128)S(1)}, f32[8,128]{1,0:T(8,128)S(1)}) custom-call(f32[1,3072]{1,0:T(1,128)S(1)} %bitcast.20, bf16[2,64,3072]{2,1,0:T(8,128)(2,1)S(1)} %copy-done.4, bf16[2,3072]{1,0:T(2,128)(2,1)S(1)} %copy-done.10, bf16[2,3,3072,128]{3,2,1,0:T(8,128)(2,1)} %bitcast.21, ...), custom_call_target="tpu_custom_call" | custom-call | flops 1207959552 | bytes 4718592 | tf_op jit(solution)/shard_map/fold/pallas_call | solution.py:316
  22.4 0.0 all-to-all-done.latent_ref
  22.4 4.8 %attention.1 = bf16[64,32,128]{2,1,0:T(8,128)(2,1)} custom-call(bf16[16,64,128]{2,1,0:T(8,128)(2,1)S(1)} %all-to-all-done.latent_ref, bf16[2,384,256]{2,1,0:T(8,128)(2,1)S(1)} %get-tuple-element.10.fold_ref, f32[2,128,128]{2,1,0:T(8,128)S(1)} %get-tuple-element.11.scale_ref, f32[8,128]{1,0:T(8,128)S(1)} %get-tuple-element.12.square_ref), custom_call_target="tpu_custom_call" | custom-call | flops 1073741824 | bytes 262144 | tf_op jit(solution)/shard_map/attention/pallas_call | solution.py:340
  27.2 8.9 %all-to-all-start.1 = ((bf16[64,32,128]{2,1,0:T(8,128)(2,1)}), bf16[64,32,128]{2,1,0:T(8,128)(2,1)S(1)}, u32[]{:S(2)}, u32[]{:S(2)}) async-start(bf16[64,32,128]{2,1,0:T(8,128)(2,1)} %attention.1), calls=%async_computation.1 | async-start | bytes 1048576 | tf_op jit(solution)/shard_map/all_to_all | solution.py:349
  36.1 0.0 copy-done.1
  36.1 0.0 copy-done.3
  36.1 0.0 copy-done.7
  36.1 0.0 copy-done.9
  36.2 1.0 %own.1 = (bf16[768,128]{1,0:T(8,128)(2,1)S(1)}, f32[128,128]{1,0:T(8,128)S(1)}, f32[128,128]{1,0:T(8,128)S(1)}) custom-call(s32[1]{0:T(128)S(6)} %copy.12.steps_ref, bf16[128,3072]{1,0:T(8,128)(2,1)S(1)} %bitcast.14, bf16[3072]{0:T(1024)(128)(2,1)S(1)} %copy-done.9, bf16[64,3072]{1,0:T(8,128)(2,1)S(1)} %bitcast.16, bf16[64,128]{1,0:T(8,128)(2,1)S(1)} %bitcast.19), custom_call_target="tpu_custom_call" | custom-call | flops 50331648 | bytes 786432 | tf_op jit(solution)/shard_map/own/pallas_call | solution.py:350
  37.1 11.8 %all-to-all-done.1.velocity_ref = bf16[64,32,128]{2,1,0:T(8,128)(2,1)S(1)} async-done(((bf16[64,32,128]{2,1,0:T(8,128)(2,1)}), bf16[64,32,128]{2,1,0:T(8,128)(2,1)S(1)}, u32[]{:S(2)}, u32[]{:S(2)}) %all-to-all-start.1) | async-done | bytes 524320 | tf_op jit(solution)/shard_map/all_to_all | solution.py:349
  48.9 0.4 gap.1
  49.3 9.1 %all_to_all.20.grad_ref = bf16[16,32,128]{2,1,0:T(8,128)(2,1)S(1)} all-to-all(bf16[16,32,128]{2,1,0:T(8,128)(2,1)S(1)} %get-tuple-element.16), channel_id=1, replica_groups=mesh['mp'=4,'seq'=16,'dp'=4] {'seq'}, dimensions={0} | all-to-all | bytes 262144 | tf_op jit(solution)/shard_map/all_to_all | solution.py:367
  58.4 0.7 total.1
  59.1 8.0 %all-to-all-start.3 = ((bf16[16,24,128]{2,1,0:T(8,128)(2,1)}), bf16[16,24,128]{2,1,0:T(8,128)(2,1)S(1)}, u32[]{:S(2)}, u32[]{:S(2)}) async-start(bf16[16,24,128]{2,1,0:T(8,128)(2,1)} %total.1), calls=%async_computation.3 | async-start | bytes 196608 | tf_op jit(solution)/shard_map/all_to_all | solution.py:376
  67.1 0.7 dmd.1
  67.8 8.8 %all-to-all-done.3.all_ref = bf16[16,24,128]{2,1,0:T(8,128)(2,1)S(1)} async-done(((bf16[16,24,128]{2,1,0:T(8,128)(2,1)}), bf16[16,24,128]{2,1,0:T(8,128)(2,1)S(1)}, u32[]{:S(2)}, u32[]{:S(2)}) %all-to-all-start.3) | async-done | bytes 98336 | tf_op jit(solution)/shard_map/all_to_all | solution.py:376
  76.6 0.8 %result.1 = f32[64,192]{1,0:T(8,128)} custom-call(bf16[16,24,128]{2,1,0:T(8,128)(2,1)S(1)} %all-to-all-done.3.all_ref), custom_call_target="tpu_custom_call" | custom-call | flops 49152 | bytes 98304 | tf_op jit(solution)/shard_map/result/pallas_call | solution.py:385
  (9 shorter events, 0.0 us)
Async XLA Ops:
  1.3 1.1 %copy-start = (bf16[1,128,3072]{2,1,0:T(8,128)(2,1)S(1)}, bf16[1,128,3072]{2,1,0:T(8,128)(2,1)}, u32[]{:S(2)}) copy-start(bf16[1,128,3072]{2,1,0:T(8,128)(2,1)} %param.10) | copy-start | bytes 2359300
  2.4 1.0 %copy-start.2 = (bf16[3072,64]{0,1:T(8,128)(2,1)S(1)}, bf16[3072,64]{0,1:T(8,128)(2,1)}, u32[]{:S(2)}) copy-start(bf16[3072,64]{0,1:T(8,128)(2,1)} %param.12) | copy-start | bytes 1179652
  3.4 0.7 copy-start.6
  4.1 0.7 copy-start.8
  8.0 14.4 %all-to-all-start = ((bf16[16,64,128]{2,1,0:T(8,128)(2,1)}), bf16[16,64,128]{2,1,0:T(8,128)(2,1)S(1)}, u32[]{:S(2)}, u32[]{:S(2)}) async-start(bf16[16,64,128]{2,1,0:T(8,128)(2,1)} %latents.1), calls=%async_computation | async-start | bytes 524288 | tf_op jit(solution)/shard_map/all_to_all | solution.py:313
  15.3 1.1 %copy-start.4 = (bf16[2,64,3072]{2,1,0:T(8,128)(2,1)S(1)}, bf16[2,64,3072]{2,1,0:T(8,128)(2,1)}, u32[]{:S(2)}) copy-start(bf16[2,64,3072]{2,1,0:T(8,128)(2,1)} %embed_hbm.1) | copy-start | bytes 2359300
  16.4 1.0 %copy-start.5 = (bf16[2,2048,64]{1,2,0:T(8,128)(2,1)S(1)}, bf16[2,2048,64]{1,2,0:T(8,128)(2,1)}, u32[]{:S(2)}) copy-start(bf16[2,2048,64]{1,2,0:T(8,128)(2,1)} %param.19) | copy-start | bytes 1572868
  17.5 0.7 copy-start.10
  18.2 0.7 copy-start.11
  18.9 17.3 %copy-start.1 = (bf16[1,128,3072]{2,1,0:T(8,128)(2,1)S(1)}, bf16[1,128,3072]{2,1,0:T(8,128)(2,1)}, u32[]{:S(2)}) copy-start(bf16[1,128,3072]{2,1,0:T(8,128)(2,1)} %param.10) | copy-start | bytes 2359300
  18.9 17.3 %copy-start.3 = (bf16[3072,64]{0,1:T(8,128)(2,1)S(1)}, bf16[3072,64]{0,1:T(8,128)(2,1)}, u32[]{:S(2)}) copy-start(bf16[3072,64]{0,1:T(8,128)(2,1)} %param.12) | copy-start | bytes 1179652
  18.9 17.3 %copy-start.7 = (bf16[1,128,64]{1,2,0:T(8,128)(2,1)S(1)}, bf16[1,128,64]{1,2,0:T(8,128)(2,1)}, u32[]{:S(2)}) copy-start(bf16[1,128,64]{1,2,0:T(8,128)(2,1)} %param.13) | copy-start | bytes 49156
  18.9 17.3 %copy-start.9 = (bf16[3072]{0:T(1024)(128)(2,1)S(1)}, bf16[3072]{0:T(1024)(128)(2,1)}, u32[]{:S(2)}) copy-start(bf16[3072]{0:T(1024)(128)(2,1)} %gain_hbm.5) | copy-start | bytes 18436
  27.2 21.7 %all-to-all-start.1 = ((bf16[64,32,128]{2,1,0:T(8,128)(2,1)}), bf16[64,32,128]{2,1,0:T(8,128)(2,1)S(1)}, u32[]{:S(2)}, u32[]{:S(2)}) async-start(bf16[64,32,128]{2,1,0:T(8,128)(2,1)} %attention.1), calls=%async_computation.1 | async-start | bytes 1048576 | tf_op jit(solution)/shard_map/all_to_all | solution.py:349
  59.1 17.5 %all-to-all-start.3 = ((bf16[16,24,128]{2,1,0:T(8,128)(2,1)}), bf16[16,24,128]{2,1,0:T(8,128)(2,1)S(1)}, u32[]{:S(2)}, u32[]{:S(2)}) async-start(bf16[16,24,128]{2,1,0:T(8,128)(2,1)} %total.1), calls=%async_computation.3 | async-start | bytes 196608 | tf_op jit(solution)/shard_map/all_to_all | solution.py:376

commit v3 on v2

v3 whole, which is shorter than its diff:
```python
import math

import jax
import jax.numpy as jnp
from jax import lax
from jax.experimental import pallas as pl
from jax.experimental.pallas import tpu as pltpu
from jax.sharding import PartitionSpec as P

F32 = jnp.float32
BF16 = jnp.bfloat16
STEPS = 1000
NN = (((1,), (0,)), ((), ()))
NT = (((1,), (1,)), ((), ()))
TN = (((0,), (0,)), ((), ()))
VMEM = pl.BlockSpec(memory_space=pltpu.VMEM)
SMEM = pl.BlockSpec(memory_space=pltpu.SMEM)
HBM = pl.BlockSpec(memory_space=pltpu.HBM)
MEBI = 1024 * 1024


def dot(left, right, dims=NN):
    return lax.dot_general(left, right, dims, preferred_element_type=F32)


def split_two(values):
    high = values.astype(BF16)
    low = (values - high.astype(F32)).astype(BF16)
    return high, low


def level_of(steps_ref):
    return (steps_ref[0].astype(F32) + 1.0) * (1.0 / (STEPS + 1.0))


def time_embedding(step_value, width):
    half_width = width // 2
    ranks = lax.broadcasted_iota(jnp.int32, (1, half_width), 1).astype(F32) / half_width
    phases = step_value * jnp.exp(-math.log(10000.0) * ranks)
    return jnp.concatenate([jnp.cos(phases), jnp.sin(phases)], axis=1)


def scaled_and_rms(features, gain):
    features_f = features.astype(F32)
    mean_square = jnp.sum(features_f * features_f, axis=1, keepdims=True) / features.shape[1]
    return (features_f * gain).astype(BF16), lax.rsqrt(mean_square + 1e-06)


def latents_kernel(steps_ref, features_hbm, gain_hbm, weight_hbm, noise_hbm, send_ref, features, gain, weight, noise, sems):
    half = lax.axis_index("mp") // 2
    tokens, width = features.shape
    part = tokens // 2
    copies = [
        pltpu.make_async_copy(gain_hbm, gain, sems.at[4]),
        pltpu.make_async_copy(weight_hbm, weight, sems.at[5]),
        pltpu.make_async_copy(noise_hbm, noise, sems.at[6]),
    ]
    halves = []
    for i in range(2):
        start = pl.multiple_of(((half + i) % 2) * part, part)
        rows = features.at[pl.ds(i * part, part), :]
        halves.append(pltpu.make_async_copy(features_hbm.at[pl.ds(start, part), :], rows, sems.at[i]))
    for copy in copies[:1] + halves + copies[1:]:
        copy.start()
    level = level_of(steps_ref)
    copies[0].wait()
    gain_row = gain[...].astype(F32).reshape(1, width)
    scaled, inverse = [], []
    for i in range(2):
        halves[i].wait()
        one, inv_rms = scaled_and_rms(features[i * part : (i + 1) * part, :], gain_row)
        scaled.append(one)
        inverse.append(inv_rms)
    inv_row = jnp.broadcast_to(jnp.concatenate(inverse, axis=0), (tokens, tokens)).T[0:1]
    copies[1].wait()
    clean = dot(weight[...], jnp.concatenate(scaled, axis=0), NT) * inv_row
    copies[2].wait()
    noise_here = pltpu.roll(noise[...].astype(F32), (tokens - half * part) % tokens, 1)
    rounded = ((1.0 - level) * clean + level * noise_here).astype(BF16)
    for target in range(send_ref.shape[0]):
        send_ref[target] = rounded


def own_kernel(steps_ref, features_hbm, gain_hbm, weight_hbm, noise_hbm, picked_ref, own_ref, inv_ref, features, gain, weight, noise, turned, sems):
    slot = lax.axis_index("mp")
    width = features.shape[1]
    pairs = ((gain_hbm, gain), (features_hbm, features), (weight_hbm, weight), (noise_hbm, noise))
    copies = [pltpu.make_async_copy(source, target, sems.at[i]) for i, (source, target) in enumerate(pairs)]
    for copy in copies:
        copy.start()
    for copy in copies:
        copy.wait()
    level = level_of(steps_ref)
    scaled, inv_rms = scaled_and_rms(features[...], gain[...].astype(F32).reshape(1, width))
    inv_row = jnp.broadcast_to(inv_rms, (128, 128)).T[0:1]
    inv_ref[...] = jnp.broadcast_to(inv_row, inv_ref.shape)
    clean = dot(weight[...], scaled, NT) * inv_row
    own_ref[0:64, :] = clean
    own_ref[64:128, :] = (1.0 - level) * clean + level * noise[...].astype(F32)
    turned[...] = scaled.T
    for s in range(16):
        start = pl.multiple_of(s * 192 + slot * 48, 16)
        picked_ref[s * 48 : (s + 1) * 48, :] = turned[pl.ds(start, 48), :]


def fold_kernel(steps_ref, embed_hbm, gain_hbm, qkv_hbm, qk_hbm, out_hbm, fold_ref, scale_ref, embed, gain, qkv, qk, out, sems):
    model = lax.axis_index("mp") % 2
    head = lax.axis_index("seq")
    width = embed.shape[1]
    parts = 3
    chunk = width // parts
    columns = pl.ds(pl.multiple_of(head * 128, 128), 128)
    pairs = ((embed_hbm.at[model], embed), (gain_hbm, gain), (qk_hbm.at[model], qk), (out_hbm.at[model, :, columns], out))
    copies = [pltpu.make_async_copy(source, target, sems.at[i]) for i, (source, target) in enumerate(pairs)]
    pieces = []
    for k in range(parts):
        span = pl.ds(k * chunk, chunk)
        pieces.append(pltpu.make_async_copy(qkv_hbm.at[model, :, span, :], qkv.at[:, span, :], sems.at[4 + k]))
    for copy in copies + pieces:
        copy.start()
    temb = time_embedding(steps_ref[0].astype(F32), width)
    squares = jnp.sum(temb * temb, axis=1, keepdims=True)
    spot = lax.broadcasted_iota(jnp.int32, (16, width), 0)
    temb_one = temb.astype(BF16).astype(F32)
    temb_two = (temb - temb_one).astype(BF16).astype(F32)
    temb_three = temb - temb_one - temb_two
    temb_rows = jnp.where(spot == 0, temb_one, jnp.where(spot == 1, temb_two, jnp.where(spot == 2, temb_three, 0.0))).astype(BF16)
    for copy in copies:
        copy.wait()
    gain_row = jnp.where(model == 0, gain[0:1, :].astype(F32), gain[1:2, :].astype(F32))
    table = embed[...]
    high, low = split_two(table.astype(F32) * gain_row)
    biased = temb * gain_row
    bias_high = biased.astype(BF16).astype(F32)
    bias_rows = jnp.where(spot == 0, bias_high, jnp.where(spot == 1, biased - bias_high, 0.0)).astype(BF16)
    rows = jnp.concatenate([high, low, bias_rows], axis=0)
    pads = jnp.zeros((48, width), BF16)
    inner = dot(table, jnp.concatenate([table, temb_rows, pads], axis=0), NT)
    acc = jnp.zeros((144, 384), F32)
    for k in range(parts):
        pieces[k].wait()
        span = slice(k * chunk, (k + 1) * chunk)
        acc += dot(rows[:, span], jnp.concatenate([qkv[i, span, :] for i in range(3)], axis=1))
    lane = lax.broadcasted_iota(jnp.int32, (64, 128), 1)
    row = lax.broadcasted_iota(jnp.int32, (64, 128), 0)

    def stacked(i):
        whole = acc[:, i * 128 : (i + 1) * 128]
        bias = whole[128:129] + whole[129:130]
        return jnp.concatenate([whole[0:64] + whole[64:128], jnp.where(row == 0, bias, 0.0)], axis=0)

    value_high, value_low = split_two(stacked(2))
    mixed = dot(out[...], value_high, NT) + dot(out[...], value_low, NT)
    linear = inner[:, 64:65] + inner[:, 65:66] + inner[:, 66:67]
    inner = jnp.where(lane < 64, inner, jnp.where(lane == 64, 2.0 * linear, 0.0))
    high, low = split_two(jnp.concatenate([stacked(1).T, mixed, inner, stacked(0).T], axis=0))
    fold_ref[...] = jnp.concatenate([high, low], axis=1)
    gains = qk[0:1, :].astype(F32) * qk[1:2, :].astype(F32) * (math.log2(math.e) / math.sqrt(128.0))
    scale_ref[0:128, :] = jnp.broadcast_to(gains, (128, 128)).T
    scale_ref[128:136, :] = jnp.broadcast_to(squares, (8, 128))


def packed(block, odd):
    left = lax.broadcasted_iota(jnp.int32, (32, 128), 1) < 64
    if odd:
        return jnp.where(left, pltpu.roll(block[0:32], 64, 1), block[32:64])
    return jnp.where(left, block[0:32], pltpu.roll(block[32:64], 64, 1))


def attention_kernel(latent_hbm, fold_hbm, scale_hbm, send_ref, latent_ref, fold_ref, scale_ref, latents, queries, sems):
    pairs = ((latent_hbm, latent_ref), (fold_hbm, fold_ref), (scale_hbm, scale_ref))
    copies = [pltpu.make_async_copy(source, target, sems.at[i]) for i, (source, target) in enumerate(pairs)]
    for copy in copies:
        copy.start()
    blocks = latent_ref.shape[0]
    keys = blocks * 128
    count = blocks * 64
    for table in (latents, queries):
        table[64:128, :] = jnp.ones((64, table.shape[1]), BF16)
        table[192:256, :] = jnp.ones((64, table.shape[1]), BF16)
    copies[0].wait()
    for s in range(blocks):
        block = latent_ref[s]
        latents[0:64, s * 128 : (s + 1) * 128] = block
        latents[128:192, s * 128 : (s + 1) * 128] = block
    for g in range(blocks // 2):
        pieces = jnp.concatenate([latent_ref[2 * g + i][:, 0:64] for i in range(2)], axis=1)
        queries[0:64, g * 128 : (g + 1) * 128] = pieces
        queries[128:192, g * 128 : (g + 1) * 128] = pieces
    for copy in copies[1:]:
        copy.wait()
    squares = scale_ref[128:129, 0:1]

    def hidden_square(inner, rows):
        return (jnp.sum(inner * rows.astype(F32), axis=0, keepdims=True) + squares) / 3072.0 + 1e-06

    projected = dot(fold_ref[0:256], latents[...])
    hidden = hidden_square(projected[192:256], latents[0:64])
    key = projected[0:128]
    key_scale = lax.rsqrt(jnp.mean(key * key, axis=0, keepdims=True) + 1e-06 * hidden)
    key = (key * key_scale).astype(BF16).T
    value = (projected[128:192] * lax.rsqrt(hidden)).astype(BF16)
    value = jnp.concatenate([value, jnp.ones((16, keys), BF16)], axis=0)
    projected = dot(fold_ref[192:384], queries[...])
    hidden = hidden_square(projected[0:64], queries[0:64])
    query = projected[64:192]
    query_scale = lax.rsqrt(jnp.mean(query * query, axis=0, keepdims=True) + 1e-06 * hidden)
    query = query * query_scale * jnp.concatenate([scale_ref[0:128]] * (count // 128), axis=1)
    query = query.astype(BF16)
    total = jnp.zeros((80, count), F32)
    step = 512
    for c in range(keys // step):
        span = slice(c * step, (c + 1) * step)
        shares = jnp.exp2(dot(key[span], query)).astype(BF16)
        total += dot(value[:, span], shares)
    mixed = total[0:64] / total[64:65]
    for s in range(blocks):
        send_ref[s] = packed(mixed[:, (s // 2) * 128 : (s // 2 + 1) * 128], s % 2).astype(BF16)


def sum_kernel(part_ref, send_ref):
    send_ref[...] = jnp.sum(part_ref[...].astype(F32), axis=0)


def gap_kernel(steps_ref, zero_ref, one_ref, two_ref, three_ref, picked_ref, own_ref, inv_ref, send_ref, gap_ref, every):
    level = level_of(steps_ref)
    blocks = send_ref.shape[0]
    slot = lax.axis_index("mp")
    for k, ref in enumerate((zero_ref, one_ref, two_ref, three_ref)):
        every[slot ^ k] = ref[...]
    left = lax.broadcasted_iota(jnp.int32, (64, 128), 1) < 64

    def velocity(model):
        first, second = every[model], every[model + 2]
        first = jnp.concatenate([first, pltpu.roll(first, 64, 1)], axis=0)
        second = jnp.concatenate([pltpu.roll(second, 64, 1), second], axis=0)
        return jnp.where(left, first, second)

    teacher = velocity(0)
    gap = level * (teacher - velocity(1))
    gap_ref[...] = gap
    distance = jnp.abs(own_ref[0:64] - (own_ref[64:128] - level * teacher))
    spread = jnp.sum(jnp.sum(distance, axis=1, keepdims=True), axis=0, keepdims=True)
    direction = (gap * inv_ref[0:1]).astype(BF16)
    grad = dot(picked_ref[...], jnp.concatenate([direction, direction], axis=0), NT)
    spread = jnp.broadcast_to(spread, (8, 128))
    spot = lax.broadcasted_iota(jnp.int32, (8, 128), 0)
    high = spread.astype(BF16).astype(F32)
    tail = jnp.where(spot == 0, high, jnp.where(spot == 1, spread - high, 0.0))
    left = lax.broadcasted_iota(jnp.int32, (24, 128), 1) < 64
    for s in range(blocks):
        packed = jnp.where(left, grad[s * 48 : s * 48 + 24], grad[s * 48 + 24 : s * 48 + 48])
        send_ref[s] = jnp.concatenate([packed, tail], axis=0).astype(BF16)


def weight_inverse(total):
    return 1.0 / ((total[24:25] + total[25:26]) / 131072.0 + 1e-05)


def total_kernel(grad_ref, send_ref, inverse_ref):
    total = jnp.sum(grad_ref[...].astype(F32), axis=0)
    inverse = weight_inverse(total)
    inverse_ref[...] = jnp.broadcast_to(inverse, inverse_ref.shape)
    whole = (total[0:24] * inverse).astype(BF16)
    for target in range(send_ref.shape[0]):
        send_ref[target] = whole


def result_kernel(all_ref, gap_ref, inverse_ref, dmd_ref, grad_ref):
    dmd_ref[...] = gap_ref[...] * inverse_ref[0:1]
    rows = []
    for m in range(4):
        total = jnp.sum(all_ref[4 * m : 4 * m + 4].astype(F32), axis=0)
        rows += [total, pltpu.roll(total, 64, 1)]
    rows.append(jnp.zeros((64, 128), F32))
    grad_ref[...] = jnp.concatenate(rows, axis=0).T[0:64, 0:192]


def call(kernel, outs, in_specs, name, flops=0, moved=0, grant=32, **more):
    return pl.pallas_call(
        kernel,
        out_shape=outs,
        in_specs=in_specs,
        out_specs=more.pop("out_specs", jax.tree.map(lambda _: VMEM, outs)),
        compiler_params=pltpu.CompilerParams(vmem_limit_bytes=grant * MEBI),
        cost_estimate=pl.CostEstimate(flops=flops, bytes_accessed=moved, transcendentals=0),
        name=name,
        **more,
    )


def per_device(
    gen_features,
    gen_gain,
    gen_weight,
    flow_noise,
    time_steps,
    embed_weight,
    norm_gain,
    qkv_weight,
    qk_gain,
    out_weight,
):
    shape = jax.ShapeDtypeStruct
    seq_count = lax.axis_size("seq")
    group = lax.axis_size("mp") * lax.axis_size("dp")
    features = gen_features[0]
    tokens, width = features.shape
    local = (time_steps, features, gen_gain, gen_weight.T, flow_noise[0].T)
    buffers = [
        pltpu.VMEM((tokens, width), BF16),
        pltpu.VMEM((width,), BF16),
        pltpu.VMEM((64, width), BF16),
        pltpu.VMEM((64, tokens), BF16),
    ]
    send = call(
        latents_kernel,
        shape((seq_count, 64, tokens), BF16),
        [SMEM] + [HBM] * 4,
        "latents",
        grant=60,
        flops=2 * tokens * width * 64,
        moved=2 * tokens * width,
        scratch_shapes=buffers + [pltpu.SemaphoreType.DMA((7,))],
    )(*local)
    every_latent = lax.all_to_all(send, "seq", 0, 0)

    fold, scale = call(
        fold_kernel,
        (shape((384, 256), BF16), shape((136, 128), F32)),
        [SMEM] + [HBM] * 5,
        "fold",
        grant=60,
        flops=2 * width * 384 * 256,
        moved=2 * width * 384,
        scratch_shapes=[
            pltpu.VMEM((64, width), BF16),
            pltpu.VMEM((2, width), BF16),
            pltpu.VMEM((3, width, 128), BF16),
            pltpu.VMEM((2, 128), BF16),
            pltpu.VMEM((64, 128), BF16),
            pltpu.SemaphoreType.DMA((7,)),
        ],
    )(
        time_steps,
        embed_weight,
        norm_gain,
        qkv_weight.transpose(0, 2, 1, 3),
        qk_gain,
        out_weight.transpose(0, 2, 1),
    )
    keys = seq_count * tokens
    send = call(
        attention_kernel,
        shape((seq_count, 32, 128), BF16),
        [HBM] * 3,
        "attention",
        grant=60,
        flops=2 * keys * (keys // 2) * 256,
        moved=2 * keys * 64,
        scratch_shapes=[
            pltpu.VMEM((seq_count, 64, tokens), BF16),
            pltpu.VMEM((384, 256), BF16),
            pltpu.VMEM((136, 128), F32),
            pltpu.VMEM((256, keys), BF16),
            pltpu.VMEM((256, keys // 2), BF16),
            pltpu.SemaphoreType.DMA((3,)),
        ],
    )(every_latent, fold, scale)
    every_part = lax.all_to_all(send, "seq", 0, 0)
    send = call(sum_kernel, shape((32, 128), F32), [VMEM], "sum", moved=2 * seq_count * 32 * 128)(every_part)
    velocities = [send] + [lax.ppermute(send, "mp", [(i, i ^ k) for i in range(4)]) for k in range(1, 4)]
    picked, own, inv = call(
        own_kernel,
        (shape((width // 4, tokens), BF16), shape((128, tokens), F32), shape((8, tokens), F32)),
        [SMEM] + [HBM] * 4,
        "own",
        flops=2 * tokens * width * 64,
        moved=2 * tokens * width,
        scratch_shapes=buffers + [pltpu.VMEM((width, tokens), BF16), pltpu.SemaphoreType.DMA((4,))],
    )(*local)
    send, gap = call(
        gap_kernel,
        (shape((seq_count, 32, 128), BF16), shape((64, tokens), F32)),
        [SMEM] + [VMEM] * 7,
        "gap",
        flops=2 * tokens * width * 16,
        moved=2 * 64 * 32 * 128,
        scratch_shapes=[pltpu.VMEM((4, 32, 128), F32)],
    )(time_steps, *velocities, picked, own, inv)
    partials = lax.all_to_all(send, "seq", 0, 0)
    send, inverse = call(
        total_kernel,
        (shape((group, 24, 128), BF16), shape((8, 128), F32)),
        [VMEM],
        "total",
        flops=seq_count * 32 * 128,
        moved=2 * seq_count * 32 * 128,
    )(partials)
    every_total = lax.all_to_all(send, ("mp", "dp"), 0, 0)
    dmd, grad = call(
        result_kernel,
        (shape((64, tokens), F32), shape((64, width // seq_count), F32)),
        [VMEM] * 3,
        "result",
        flops=group * 24 * 128,
        moved=2 * group * 24 * 128,
    )(every_total, gap, inverse)
    return dmd.T[None], grad.T


def solution(mesh):
    placed = (
        P("dp", "seq", None),
        P(),
        P(),
        P("dp", "seq", None),
        P("dp"),
        P(),
        P(),
        P(None, None, None, "seq"),
        P(),
        P(),
    )
    return jax.shard_map(
        per_device,
        mesh=mesh,
        in_specs=placed,
        out_specs=(P("dp", "seq", None), P("seq", None)),
        check_vma=False,
    )
```

time: 78.1 us -> 71.2 us (0.912)
  the two profiles are of different devices: /device:TPU:1 before, /device:TPU:32 now
where the time goes in v3:
time: 71.2 us; the launch traced here: 69.9 us
  blocking collectives  37.4 us (53%)
  Pallas kernels  12.7 us (18%)
  starting transfers between devices  10.6 us (15%)
  waiting for transfers between devices  7.16 us (10%)
  between operations  1.36 us (2%)
  local copies, waits for them, and re-layouts  0.73 us (1%)
    all_to_all x1, blocking collectives, per_device(): every_total = lax.all_to_all(send, ('mp', 'dp'), 0, 0)  18.2 us
    all_to_all x1, blocking collectives, per_device(): every_part = lax.all_to_all(send, 'seq', 0, 0)  9.94 us
    all_to_all x1, blocking collectives, per_device(): partials = lax.all_to_all(send, 'seq', 0, 0)  9.31 us
    all_to_all x1, starting transfers between devices, per_device(): every_latent = lax.all_to_all(send, 'seq', 0, 0)  5.78 us
    ppermute x3, starting transfers between devices, per_device(): lax.ppermute(send, 'mp', [(i, i ^ k) for i in range(4)])  4.78 us
    pallas_call x1, Pallas kernels, per_device(): call(attention_kernel, shape((seq_count, 32, 128), BF16), [HBM] * 3, 'att...  4.41 us
    ppermute x3, waiting for transfers between devices, per_device(): lax.ppermute(send, 'mp', [(i, i ^ k) for i in range(4)])  3.77 us
    all_to_all x1, waiting for transfers between devices, per_device(): every_latent = lax.all_to_all(send, 'seq', 0, 0)  3.4 us
  transfers between devices with their start and end apart: 4, of which 3 were waited for; matrix products, arithmetic and copies ran while one was open for 0% of the time, Pallas kernels for 6%

profile of v3, /device:TPU:32, one launch (start us, length us, event | category | flops | bytes accessed | tf_op | source)
XLA Modules:
  0.0 69.9 jit_solution(6807416166980590378)
XLA Ops:
  1.3 2.8 %latents.1 = bf16[16,64,128]{2,1,0:T(8,128)(2,1)} custom-call(s32[1]{0:T(128)S(6)} %copy.12.steps_ref, bf16[128,3072]{1,0:T(8,128)(2,1)} %bitcast.11, bf16[3072]{0:T(1024)(128)(2,1)} %gain_hbm.5, bf16[64,3072]{1,0:T(8,128)(2,1)} %bitcast.13, bf16[64,128]{1,0:T(8,128)(2,1)} %bitcast.15), custom_call_target="tpu_custom_call" | custom-call | flops 50331648 | bytes 786432 | tf_op jit(solution)/shard_map/latents/pallas_call | solution.py:316
  4.1 5.8 %all-to-all-start = ((bf16[16,64,128]{2,1,0:T(8,128)(2,1)}), bf16[16,64,128]{2,1,0:T(8,128)(2,1)S(1)}, u32[]{:S(2)}, u32[]{:S(2)}) async-start(bf16[16,64,128]{2,1,0:T(8,128)(2,1)} %latents.1), calls=%async_computation | async-start | bytes 524288 | tf_op jit(solution)/shard_map/all_to_all | solution.py:326
  9.9 0.0 copy-start
  9.9 0.0 copy-start.1
  9.9 0.0 copy-start.2
  9.9 0.0 copy-start.3
  9.9 3.3 %fold.1 = (bf16[384,256]{1,0:T(8,128)(2,1)}, f32[136,128]{1,0:T(8,128)}) custom-call(s32[1]{0:T(128)S(6)} %copy.12.steps_ref, bf16[2,64,3072]{2,1,0:T(8,128)(2,1)} %embed_hbm.1, bf16[2,3072]{1,0:T(2,128)(2,1)} %gain_hbm.4, bf16[2,3,3072,128]{3,2,1,0:T(8,128)(2,1)} %bitcast.17, bf16[2,2,128]{2,1,0:T(2,128)(2,1)} %qk_hbm.1, bf16[2,64,2048]{2,1,0:T(8,128)(2,1)} %bitcast.18), custom_call_target="tpu_custom_call" | custom-call | flops 603979776 | bytes 2359296 | tf_op jit(solution)/shard_map/fold/pallas_call | solution.py:328
  13.3 3.4 %all-to-all-done.latent_hbm = bf16[16,64,128]{2,1,0:T(8,128)(2,1)S(1)} async-done(((bf16[16,64,128]{2,1,0:T(8,128)(2,1)}), bf16[16,64,128]{2,1,0:T(8,128)(2,1)S(1)}, u32[]{:S(2)}, u32[]{:S(2)}) %all-to-all-start) | async-done | bytes 262176 | tf_op jit(solution)/shard_map/all_to_all | solution.py:326
  16.7 0.0 copy-start.4
  16.7 0.7 %copy-done.4 = bf16[16,64,128]{2,1,0:T(8,128)(2,1)} copy-done((bf16[16,64,128]{2,1,0:T(8,128)(2,1)}, bf16[16,64,128]{2,1,0:T(8,128)(2,1)S(1)}, u32[]{:S(2)}) %copy-start.4) | copy-done | bytes 262168
  17.4 4.4 %attention.1 = bf16[16,32,128]{2,1,0:T(8,128)(2,1)} custom-call(bf16[16,64,128]{2,1,0:T(8,128)(2,1)} %copy-done.4, bf16[384,256]{1,0:T(8,128)(2,1)} %get-tuple-element.13.fold_hbm, f32[136,128]{1,0:T(8,128)} %get-tuple-element.14.scale_hbm), custom_call_target="tpu_custom_call" | custom-call | flops 1073741824 | bytes 262144 | tf_op jit(solution)/shard_map/attention/pallas_call | solution.py:353
  21.8 9.9 %all_to_all.20.part_ref = bf16[16,32,128]{2,1,0:T(8,128)(2,1)S(1)} all-to-all(bf16[16,32,128]{2,1,0:T(8,128)(2,1)} %attention.1), channel_id=1, replica_groups=mesh['mp'=4,'seq'=16,'dp'=4] {'seq'}, dimensions={0} | all-to-all | bytes 262144 | tf_op jit(solution)/shard_map/all_to_all | solution.py:370
  31.8 1.7 %collective-permute-start = (f32[32,128]{1,0:T(8,128)S(1)}, f32[32,128]{1,0:T(8,128)S(1)}, u32[]{:S(2)}, u32[]{:S(2)}) collective-permute-start(f32[32,128]{1,0:T(8,128)S(1)} %sum.1.zero_ref), channel_id=1, source_target_pairs={{0,64},{64,0},{128,192},{192,128},{1,65},{65,1},{129,193},{193,129... | collective-permute-start | bytes 49160 | tf_op jit(solution)/shard_map/ppermute | solution.py:372
  33.4 2.9 %collective-permute-start.1 = (f32[32,128]{1,0:T(8,128)S(1)}, f32[32,128]{1,0:T(8,128)S(1)}, u32[]{:S(2)}, u32[]{:S(2)}) collective-permute-start(f32[32,128]{1,0:T(8,128)S(1)} %sum.1.zero_ref), channel_id=1, source_target_pairs={{0,128},{64,192},{128,0},{192,64},{1,129},{65,193},{129,1},{193,65... | collective-permute-start | bytes 49160 | tf_op jit(solution)/shard_map/ppermute | solution.py:372
  36.3 0.2 collective-permute-start.2
  36.6 0.0 copy-done
  36.6 0.0 copy-done.1
  36.6 0.0 copy-done.2
  36.6 0.0 copy-done.3
  36.6 0.9 %own.1 = (bf16[768,128]{1,0:T(8,128)(2,1)S(1)}, f32[128,128]{1,0:T(8,128)S(1)}, f32[8,128]{1,0:T(8,128)S(1)}) custom-call(s32[1]{0:T(128)S(6)} %copy.12.steps_ref, bf16[128,3072]{1,0:T(8,128)(2,1)S(1)} %bitcast.12, bf16[3072]{0:T(1024)(128)(2,1)S(1)} %copy-done.3, bf16[64,3072]{1,0:T(8,128)(2,1)S(1)} %bitcast.14, bf16[64,128]{1,0:T(8,128)(2,1)S(1)} %bitcast.16), custom_call_target="tpu_custom_call" | custom-call | flops 50331648 | bytes 786432 | tf_op jit(solution)/shard_map/own/pallas_call | solution.py:373
  37.5 0.0 collective-permute-done.one_ref
  37.5 1.2 %collective-permute-done.1.two_ref = f32[32,128]{1,0:T(8,128)S(1)} collective-permute-done((f32[32,128]{1,0:T(8,128)S(1)}, f32[32,128]{1,0:T(8,128)S(1)}, u32[]{:S(2)}, u32[]{:S(2)}) %collective-permute-start.1) | collective-permute-done | bytes 16416 | tf_op jit(solution)/shard_map/ppermute | solution.py:372
  38.7 2.6 %collective-permute-done.2.three_ref = f32[32,128]{1,0:T(8,128)S(1)} collective-permute-done((f32[32,128]{1,0:T(8,128)S(1)}, f32[32,128]{1,0:T(8,128)S(1)}, u32[]{:S(2)}, u32[]{:S(2)}) %collective-permute-start.2) | collective-permute-done | bytes 16416 | tf_op jit(solution)/shard_map/ppermute | solution.py:372
  41.3 0.3 gap.1
  41.6 9.3 %all_to_all.21.grad_ref = bf16[16,32,128]{2,1,0:T(8,128)(2,1)S(1)} all-to-all(bf16[16,32,128]{2,1,0:T(8,128)(2,1)S(1)} %get-tuple-element.18), channel_id=1, replica_groups=mesh['mp'=4,'seq'=16,'dp'=4] {'seq'}, dimensions={0} | all-to-all | bytes 262144 | tf_op jit(solution)/shard_map/all_to_all | solution.py:391
  51.0 18.2 %all_to_all.22.all_ref = bf16[16,24,128]{2,1,0:T(8,128)(2,1)S(1)} all-to-all(bf16[16,24,128]{2,1,0:T(8,128)(2,1)S(1)} %get-tuple-element.19), channel_id=1, replica_groups=mesh['mp'=4,'seq'=16,'dp'=4] {'mp','dp'}, dimensions={0} | all-to-all | bytes 196608 | tf_op jit(solution)/shard_map/all_to_all | solution.py:400
  69.1 0.8 %result.1 = (f32[64,128]{1,0:T(8,128)}, f32[64,192]{1,0:T(8,128)}) custom-call(bf16[16,24,128]{2,1,0:T(8,128)(2,1)S(1)} %all_to_all.22.all_ref, f32[64,128]{1,0:T(8,128)S(1)} %get-tuple-element.20.gap_ref, f32[8,128]{1,0:T(8,128)S(1)} %get-tuple-element.21.inverse_ref), custom_call_target="tpu_custom_call" | custom-call | flops 49152 | bytes 98304 | tf_op jit(solution)/shard_map/result/pallas_call | solution.py:401
  (2 shorter events, 0.1 us)
Async XLA Ops:
  4.1 12.6 %all-to-all-start = ((bf16[16,64,128]{2,1,0:T(8,128)(2,1)}), bf16[16,64,128]{2,1,0:T(8,128)(2,1)S(1)}, u32[]{:S(2)}, u32[]{:S(2)}) async-start(bf16[16,64,128]{2,1,0:T(8,128)(2,1)} %latents.1), calls=%async_computation | async-start | bytes 524288 | tf_op jit(solution)/shard_map/all_to_all | solution.py:326
  9.9 26.7 %copy-start = (bf16[1,128,3072]{2,1,0:T(8,128)(2,1)S(1)}, bf16[1,128,3072]{2,1,0:T(8,128)(2,1)}, u32[]{:S(2)}) copy-start(bf16[1,128,3072]{2,1,0:T(8,128)(2,1)} %param.10) | copy-start | bytes 2359300
  9.9 26.7 %copy-start.1 = (bf16[3072,64]{0,1:T(8,128)(2,1)S(1)}, bf16[3072,64]{0,1:T(8,128)(2,1)}, u32[]{:S(2)}) copy-start(bf16[3072,64]{0,1:T(8,128)(2,1)} %param.12) | copy-start | bytes 1179652
  9.9 26.7 %copy-start.2 = (bf16[1,128,64]{1,2,0:T(8,128)(2,1)S(1)}, bf16[1,128,64]{1,2,0:T(8,128)(2,1)}, u32[]{:S(2)}) copy-start(bf16[1,128,64]{1,2,0:T(8,128)(2,1)} %param.13) | copy-start | bytes 49156
  9.9 26.6 %copy-start.3 = (bf16[3072]{0:T(1024)(128)(2,1)S(1)}, bf16[3072]{0:T(1024)(128)(2,1)}, u32[]{:S(2)}) copy-start(bf16[3072]{0:T(1024)(128)(2,1)} %gain_hbm.5) | copy-start | bytes 18436
  16.7 0.7 %copy-start.4 = (bf16[16,64,128]{2,1,0:T(8,128)(2,1)}, bf16[16,64,128]{2,1,0:T(8,128)(2,1)S(1)}, u32[]{:S(2)}) copy-start(bf16[16,64,128]{2,1,0:T(8,128)(2,1)S(1)} %all-to-all-done.latent_hbm) | copy-start | bytes 786436
  31.8 5.7 %collective-permute-start = (f32[32,128]{1,0:T(8,128)S(1)}, f32[32,128]{1,0:T(8,128)S(1)}, u32[]{:S(2)}, u32[]{:S(2)}) collective-permute-start(f32[32,128]{1,0:T(8,128)S(1)} %sum.1.zero_ref), channel_id=1, source_target_pairs={{0,64},{64,0},{128,192},{192,128},{1,65},{65,1},{129,193},{193,129... | collective-permute-start | bytes 49160 | tf_op jit(solution)/shard_map/ppermute | solution.py:372
  33.4 5.2 %collective-permute-start.1 = (f32[32,128]{1,0:T(8,128)S(1)}, f32[32,128]{1,0:T(8,128)S(1)}, u32[]{:S(2)}, u32[]{:S(2)}) collective-permute-start(f32[32,128]{1,0:T(8,128)S(1)} %sum.1.zero_ref), channel_id=1, source_target_pairs={{0,128},{64,192},{128,0},{192,64},{1,129},{65,193},{129,1},{193,65... | collective-permute-start | bytes 49160 | tf_op jit(solution)/shard_map/ppermute | solution.py:372
  36.3 4.9 %collective-permute-start.2 = (f32[32,128]{1,0:T(8,128)S(1)}, f32[32,128]{1,0:T(8,128)S(1)}, u32[]{:S(2)}, u32[]{:S(2)}) collective-permute-start(f32[32,128]{1,0:T(8,128)S(1)} %sum.1.zero_ref), channel_id=1, source_target_pairs={{0,192},{64,128},{128,64},{192,0},{1,193},{65,129},{129,65},{193,1... | collective-permute-start | bytes 49160 | tf_op jit(solution)/shard_map/ppermute | solution.py:372

commit v4 on v3

--- a/solution.py
+++ b/solution.py
@@ -29,6 +29,16 @@
     return high, low
 
 
+def place():
+    slot = lax.axis_index("mp")
+    half = slot // 2
+    return slot, (slot + half) % 2, half
+
+
+def slot_of(model, half):
+    return 2 * half + (model + half) % 2
+
+
 def level_of(steps_ref):
     return (steps_ref[0].astype(F32) + 1.0) * (1.0 / (STEPS + 1.0))
 
@@ -47,42 +57,52 @@
 
 
 def latents_kernel(steps_ref, features_hbm, gain_hbm, weight_hbm, noise_hbm, send_ref, features, gain, weight, noise, sems):
-    half = lax.axis_index("mp") // 2
+    _, _, half = place()
     tokens, width = features.shape
     part = tokens // 2
     copies = [
-        pltpu.make_async_copy(gain_hbm, gain, sems.at[4]),
-        pltpu.make_async_copy(weight_hbm, weight, sems.at[5]),
-        pltpu.make_async_copy(noise_hbm, noise, sems.at[6]),
+        pltpu.make_async_copy(gain_hbm, gain, sems.at[0]),
+        pltpu.make_async_copy(noise_hbm, noise, sems.at[2]),
     ]
-    halves = []
-    for i in range(2):
-        start = pl.multiple_of(((half + i) % 2) * part, part)
-        rows = features.at[pl.ds(i * part, part), :]
-        halves.append(pltpu.make_async_copy(features_hbm.at[pl.ds(start, part), :], rows, sems.at[i]))
-    for copy in copies[:1] + halves + copies[1:]:
+    parts = 2
+    chunk = width // parts
+    pieces = []
+    for k in range(parts):
+        span = pl.ds(k * chunk, chunk)
+        group = [pltpu.make_async_copy(weight_hbm.at[:, span], weight.at[:, span], sems.at[3 + 3 * k])]
+        for i in range(2):
+            start = pl.multiple_of(((half + i) % 2) * part, part)
+            here = features.at[pl.ds(i * part, part), span]
+            group.append(pltpu.make_async_copy(features_hbm.at[pl.ds(start, part), span], here, sems.at[4 + 3 * k + i]))
+        pieces.append(group)
+    for copy in copies[:1] + sum(pieces, []) + copies[1:]:
         copy.start()
     level = level_of(steps_ref)
     copies[0].wait()
     gain_row = gain[...].astype(F32).reshape(1, width)
-    scaled, inverse = [], []
-    for i in range(2):
-        halves[i].wait()
-        one, inv_rms = scaled_and_rms(features[i * part : (i + 1) * part, :], gain_row)
-        scaled.append(one)
-        inverse.append(inv_rms)
-    inv_row = jnp.broadcast_to(jnp.concatenate(inverse, axis=0), (tokens, tokens)).T[0:1]
+    clean = jnp.zeros((64, tokens), F32)
+    squares = jnp.zeros((tokens, 128), F32)
+    for k in range(parts):
+        for copy in pieces[k]:
+            copy.wait()
+        span = slice(k * chunk, (k + 1) * chunk)
+        values = features[:, span].astype(F32)
+        for j in range(chunk // 128):
+            one = values[:, j * 128 : (j + 1) * 128]
+            squares += one * one
+        clean += dot(weight[:, span], (values * gain_row[:, span]).astype(BF16), NT)
+    mean_square = jnp.sum(squares, axis=1, keepdims=True) / width
+    inv_row = lax.rsqrt(jnp.broadcast_to(mean_square, (tokens, tokens)).T[0:1] + 1e-06)
+    clean = clean * inv_row
     copies[1].wait()
-    clean = dot(weight[...], jnp.concatenate(scaled, axis=0), NT) * inv_row
-    copies[2].wait()
     noise_here = pltpu.roll(noise[...].astype(F32), (tokens - half * part) % tokens, 1)
     rounded = ((1.0 - level) * clean + level * noise_here).astype(BF16)
     for target in range(send_ref.shape[0]):
         send_ref[target] = rounded
 
 
-def own_kernel(steps_ref, features_hbm, gain_hbm, weight_hbm, noise_hbm, picked_ref, own_ref, inv_ref, features, gain, weight, noise, turned, sems):
-    slot = lax.axis_index("mp")
+def own_kernel(steps_ref, features_hbm, gain_hbm, weight_hbm, noise_hbm, picked_ref, own_ref, features, gain, weight, noise, turned, sems):
+    _, model, half = place()
     width = features.shape[1]
     pairs = ((gain_hbm, gain), (features_hbm, features), (weight_hbm, weight), (noise_hbm, noise))
     copies = [pltpu.make_async_copy(source, target, sems.at[i]) for i, (source, target) in enumerate(pairs)]
@@ -93,18 +113,23 @@
     level = level_of(steps_ref)
     scaled, inv_rms = scaled_and_rms(features[...], gain[...].astype(F32).reshape(1, width))
     inv_row = jnp.broadcast_to(inv_rms, (128, 128)).T[0:1]
-    inv_ref[...] = jnp.broadcast_to(inv_row, inv_ref.shape)
     clean = dot(weight[...], scaled, NT) * inv_row
-    own_ref[0:64, :] = clean
-    own_ref[64:128, :] = (1.0 - level) * clean + level * noise[...].astype(F32)
+    noisy = (1.0 - level) * clean + level * noise[...].astype(F32)
+    first = half == 0
+    own_ref[0:32, :] = jnp.where(first, packed(clean, 0), packed(clean, 1))
+    own_ref[32:64, :] = jnp.where(first, packed(noisy, 0), packed(noisy, 1))
+    inverse = jnp.broadcast_to(inv_row, (8, 128))
+    left = lax.broadcasted_iota(jnp.int32, (8, 128), 1) < 64
+    turned_row = pltpu.roll(inverse, 64, 1)
+    own_ref[64:72, :] = jnp.where(left, jnp.where(first, inverse, turned_row), jnp.where(first, turned_row, inverse))
     turned[...] = scaled.T
     for s in range(16):
-        start = pl.multiple_of(s * 192 + slot * 48, 16)
-        picked_ref[s * 48 : (s + 1) * 48, :] = turned[pl.ds(start, 48), :]
+        start = pl.multiple_of(s * 192 + model * 96, 32)
+        picked_ref[s * 96 : (s + 1) * 96, :] = turned[pl.ds(start, 96), :]
 
 
 def fold_kernel(steps_ref, embed_hbm, gain_hbm, qkv_hbm, qk_hbm, out_hbm, fold_ref, scale_ref, embed, gain, qkv, qk, out, sems):
-    model = lax.axis_index("mp") % 2
+    _, model, _ = place()
     head = lax.axis_index("seq")
     width = embed.shape[1]
     parts = 3
@@ -215,62 +240,69 @@
         total += dot(value[:, span], shares)
     mixed = total[0:64] / total[64:65]
     for s in range(blocks):
-        send_ref[s] = packed(mixed[:, (s // 2) * 128 : (s // 2 + 1) * 128], s % 2).astype(BF16)
-
-
-def sum_kernel(part_ref, send_ref):
-    send_ref[...] = jnp.sum(part_ref[...].astype(F32), axis=0)
-
-
-def gap_kernel(steps_ref, zero_ref, one_ref, two_ref, three_ref, picked_ref, own_ref, inv_ref, send_ref, gap_ref, every):
+        block = packed(mixed[:, (s // 2) * 128 : (s // 2 + 1) * 128], s % 2).astype(BF16)
+        send_ref[s] = block
+        send_ref[blocks + s] = block
+
+
+def gap_kernel(steps_ref, velocity_ref, picked_ref, own_ref, send_ref, gap_ref):
     level = level_of(steps_ref)
-    blocks = send_ref.shape[0]
-    slot = lax.axis_index("mp")
-    for k, ref in enumerate((zero_ref, one_ref, two_ref, three_ref)):
-        every[slot ^ k] = ref[...]
+    _, _, half = place()
+    teacher = jnp.sum(velocity_ref[0:16].astype(F32), axis=0)
+    gap = level * (teacher - jnp.sum(velocity_ref[16:32].astype(F32), axis=0))
+    gap_ref[...] = gap
+    distance = jnp.abs(own_ref[0:32] - (own_ref[32:64] - level * teacher))
+    spread = jnp.sum(jnp.sum(distance, axis=1, keepdims=True), axis=0, keepdims=True)
+    direction = gap * own_ref[64:65]
+    turned = pltpu.roll(direction, 64, 1)
     left = lax.broadcasted_iota(jnp.int32, (64, 128), 1) < 64
-
-    def velocity(model):
-        first, second = every[model], every[model + 2]
-        first = jnp.concatenate([first, pltpu.roll(first, 64, 1)], axis=0)
-        second = jnp.concatenate([pltpu.roll(second, 64, 1), second], axis=0)
-        return jnp.where(left, first, second)
-
-    teacher = velocity(0)
-    gap = level * (teacher - velocity(1))
-    gap_ref[...] = gap
-    distance = jnp.abs(own_ref[0:64] - (own_ref[64:128] - level * teacher))
-    spread = jnp.sum(jnp.sum(distance, axis=1, keepdims=True), axis=0, keepdims=True)
-    direction = (gap * inv_ref[0:1]).astype(BF16)
-    grad = dot(picked_ref[...], jnp.concatenate([direction, direction], axis=0), NT)
+    rows = jnp.where(
+        half == 0,
+        jnp.where(left, jnp.concatenate([direction, turned], axis=0), 0.0),
+        jnp.where(left, 0.0, jnp.concatenate([turned, direction], axis=0)),
+    ).astype(BF16)
+    grad = dot(picked_ref[...], jnp.concatenate([rows, rows], axis=0), NT)
+    tail = spread_rows(spread)
+    left = left[0:48]
+    for s in range(send_ref.shape[0]):
+        pair = jnp.where(left, grad[s * 96 : s * 96 + 48], grad[s * 96 + 48 : s * 96 + 96])
+        send_ref[s] = jnp.concatenate([pair, tail], axis=0).astype(BF16)
+
+
+def spread_rows(spread):
     spread = jnp.broadcast_to(spread, (8, 128))
     spot = lax.broadcasted_iota(jnp.int32, (8, 128), 0)
     high = spread.astype(BF16).astype(F32)
-    tail = jnp.where(spot == 0, high, jnp.where(spot == 1, spread - high, 0.0))
-    left = lax.broadcasted_iota(jnp.int32, (24, 128), 1) < 64
-    for s in range(blocks):
-        packed = jnp.where(left, grad[s * 48 : s * 48 + 24], grad[s * 48 + 24 : s * 48 + 48])
-        send_ref[s] = jnp.concatenate([packed, tail], axis=0).astype(BF16)
-
-
-def weight_inverse(total):
-    return 1.0 / ((total[24:25] + total[25:26]) / 131072.0 + 1e-05)
-
-
-def total_kernel(grad_ref, send_ref, inverse_ref):
+    return jnp.where(spot == 0, high, jnp.where(spot == 1, spread - high, 0.0))
+
+
+def total_kernel(grad_ref, send_ref):
     total = jnp.sum(grad_ref[...].astype(F32), axis=0)
-    inverse = weight_inverse(total)
-    inverse_ref[...] = jnp.broadcast_to(inverse, inverse_ref.shape)
-    whole = (total[0:24] * inverse).astype(BF16)
+    tail = spread_rows(total[48:49] + total[49:50])
+    whole = jnp.concatenate([total[0:48], tail], axis=0).astype(BF16)
     for target in range(send_ref.shape[0]):
         send_ref[target] = whole
 
 
-def result_kernel(all_ref, gap_ref, inverse_ref, dmd_ref, grad_ref):
-    dmd_ref[...] = gap_ref[...] * inverse_ref[0:1]
+def result_kernel(all_ref, gap_ref, other_ref, dmd_ref, grad_ref):
+    _, _, half = place()
+    sample = lax.axis_index("dp")
+    totals = [jnp.zeros((48, 128), F32)] * 2
+    mine = jnp.zeros((1, 128), F32)
+    for d in range(4):
+        sums = [sum(all_ref[4 * slot_of(m, h) + d].astype(F32) for h in range(2)) for m in range(2)]
+        inverse = 1.0 / ((sums[0][48:49] + sums[0][49:50]) / 131072.0 + 1e-05)
+        mine = jnp.where(sample == d, inverse, mine)
+        totals = [total + one[0:48] * inverse for total, one in zip(totals, sums)]
+    own = gap_ref[...] * mine
+    other = other_ref[...] * mine
+    first = jnp.where(half == 0, own, other)
+    second = jnp.where(half == 0, other, own)
+    left = lax.broadcasted_iota(jnp.int32, (32, 128), 1) < 64
+    dmd_ref[0:32, :] = jnp.where(left, first, pltpu.roll(second, 64, 1))
+    dmd_ref[32:64, :] = jnp.where(left, pltpu.roll(first, 64, 1), second)
     rows = []
-    for m in range(4):
-        total = jnp.sum(all_ref[4 * m : 4 * m + 4].astype(F32), axis=0)
+    for total in totals:
         rows += [total, pltpu.roll(total, 64, 1)]
     rows.append(jnp.zeros((64, 128), F32))
     grad_ref[...] = jnp.concatenate(rows, axis=0).T[0:64, 0:192]
@@ -287,6 +319,10 @@
         name=name,
         **more,
     )
+
+
+def pairs_of(seq_count):
+    return [[slot_of(m, half) * seq_count + s for m in range(2) for s in range(seq_count)] for half in range(2)]
 
 
 def per_device(
@@ -318,10 +354,10 @@
         shape((seq_count, 64, tokens), BF16),
         [SMEM] + [HBM] * 4,
         "latents",
-        grant=60,
+        grant=63,
         flops=2 * tokens * width * 64,
         moved=2 * tokens * width,
-        scratch_shapes=buffers + [pltpu.SemaphoreType.DMA((7,))],
+        scratch_shapes=buffers + [pltpu.SemaphoreType.DMA((9,))],
     )(*local)
     every_latent = lax.all_to_all(send, "seq", 0, 0)
 
@@ -330,7 +366,7 @@
         (shape((384, 256), BF16), shape((136, 128), F32)),
         [SMEM] + [HBM] * 5,
         "fold",
-        grant=60,
+        grant=63,
         flops=2 * width * 384 * 256,
         moved=2 * width * 384,
         scratch_shapes=[
@@ -352,10 +388,10 @@
     keys = seq_count * tokens
     send = call(
         attention_kernel,
-        shape((seq_count, 32, 128), BF16),
+        shape((2 * seq_count, 32, 128), BF16),
         [HBM] * 3,
         "attention",
-        grant=60,
+        grant=63,
         flops=2 * keys * (keys // 2) * 256,
         moved=2 * keys * 64,
         scratch_shapes=[
@@ -367,12 +403,11 @@
             pltpu.SemaphoreType.DMA((3,)),
         ],
     )(every_latent, fold, scale)
-    every_part = lax.all_to_all(send, "seq", 0, 0)
-    send = call(sum_kernel, shape((32, 128), F32), [VMEM], "sum", moved=2 * seq_count * 32 * 128)(every_part)
-    velocities = [send] + [lax.ppermute(send, "mp", [(i, i ^ k) for i in range(4)]) for k in range(1, 4)]
-    picked, own, inv = call(
+    whole = ("mp", "seq")
+    velocities = lax.all_to_all(send, whole, 0, 0, axis_index_groups=pairs_of(seq_count))
+    picked, own = call(
         own_kernel,
-        (shape((width // 4, tokens), BF16), shape((128, tokens), F32), shape((8, tokens), F32)),
+        (shape((width // 2, tokens), BF16), shape((72, tokens), F32)),
         [SMEM] + [HBM] * 4,
         "own",
         flops=2 * tokens * width * 64,
@@ -381,21 +416,21 @@
     )(*local)
     send, gap = call(
         gap_kernel,
-        (shape((seq_count, 32, 128), BF16), shape((64, tokens), F32)),
-        [SMEM] + [VMEM] * 7,
+        (shape((seq_count, 56, 128), BF16), shape((32, 128), F32)),
+        [SMEM] + [VMEM] * 3,
         "gap",
         flops=2 * tokens * width * 16,
         moved=2 * 64 * 32 * 128,
-        scratch_shapes=[pltpu.VMEM((4, 32, 128), F32)],
-    )(time_steps, *velocities, picked, own, inv)
+    )(time_steps, velocities, picked, own)
+    other = lax.ppermute(gap, "mp", [(slot_of(m, h), slot_of(m, 1 - h)) for m in range(2) for h in range(2)])
     partials = lax.all_to_all(send, "seq", 0, 0)
-    send, inverse = call(
+    send = call(
         total_kernel,
-        (shape((group, 24, 128), BF16), shape((8, 128), F32)),
+        shape((group, 56, 128), BF16),
         [VMEM],
         "total",
-        flops=seq_count * 32 * 128,
-        moved=2 * seq_count * 32 * 128,
+        flops=seq_count * 56 * 128,
+        moved=2 * seq_count * 56 * 128,
     )(partials)
     every_total = lax.all_to_all(send, ("mp", "dp"), 0, 0)
     dmd, grad = call(
@@ -405,7 +440,7 @@
         "result",
         flops=group * 24 * 128,
         moved=2 * group * 24 * 128,
-    )(every_total, gap, inverse)
+    )(every_total, gap, other)
     return dmd.T[None], grad.T
 
 

time: 71.2 us -> 69.4 us (0.975); the launches traced: 69.9 us -> 68.9 us
  blocking collectives: 37.4 us -> 10.1 us
  starting transfers between devices: 10.6 us -> 24 us
  waiting for transfers between devices: 7.16 us -> 19.1 us
    all_to_all x2 -> x0, blocking collectives: 28.1 us -> none  [the longest x1 18.2 us: per_device(): every_total = lax.all_to_all(send, ('mp', 'dp'), 0, 0)]
    all_to_all x0 -> x2, starting transfers between devices: none -> 15.1 us  [the longest x1 10.1 us: per_device(): every_total = lax.all_to_all(send, ('mp', 'dp'), 0, 0)]
    all_to_all x0 -> x2, waiting for transfers between devices: none -> 13.5 us  [the longest x1 7.69 us: per_device(): every_total = lax.all_to_all(send, ('mp', 'dp'), 0, 0)]
    ppermute x3 -> x1, waiting for transfers between devices: 3.77 us -> 2.07 us  [per_device(): lax.ppermute(gap, 'mp', [(slot_of(m, h), slot_of(m, 1 - h)) for m in rang...]
    ppermute x3 -> x1, starting transfers between devices: 4.78 us -> 3.14 us  [per_device(): lax.ppermute(gap, 'mp', [(slot_of(m, h), slot_of(m, 1 - h)) for m in rang...]
    pallas_call x5 -> x4, Pallas kernels: 5.7 us -> 6.61 us  [the longest x1 4.48 us: per_device(): call(attention_kernel, shape((2 * seq_count, 32, 128), BF16), [HBM] * 3,...]
    all_to_all x1, blocking collectives: 9.31 us -> 10.1 us  [per_device(): partials = lax.all_to_all(send, 'seq', 0, 0)]
  transfers between devices with their start and end apart: 4 -> 4, of which waited for: 3 -> 4; matrix products, arithmetic and copies ran while one was open for 0% -> 0% of each run, Pallas kernels for 6% -> 6%
where the time goes in v4:
time: 69.4 us; the launch traced here: 68.9 us
  starting transfers between devices  24 us (35%)
  waiting for transfers between devices  19.1 us (28%)
  Pallas kernels  13.3 us (19%)
  blocking collectives  10.1 us (15%)
  between operations  1.39 us (2%)
  local copies, waits for them, and re-layouts  1.01 us (1%)
    all_to_all x1, starting transfers between devices, per_device(): every_total = lax.all_to_all(send, ('mp', 'dp'), 0, 0)  10.1 us
    all_to_all x1, blocking collectives, per_device(): partials = lax.all_to_all(send, 'seq', 0, 0)  10.1 us
    all_to_all x1, waiting for transfers between devices, per_device(): every_total = lax.all_to_all(send, ('mp', 'dp'), 0, 0)  7.69 us
    all_to_all x1, starting transfers between devices, per_device(): every_latent = lax.all_to_all(send, 'seq', 0, 0)  5.79 us
    all_to_all x1, waiting for transfers between devices, per_device(): lax.all_to_all(send, whole, 0, 0, axis_index_groups=pairs_of(seq_count))  5.77 us
    all_to_all x1, starting transfers between devices, per_device(): lax.all_to_all(send, whole, 0, 0, axis_index_groups=pairs_of(seq_count))  4.94 us
    pallas_call x1, Pallas kernels, per_device(): call(attention_kernel, shape((2 * seq_count, 32, 128), BF16), [HBM] * 3,...  4.48 us
    all_to_all x1, waiting for transfers between devices, per_device(): every_latent = lax.all_to_all(send, 'seq', 0, 0)  3.59 us
  transfers between devices with their start and end apart: 4, of which 4 were waited for; matrix products, arithmetic and copies ran while one was open for 0% of the time, Pallas kernels for 6%

profile of v4, /device:TPU:32, one launch (start us, length us, event | category | flops | bytes accessed | tf_op | source)
XLA Modules:
  0.0 68.9 jit_solution(5707475618139370429)
XLA Ops:
  1.3 2.6 %latents.1 = bf16[16,64,128]{2,1,0:T(8,128)(2,1)} custom-call(s32[1]{0:T(128)S(6)} %copy.12.steps_ref, bf16[128,3072]{1,0:T(8,128)(2,1)} %bitcast.11, bf16[3072]{0:T(1024)(128)(2,1)} %gain_hbm.5, bf16[64,3072]{1,0:T(8,128)(2,1)} %bitcast.13, bf16[64,128]{1,0:T(8,128)(2,1)} %bitcast.15), custom_call_target="tpu_custom_call" | custom-call | flops 50331648 | bytes 786432 | tf_op jit(solution)/shard_map/latents/pallas_call | solution.py:352
  3.9 5.8 %all-to-all-start = ((bf16[16,64,128]{2,1,0:T(8,128)(2,1)}), bf16[16,64,128]{2,1,0:T(8,128)(2,1)}, u32[]{:S(2)}, u32[]{:S(2)}) async-start(bf16[16,64,128]{2,1,0:T(8,128)(2,1)} %latents.1), calls=%async_computation | async-start | bytes 524288 | tf_op jit(solution)/shard_map/all_to_all | solution.py:362
  9.7 0.0 copy-start
  9.7 0.0 copy-start.2
  9.7 0.0 copy-start.3
  9.7 3.3 %fold.1 = (bf16[384,256]{1,0:T(8,128)(2,1)}, f32[136,128]{1,0:T(8,128)}) custom-call(s32[1]{0:T(128)S(6)} %copy.12.steps_ref, bf16[2,64,3072]{2,1,0:T(8,128)(2,1)} %embed_hbm.1, bf16[2,3072]{1,0:T(2,128)(2,1)} %gain_hbm.4, bf16[2,3,3072,128]{3,2,1,0:T(8,128)(2,1)} %bitcast.17, bf16[2,2,128]{2,1,0:T(2,128)(2,1)} %qk_hbm.1, bf16[2,64,2048]{2,1,0:T(8,128)(2,1)} %bitcast.18), custom_call_target="tpu_custom_call" | custom-call | flops 603979776 | bytes 2359296 | tf_op jit(solution)/shard_map/fold/pallas_call | solution.py:364
  13.0 3.6 %all-to-all-done.latent_hbm = bf16[16,64,128]{2,1,0:T(8,128)(2,1)} async-done(((bf16[16,64,128]{2,1,0:T(8,128)(2,1)}), bf16[16,64,128]{2,1,0:T(8,128)(2,1)}, u32[]{:S(2)}, u32[]{:S(2)}) %all-to-all-start) | async-done | bytes 262176 | tf_op jit(solution)/shard_map/all_to_all | solution.py:362
  16.6 4.5 %attention.1 = bf16[32,32,128]{2,1,0:T(8,128)(2,1)} custom-call(bf16[16,64,128]{2,1,0:T(8,128)(2,1)} %all-to-all-done.latent_hbm, bf16[384,256]{1,0:T(8,128)(2,1)} %get-tuple-element.10.fold_hbm, f32[136,128]{1,0:T(8,128)} %get-tuple-element.11.scale_hbm), custom_call_target="tpu_custom_call" | custom-call | flops 1073741824 | bytes 262144 | tf_op jit(solution)/shard_map/attention/pallas_call | solution.py:389
  21.1 4.9 %all-to-all-start.1 = ((bf16[32,32,128]{2,1,0:T(8,128)(2,1)}), bf16[32,32,128]{2,1,0:T(8,128)(2,1)S(1)}, u32[]{:S(2)}, u32[]{:S(2)}) async-start(bf16[32,32,128]{2,1,0:T(8,128)(2,1)} %attention.1), calls=%async_computation.1 | async-start | bytes 524288 | tf_op jit(solution)/shard_map/all_to_all | solution.py:407
  26.1 0.0 copy-done
  26.1 0.0 copy-done.2
  26.1 0.0 copy-done.3
  26.1 0.0 copy-start.1
  26.1 1.0 %copy-done.1 = bf16[3072,64]{0,1:T(8,128)(2,1)S(1)} copy-done((bf16[3072,64]{0,1:T(8,128)(2,1)S(1)}, bf16[3072,64]{0,1:T(8,128)(2,1)}, u32[]{:S(2)}) %copy-start.1) | copy-done | bytes 393240
  27.1 1.0 %own.1 = (bf16[1536,128]{1,0:T(8,128)(2,1)S(1)}, f32[72,128]{1,0:T(8,128)S(1)}) custom-call(s32[1]{0:T(128)S(6)} %copy.12.steps_ref, bf16[128,3072]{1,0:T(8,128)(2,1)S(1)} %bitcast.12, bf16[3072]{0:T(1024)(128)(2,1)S(1)} %copy-done.3, bf16[64,3072]{1,0:T(8,128)(2,1)S(1)} %bitcast.14, bf16[64,128]{1,0:T(8,128)(2,1)S(1)} %bitcast.16), custom_call_target="tpu_custom_call" | custom-call | flops 50331648 | bytes 786432 | tf_op jit(solution)/shard_map/own/pallas_call | solution.py:408
  28.1 5.8 %all-to-all-done.1.velocity_ref = bf16[32,32,128]{2,1,0:T(8,128)(2,1)S(1)} async-done(((bf16[32,32,128]{2,1,0:T(8,128)(2,1)}), bf16[32,32,128]{2,1,0:T(8,128)(2,1)S(1)}, u32[]{:S(2)}, u32[]{:S(2)}) %all-to-all-start.1) | async-done | bytes 262176 | tf_op jit(solution)/shard_map/all_to_all | solution.py:407
  33.9 0.4 gap.1
  34.3 10.1 %all_to_all.20.grad_ref = bf16[16,56,128]{2,1,0:T(8,128)(2,1)S(1)} all-to-all(bf16[16,56,128]{2,1,0:T(8,128)(2,1)S(1)} %get-tuple-element.14), channel_id=1, replica_groups=mesh['mp'=4,'seq'=16,'dp'=4] {'seq'}, dimensions={0} | all-to-all | bytes 458752 | tf_op jit(solution)/shard_map/all_to_all | solution.py:426
  44.3 0.7 %total.1 = bf16[16,56,128]{2,1,0:T(8,128)(2,1)} custom-call(bf16[16,56,128]{2,1,0:T(8,128)(2,1)S(1)} %all_to_all.20.grad_ref), custom_call_target="tpu_custom_call" | custom-call | flops 114688 | bytes 229376 | tf_op jit(solution)/shard_map/total/pallas_call | solution.py:427
  45.1 10.1 %all-to-all-start.3 = ((bf16[16,56,128]{2,1,0:T(8,128)(2,1)}), bf16[16,56,128]{2,1,0:T(8,128)(2,1)S(1)}, u32[]{:S(2)}, u32[]{:S(2)}) async-start(bf16[16,56,128]{2,1,0:T(8,128)(2,1)} %total.1), calls=%async_computation.3 | async-start | bytes 458752 | tf_op jit(solution)/shard_map/all_to_all | solution.py:435
  55.2 3.1 %collective-permute-start = (f32[32,128]{1,0:T(8,128)S(1)}, f32[32,128]{1,0:T(8,128)S(1)}, u32[]{:S(2)}, u32[]{:S(2)}) collective-permute-start(f32[32,128]{1,0:T(8,128)S(1)} %get-tuple-element.15.gap_ref), channel_id=1, source_target_pairs={{0,192},{192,0},{64,128},{128,64},{1,193},{193,1},{65,129},{129,65... | collective-permute-start | bytes 49160 | tf_op jit(solution)/shard_map/ppermute | solution.py:425
  58.4 2.1 %collective-permute-done.other_ref = f32[32,128]{1,0:T(8,128)S(1)} collective-permute-done((f32[32,128]{1,0:T(8,128)S(1)}, f32[32,128]{1,0:T(8,128)S(1)}, u32[]{:S(2)}, u32[]{:S(2)}) %collective-permute-start) | collective-permute-done | bytes 16416 | tf_op jit(solution)/shard_map/ppermute | solution.py:425
  60.4 7.7 %all-to-all-done.3.all_ref = bf16[16,56,128]{2,1,0:T(8,128)(2,1)S(1)} async-done(((bf16[16,56,128]{2,1,0:T(8,128)(2,1)}), bf16[16,56,128]{2,1,0:T(8,128)(2,1)S(1)}, u32[]{:S(2)}, u32[]{:S(2)}) %all-to-all-start.3) | async-done | bytes 229408 | tf_op jit(solution)/shard_map/all_to_all | solution.py:435
  68.1 0.8 %result.1 = (f32[64,128]{1,0:T(8,128)}, f32[64,192]{1,0:T(8,128)}) custom-call(bf16[16,56,128]{2,1,0:T(8,128)(2,1)S(1)} %all-to-all-done.3.all_ref, f32[32,128]{1,0:T(8,128)S(1)} %get-tuple-element.15.gap_ref, f32[32,128]{1,0:T(8,128)S(1)} %collective-permute-done.other_ref), custom_call_target="tpu_custom_call" | custom-call | flops 49152 | bytes 98304 | tf_op jit(solution)/shard_map/result/pallas_call | solution.py:436
Async XLA Ops:
  3.9 12.7 %all-to-all-start = ((bf16[16,64,128]{2,1,0:T(8,128)(2,1)}), bf16[16,64,128]{2,1,0:T(8,128)(2,1)}, u32[]{:S(2)}, u32[]{:S(2)}) async-start(bf16[16,64,128]{2,1,0:T(8,128)(2,1)} %latents.1), calls=%async_computation | async-start | bytes 524288 | tf_op jit(solution)/shard_map/all_to_all | solution.py:362
  9.7 16.4 %copy-start = (bf16[1,128,3072]{2,1,0:T(8,128)(2,1)S(1)}, bf16[1,128,3072]{2,1,0:T(8,128)(2,1)}, u32[]{:S(2)}) copy-start(bf16[1,128,3072]{2,1,0:T(8,128)(2,1)} %param.10) | copy-start | bytes 2359300
  9.7 16.4 %copy-start.2 = (bf16[1,128,64]{1,2,0:T(8,128)(2,1)S(1)}, bf16[1,128,64]{1,2,0:T(8,128)(2,1)}, u32[]{:S(2)}) copy-start(bf16[1,128,64]{1,2,0:T(8,128)(2,1)} %param.13) | copy-start | bytes 49156
  9.7 16.4 %copy-start.3 = (bf16[3072]{0:T(1024)(128)(2,1)S(1)}, bf16[3072]{0:T(1024)(128)(2,1)}, u32[]{:S(2)}) copy-start(bf16[3072]{0:T(1024)(128)(2,1)} %gain_hbm.5) | copy-start | bytes 18436
  21.1 12.8 %all-to-all-start.1 = ((bf16[32,32,128]{2,1,0:T(8,128)(2,1)}), bf16[32,32,128]{2,1,0:T(8,128)(2,1)S(1)}, u32[]{:S(2)}, u32[]{:S(2)}) async-start(bf16[32,32,128]{2,1,0:T(8,128)(2,1)} %attention.1), calls=%async_computation.1 | async-start | bytes 524288 | tf_op jit(solution)/shard_map/all_to_all | solution.py:407
  26.1 1.0 %copy-start.1 = (bf16[3072,64]{0,1:T(8,128)(2,1)S(1)}, bf16[3072,64]{0,1:T(8,128)(2,1)}, u32[]{:S(2)}) copy-start(bf16[3072,64]{0,1:T(8,128)(2,1)} %param.12) | copy-start | bytes 1179652
  45.1 23.1 %all-to-all-start.3 = ((bf16[16,56,128]{2,1,0:T(8,128)(2,1)}), bf16[16,56,128]{2,1,0:T(8,128)(2,1)S(1)}, u32[]{:S(2)}, u32[]{:S(2)}) async-start(bf16[16,56,128]{2,1,0:T(8,128)(2,1)} %total.1), calls=%async_computation.3 | async-start | bytes 458752 | tf_op jit(solution)/shard_map/all_to_all | solution.py:435
  55.2 5.2 %collective-permute-start = (f32[32,128]{1,0:T(8,128)S(1)}, f32[32,128]{1,0:T(8,128)S(1)}, u32[]{:S(2)}, u32[]{:S(2)}) collective-permute-start(f32[32,128]{1,0:T(8,128)S(1)} %get-tuple-element.15.gap_ref), channel_id=1, source_target_pairs={{0,192},{192,0},{64,128},{128,64},{1,193},{193,1},{65,129},{129,65... | collective-permute-start | bytes 49160 | tf_op jit(solution)/shard_map/ppermute | solution.py:425

commit v5 on v4

--- a/solution.py
+++ b/solution.py
@@ -192,18 +192,13 @@
     return jnp.where(left, block[0:32], pltpu.roll(block[32:64], 64, 1))
 
 
-def attention_kernel(latent_hbm, fold_hbm, scale_hbm, send_ref, latent_ref, fold_ref, scale_ref, latents, queries, sems):
-    pairs = ((latent_hbm, latent_ref), (fold_hbm, fold_ref), (scale_hbm, scale_ref))
-    copies = [pltpu.make_async_copy(source, target, sems.at[i]) for i, (source, target) in enumerate(pairs)]
-    for copy in copies:
-        copy.start()
+def attention_kernel(latent_ref, fold_ref, scale_ref, send_ref, latents, queries):
     blocks = latent_ref.shape[0]
     keys = blocks * 128
     count = blocks * 64
     for table in (latents, queries):
         table[64:128, :] = jnp.ones((64, table.shape[1]), BF16)
         table[192:256, :] = jnp.ones((64, table.shape[1]), BF16)
-    copies[0].wait()
     for s in range(blocks):
         block = latent_ref[s]
         latents[0:64, s * 128 : (s + 1) * 128] = block
@@ -212,8 +207,6 @@
         pieces = jnp.concatenate([latent_ref[2 * g + i][:, 0:64] for i in range(2)], axis=1)
         queries[0:64, g * 128 : (g + 1) * 128] = pieces
         queries[128:192, g * 128 : (g + 1) * 128] = pieces
-    for copy in copies[1:]:
-        copy.wait()
     squares = scale_ref[128:129, 0:1]
 
     def hidden_square(inner, rows):
@@ -308,6 +301,10 @@
     grad_ref[...] = jnp.concatenate(rows, axis=0).T[0:64, 0:192]
 
 
+def in_hbm(arrays):
+    return [pltpu.with_memory_space_constraint(one, pltpu.HBM) for one in arrays]
+
+
 def call(kernel, outs, in_specs, name, flops=0, moved=0, grant=32, **more):
     return pl.pallas_call(
         kernel,
@@ -342,7 +339,7 @@
     group = lax.axis_size("mp") * lax.axis_size("dp")
     features = gen_features[0]
     tokens, width = features.shape
-    local = (time_steps, features, gen_gain, gen_weight.T, flow_noise[0].T)
+    local = [time_steps] + in_hbm((features, gen_gain, gen_weight.T, flow_noise[0].T))
     buffers = [
         pltpu.VMEM((tokens, width), BF16),
         pltpu.VMEM((width,), BF16),
@@ -354,7 +351,6 @@
         shape((seq_count, 64, tokens), BF16),
         [SMEM] + [HBM] * 4,
         "latents",
-        grant=63,
         flops=2 * tokens * width * 64,
         moved=2 * tokens * width,
         scratch_shapes=buffers + [pltpu.SemaphoreType.DMA((9,))],
@@ -366,7 +362,6 @@
         (shape((384, 256), BF16), shape((136, 128), F32)),
         [SMEM] + [HBM] * 5,
         "fold",
-        grant=63,
         flops=2 * width * 384 * 256,
         moved=2 * width * 384,
         scratch_shapes=[
@@ -379,32 +374,8 @@
         ],
     )(
         time_steps,
-        embed_weight,
-        norm_gain,
-        qkv_weight.transpose(0, 2, 1, 3),
-        qk_gain,
-        out_weight.transpose(0, 2, 1),
+        *in_hbm((embed_weight, norm_gain, qkv_weight.transpose(0, 2, 1, 3), qk_gain, out_weight.transpose(0, 2, 1))),
     )
-    keys = seq_count * tokens
-    send = call(
-        attention_kernel,
-        shape((2 * seq_count, 32, 128), BF16),
-        [HBM] * 3,
-        "attention",
-        grant=63,
-        flops=2 * keys * (keys // 2) * 256,
-        moved=2 * keys * 64,
-        scratch_shapes=[
-            pltpu.VMEM((seq_count, 64, tokens), BF16),
-            pltpu.VMEM((384, 256), BF16),
-            pltpu.VMEM((136, 128), F32),
-            pltpu.VMEM((256, keys), BF16),
-            pltpu.VMEM((256, keys // 2), BF16),
-            pltpu.SemaphoreType.DMA((3,)),
-        ],
-    )(every_latent, fold, scale)
-    whole = ("mp", "seq")
-    velocities = lax.all_to_all(send, whole, 0, 0, axis_index_groups=pairs_of(seq_count))
     picked, own = call(
         own_kernel,
         (shape((width // 2, tokens), BF16), shape((72, tokens), F32)),
@@ -414,6 +385,22 @@
         moved=2 * tokens * width,
         scratch_shapes=buffers + [pltpu.VMEM((width, tokens), BF16), pltpu.SemaphoreType.DMA((4,))],
     )(*local)
+    fold, scale, picked, own = lax.optimization_barrier((fold, scale, picked, own))
+    keys = seq_count * tokens
+    send = call(
+        attention_kernel,
+        shape((2 * seq_count, 32, 128), BF16),
+        [VMEM] * 3,
+        "attention",
+        flops=2 * keys * (keys // 2) * 256,
+        moved=2 * keys * 64,
+        scratch_shapes=[
+            pltpu.VMEM((256, keys), BF16),
+            pltpu.VMEM((256, keys // 2), BF16),
+        ],
+    )(every_latent, fold, scale)
+    whole = ("mp", "seq")
+    velocities = lax.all_to_all(send, whole, 0, 0, axis_index_groups=pairs_of(seq_count))
     send, gap = call(
         gap_kernel,
         (shape((seq_count, 56, 128), BF16), shape((32, 128), F32)),

time: 69.4 us -> 66.6 us (0.960)
  blocking collectives: 10.1 us -> 22.3 us
  waiting for transfers between devices: 19.1 us -> 12 us
  starting transfers between devices: 24 us -> 18.7 us
  Pallas kernels: 13.3 us -> 11.7 us
  local copies, waits for them, and re-layouts: 1.01 us -> 0 us
    all_to_all x0 -> x1, blocking collectives: none -> 12.3 us  [per_device(): lax.all_to_all(send, whole, 0, 0, axis_index_groups=pairs_of(seq_count))]
    all_to_all x1 -> x0, waiting for transfers between devices: 5.77 us -> none  [per_device(): lax.all_to_all(send, whole, 0, 0, axis_index_groups=pairs_of(seq_count))]
    all_to_all x1 -> x0, starting transfers between devices: 4.94 us -> none  [per_device(): lax.all_to_all(send, whole, 0, 0, axis_index_groups=pairs_of(seq_count))]
    pallas_call x1, Pallas kernels: 4.48 us -> 2.66 us  [per_device(): call(attention_kernel, shape((2 * seq_count, 32, 128), BF16), [VMEM] * 3,...]
    all_to_all x1, waiting for transfers between devices: 3.59 us -> 2.21 us  [per_device(): every_latent = lax.all_to_all(send, 'seq', 0, 0)]
    unnamed x8 -> x0, local copies, waits for them, and re-layouts: 1.01 us -> none
    pallas_call x1, Pallas kernels: 1.04 us -> 2.02 us  [per_device(): call(own_kernel, (shape((width // 2, tokens), BF16), shape((72, tokens),...]
    pallas_call x1, Pallas kernels: 3.3 us -> 2.54 us  [per_device(): call(fold_kernel, (shape((384, 256), BF16), shape((136, 128), F32)), [SME...]
  transfers between devices with their start and end apart: 4 -> 3, of which waited for: 4 -> 3; matrix products, arithmetic and copies ran while one was open for 0% -> 0% of each run, Pallas kernels for 6% -> 7%
where the time goes in v5:
time: 66.6 us; the launch traced here: 66.1 us
  blocking collectives  22.3 us (33%)
  starting transfers between devices  18.7 us (28%)
  waiting for transfers between devices  12 us (18%)
  Pallas kernels  11.7 us (18%)
  between operations  1.33 us (2%)
    all_to_all x1, blocking collectives, per_device(): lax.all_to_all(send, whole, 0, 0, axis_index_groups=pairs_of(seq_count))  12.3 us
    all_to_all x1, blocking collectives, per_device(): partials = lax.all_to_all(send, 'seq', 0, 0)  10.1 us
    all_to_all x1, starting transfers between devices, per_device(): every_total = lax.all_to_all(send, ('mp', 'dp'), 0, 0)  9.81 us
    all_to_all x1, waiting for transfers between devices, per_device(): every_total = lax.all_to_all(send, ('mp', 'dp'), 0, 0)  7.69 us
    all_to_all x1, starting transfers between devices, per_device(): every_latent = lax.all_to_all(send, 'seq', 0, 0)  5.79 us
    ppermute x1, starting transfers between devices, per_device(): lax.ppermute(gap, 'mp', [(slot_of(m, h), slot_of(m, 1 - h)) for m in rang...  3.14 us
    pallas_call x1, Pallas kernels, per_device(): call(attention_kernel, shape((2 * seq_count, 32, 128), BF16), [VMEM] * 3,...  2.66 us
    pallas_call x1, Pallas kernels, per_device(): call(latents_kernel, shape((seq_count, 64, tokens), BF16), [SMEM] + [HBM]...  2.63 us
  transfers between devices with their start and end apart: 3, of which 3 were waited for; matrix products, arithmetic and copies ran while one was open for 0% of the time, Pallas kernels for 7%

profile of v5, /device:TPU:32, one launch (start us, length us, event | category | flops | bytes accessed | tf_op | source)
XLA Modules:
  0.0 66.1 jit_solution(7555114770282566165)
XLA Ops:
  1.3 2.6 %latents.1 = bf16[16,64,128]{2,1,0:T(8,128)(2,1)} custom-call(s32[1]{0:T(128)S(6)} %copy.12.steps_ref, bf16[128,3072]{1,0:T(8,128)(2,1)} %bitcast.12, bf16[3072]{0:T(1024)(128)(2,1)} %gain_hbm.5, bf16[64,3072]{1,0:T(8,128)(2,1)} %bitcast.14, bf16[64,128]{1,0:T(8,128)(2,1)} %bitcast.17), custom_call_target="tpu_custom_call" | custom-call | flops 50331648 | bytes 786432 | tf_op jit(solution)/shard_map/latents/pallas_call | solution.py:349
  3.9 5.8 %all-to-all-start = ((bf16[16,64,128]{2,1,0:T(8,128)(2,1)}), bf16[16,64,128]{2,1,0:T(8,128)(2,1)S(1)}, u32[]{:S(2)}, u32[]{:S(2)}) async-start(bf16[16,64,128]{2,1,0:T(8,128)(2,1)} %latents.1), calls=%async_computation | async-start | bytes 524288 | tf_op jit(solution)/shard_map/all_to_all | solution.py:358
  9.7 2.0 %own.1 = (bf16[1536,128]{1,0:T(8,128)(2,1)S(1)}, f32[72,128]{1,0:T(8,128)S(1)}) custom-call(s32[1]{0:T(128)S(6)} %copy.12.steps_ref, bf16[128,3072]{1,0:T(8,128)(2,1)} %bitcast.13, bf16[3072]{0:T(1024)(128)(2,1)} %gain_hbm.5, bf16[64,3072]{1,0:T(8,128)(2,1)} %bitcast.15, bf16[64,128]{1,0:T(8,128)(2,1)} %bitcast.18), custom_call_target="tpu_custom_call" | custom-call | flops 50331648 | bytes 786432 | tf_op jit(solution)/shard_map/own/pallas_call | solution.py:379
  11.7 2.5 %fold.1 = (bf16[384,256]{1,0:T(8,128)(2,1)S(1)}, f32[136,128]{1,0:T(8,128)S(1)}) custom-call(s32[1]{0:T(128)S(6)} %copy.12.steps_ref, bf16[2,64,3072]{2,1,0:T(8,128)(2,1)} %embed_hbm.1, bf16[2,3072]{1,0:T(2,128)(2,1)} %gain_hbm.4, bf16[2,3,3072,128]{3,2,1,0:T(8,128)(2,1)} %bitcast.11, bf16[2,2,128]{2,1,0:T(2,128)(2,1)} %qk_hbm.1, bf16[2,64,2048]{2,1,0:T(8,128)(2,1)} %bitcast.16), custom_call_target="tpu_custom_call" | custom-call | flops 603979776 | bytes 2359296 | tf_op jit(solution)/shard_map/fold/pallas_call | solution.py:360
  14.3 2.2 %all-to-all-done.latent_ref = bf16[16,64,128]{2,1,0:T(8,128)(2,1)S(1)} async-done(((bf16[16,64,128]{2,1,0:T(8,128)(2,1)}), bf16[16,64,128]{2,1,0:T(8,128)(2,1)S(1)}, u32[]{:S(2)}, u32[]{:S(2)}) %all-to-all-start) | async-done | bytes 262176 | tf_op jit(solution)/shard_map/all_to_all | solution.py:358
  16.5 2.7 %attention.1 = bf16[32,32,128]{2,1,0:T(8,128)(2,1)S(1)} custom-call(bf16[16,64,128]{2,1,0:T(8,128)(2,1)S(1)} %all-to-all-done.latent_ref, bf16[384,256]{1,0:T(8,128)(2,1)S(1)} %get-tuple-element.18.fold_ref, f32[136,128]{1,0:T(8,128)S(1)} %get-tuple-element.19.scale_ref), custom_call_target="tpu_custom_call" | custom-call | flops 1073741824 | bytes 262144 | tf_op jit(solution)/shard_map/attention/pallas_call | solution.py:390
  19.2 12.3 %all_to_all.20.velocity_ref = bf16[32,32,128]{2,1,0:T(8,128)(2,1)S(1)} all-to-all(bf16[32,32,128]{2,1,0:T(8,128)(2,1)S(1)} %attention.1), channel_id=1, replica_groups={{0,4,8,12,16,20,24,28,32,36,40,44,48,52,56,60,64,68,72,76,80,84,88,92,9..., dimensions={0} | all-to-all | bytes 524288 | tf_op jit(solution)/shard_map/all_to_all | solution.py:403
  31.4 0.4 gap.1
  31.8 10.1 %all_to_all.21.grad_ref = bf16[16,56,128]{2,1,0:T(8,128)(2,1)S(1)} all-to-all(bf16[16,56,128]{2,1,0:T(8,128)(2,1)S(1)} %get-tuple-element.22), channel_id=1, replica_groups=mesh['mp'=4,'seq'=16,'dp'=4] {'seq'}, dimensions={0} | all-to-all | bytes 458752 | tf_op jit(solution)/shard_map/all_to_all | solution.py:413
  41.8 0.7 %total.1 = bf16[16,56,128]{2,1,0:T(8,128)(2,1)} custom-call(bf16[16,56,128]{2,1,0:T(8,128)(2,1)S(1)} %all_to_all.21.grad_ref), custom_call_target="tpu_custom_call" | custom-call | flops 114688 | bytes 229376 | tf_op jit(solution)/shard_map/total/pallas_call | solution.py:414
  42.6 9.8 %all-to-all-start.3 = ((bf16[16,56,128]{2,1,0:T(8,128)(2,1)}), bf16[16,56,128]{2,1,0:T(8,128)(2,1)S(1)}, u32[]{:S(2)}, u32[]{:S(2)}) async-start(bf16[16,56,128]{2,1,0:T(8,128)(2,1)} %total.1), calls=%async_computation.3 | async-start | bytes 458752 | tf_op jit(solution)/shard_map/all_to_all | solution.py:422
  52.4 3.1 %collective-permute-start = (f32[32,128]{1,0:T(8,128)S(1)}, f32[32,128]{1,0:T(8,128)S(1)}, u32[]{:S(2)}, u32[]{:S(2)}) collective-permute-start(f32[32,128]{1,0:T(8,128)S(1)} %get-tuple-element.23.gap_ref), channel_id=1, source_target_pairs={{0,192},{192,0},{64,128},{128,64},{1,193},{193,1},{65,129},{129,65... | collective-permute-start | bytes 49160 | tf_op jit(solution)/shard_map/ppermute | solution.py:412
  55.5 2.1 %collective-permute-done.other_ref = f32[32,128]{1,0:T(8,128)S(1)} collective-permute-done((f32[32,128]{1,0:T(8,128)S(1)}, f32[32,128]{1,0:T(8,128)S(1)}, u32[]{:S(2)}, u32[]{:S(2)}) %collective-permute-start) | collective-permute-done | bytes 16416 | tf_op jit(solution)/shard_map/ppermute | solution.py:412
  57.6 7.7 %all-to-all-done.3.all_ref = bf16[16,56,128]{2,1,0:T(8,128)(2,1)S(1)} async-done(((bf16[16,56,128]{2,1,0:T(8,128)(2,1)}), bf16[16,56,128]{2,1,0:T(8,128)(2,1)S(1)}, u32[]{:S(2)}, u32[]{:S(2)}) %all-to-all-start.3) | async-done | bytes 229408 | tf_op jit(solution)/shard_map/all_to_all | solution.py:422
  65.3 0.8 %result.1 = (f32[64,128]{1,0:T(8,128)}, f32[64,192]{1,0:T(8,128)}) custom-call(bf16[16,56,128]{2,1,0:T(8,128)(2,1)S(1)} %all-to-all-done.3.all_ref, f32[32,128]{1,0:T(8,128)S(1)} %get-tuple-element.23.gap_ref, f32[32,128]{1,0:T(8,128)S(1)} %collective-permute-done.other_ref), custom_call_target="tpu_custom_call" | custom-call | flops 49152 | bytes 98304 | tf_op jit(solution)/shard_map/result/pallas_call | solution.py:423
Async XLA Ops:
  3.9 12.6 %all-to-all-start = ((bf16[16,64,128]{2,1,0:T(8,128)(2,1)}), bf16[16,64,128]{2,1,0:T(8,128)(2,1)S(1)}, u32[]{:S(2)}, u32[]{:S(2)}) async-start(bf16[16,64,128]{2,1,0:T(8,128)(2,1)} %latents.1), calls=%async_computation | async-start | bytes 524288 | tf_op jit(solution)/shard_map/all_to_all | solution.py:358
  42.6 22.7 %all-to-all-start.3 = ((bf16[16,56,128]{2,1,0:T(8,128)(2,1)}), bf16[16,56,128]{2,1,0:T(8,128)(2,1)S(1)}, u32[]{:S(2)}, u32[]{:S(2)}) async-start(bf16[16,56,128]{2,1,0:T(8,128)(2,1)} %total.1), calls=%async_computation.3 | async-start | bytes 458752 | tf_op jit(solution)/shard_map/all_to_all | solution.py:422
  52.4 5.2 %collective-permute-start = (f32[32,128]{1,0:T(8,128)S(1)}, f32[32,128]{1,0:T(8,128)S(1)}, u32[]{:S(2)}, u32[]{:S(2)}) collective-permute-start(f32[32,128]{1,0:T(8,128)S(1)} %get-tuple-element.23.gap_ref), channel_id=1, source_target_pairs={{0,192},{192,0},{64,128},{128,64},{1,193},{193,1},{65,129},{129,65... | collective-permute-start | bytes 49160 | tf_op jit(solution)/shard_map/ppermute | solution.py:412

commit v6 on v5

--- a/solution.py
+++ b/solution.py
@@ -37,6 +37,11 @@
 
 def slot_of(model, half):
     return 2 * half + (model + half) % 2
+
+
+SEQ_ORDER = list(range(15, -1, -1))
+LAST_ORDER = list(range(15, -1, -1))
+MODEL_ORDER = [1, 0]
 
 
 def level_of(steps_ref):
@@ -124,7 +129,7 @@
     own_ref[64:72, :] = jnp.where(left, jnp.where(first, inverse, turned_row), jnp.where(first, turned_row, inverse))
     turned[...] = scaled.T
     for s in range(16):
-        start = pl.multiple_of(s * 192 + model * 96, 32)
+        start = pl.multiple_of(SEQ_ORDER[s] * 192 + model * 96, 32)
         picked_ref[s * 96 : (s + 1) * 96, :] = turned[pl.ds(start, 96), :]
 
 
@@ -210,7 +215,8 @@
     squares = scale_ref[128:129, 0:1]
 
     def hidden_square(inner, rows):
-        return (jnp.sum(inner * rows.astype(F32), axis=0, keepdims=True) + squares) / 3072.0 + 1e-06
+        total = jnp.sum(inner * rows.astype(F32), axis=0, keepdims=True) + squares
+        return jnp.maximum(total, 0.0) / 3072.0 + 1e-06
 
     projected = dot(fold_ref[0:256], latents[...])
     hidden = hidden_square(projected[192:256], latents[0:64])
@@ -241,8 +247,9 @@
 def gap_kernel(steps_ref, velocity_ref, picked_ref, own_ref, send_ref, gap_ref):
     level = level_of(steps_ref)
     _, _, half = place()
-    teacher = jnp.sum(velocity_ref[0:16].astype(F32), axis=0)
-    gap = level * (teacher - jnp.sum(velocity_ref[16:32].astype(F32), axis=0))
+    sums = [jnp.sum(velocity_ref[16 * i : 16 * i + 16].astype(F32), axis=0) for i in range(2)]
+    teacher = sums[MODEL_ORDER.index(0)]
+    gap = level * (teacher - sums[MODEL_ORDER.index(1)])
     gap_ref[...] = gap
     distance = jnp.abs(own_ref[0:32] - (own_ref[32:64] - level * teacher))
     spread = jnp.sum(jnp.sum(distance, axis=1, keepdims=True), axis=0, keepdims=True)
@@ -283,7 +290,7 @@
     totals = [jnp.zeros((48, 128), F32)] * 2
     mine = jnp.zeros((1, 128), F32)
     for d in range(4):
-        sums = [sum(all_ref[4 * slot_of(m, h) + d].astype(F32) for h in range(2)) for m in range(2)]
+        sums = [sum(all_ref[LAST_ORDER.index(slot_of(m, h) + 4 * d)].astype(F32) for h in range(2)) for m in range(2)]
         inverse = 1.0 / ((sums[0][48:49] + sums[0][49:50]) / 131072.0 + 1e-05)
         mine = jnp.where(sample == d, inverse, mine)
         totals = [total + one[0:48] * inverse for total, one in zip(totals, sums)]
@@ -319,7 +326,7 @@
 
 
 def pairs_of(seq_count):
-    return [[slot_of(m, half) * seq_count + s for m in range(2) for s in range(seq_count)] for half in range(2)]
+    return [[slot_of(m, half) * seq_count + s for m in MODEL_ORDER for s in SEQ_ORDER] for half in range(2)]
 
 
 def per_device(
@@ -355,7 +362,7 @@
         moved=2 * tokens * width,
         scratch_shapes=buffers + [pltpu.SemaphoreType.DMA((9,))],
     )(*local)
-    every_latent = lax.all_to_all(send, "seq", 0, 0)
+    every_latent = lax.all_to_all(send, "seq", 0, 0, axis_index_groups=[SEQ_ORDER])
 
     fold, scale = call(
         fold_kernel,
@@ -410,7 +417,7 @@
         moved=2 * 64 * 32 * 128,
     )(time_steps, velocities, picked, own)
     other = lax.ppermute(gap, "mp", [(slot_of(m, h), slot_of(m, 1 - h)) for m in range(2) for h in range(2)])
-    partials = lax.all_to_all(send, "seq", 0, 0)
+    partials = lax.all_to_all(send, "seq", 0, 0, axis_index_groups=[SEQ_ORDER])
     send = call(
         total_kernel,
         shape((group, 56, 128), BF16),
@@ -419,7 +426,7 @@
         flops=seq_count * 56 * 128,
         moved=2 * seq_count * 56 * 128,
     )(partials)
-    every_total = lax.all_to_all(send, ("mp", "dp"), 0, 0)
+    every_total = lax.all_to_all(send, ("dp", "mp"), 0, 0, axis_index_groups=[LAST_ORDER])
     dmd, grad = call(
         result_kernel,
         (shape((64, tokens), F32), shape((64, width // seq_count), F32)),

time: 66.6 us -> 60.7 us (0.911)
  waiting for transfers between devices: 12 us -> 8.04 us
  blocking collectives: 22.3 us -> 21 us
  starting transfers between devices: 18.7 us -> 17.5 us
    all_to_all x2, waiting for transfers between devices: 9.9 us -> 3.66 us  [the longest x1 2.56 us: per_device(): lax.all_to_all(send, ('dp', 'mp'), 0, 0, axis_index_groups=[LAST_ORDER])]
    ppermute x1, starting transfers between devices: 3.14 us -> 0.56 us  [per_device(): lax.ppermute(gap, 'mp', [(slot_of(m, h), slot_of(m, 1 - h)) for m in rang...]
    ppermute x1, waiting for transfers between devices: 2.07 us -> 4.39 us  [per_device(): lax.ppermute(gap, 'mp', [(slot_of(m, h), slot_of(m, 1 - h)) for m in rang...]
    all_to_all x1, blocking collectives: 12.3 us -> 10.7 us  [per_device(): lax.all_to_all(send, whole, 0, 0, axis_index_groups=pairs_of(seq_count))]
    all_to_all x2, starting transfers between devices: 15.6 us -> 16.9 us  [the longest x1 11.3 us: per_device(): lax.all_to_all(send, ('dp', 'mp'), 0, 0, axis_index_groups=[LAST_ORDER])]
  transfers between devices with their start and end apart: 3 -> 3, of which waited for: 3 -> 3; matrix products, arithmetic and copies ran while one was open for 0% -> 0% of each run, Pallas kernels for 7% -> 8%
where the time goes in v6:
time: 60.7 us; the launch traced here: 59.6 us
  blocking collectives  21 us (35%)
  starting transfers between devices  17.5 us (29%)
  Pallas kernels  11.7 us (19%)
  waiting for transfers between devices  8.04 us (13%)
  between operations  1.32 us (2%)
    all_to_all x1, starting transfers between devices, per_device(): lax.all_to_all(send, ('dp', 'mp'), 0, 0, axis_index_groups=[LAST_ORDER])  11.3 us
    all_to_all x1, blocking collectives, per_device(): lax.all_to_all(send, whole, 0, 0, axis_index_groups=pairs_of(seq_count))  10.7 us
    all_to_all x1, blocking collectives, per_device(): partials = lax.all_to_all(send, 'seq', 0, 0, axis_index_groups=[SEQ_ORDER])  10.3 us
    all_to_all x1, starting transfers between devices, per_device(): lax.all_to_all(send, 'seq', 0, 0, axis_index_groups=[SEQ_ORDER])  5.64 us
    ppermute x1, waiting for transfers between devices, per_device(): lax.ppermute(gap, 'mp', [(slot_of(m, h), slot_of(m, 1 - h)) for m in rang...  4.39 us
    pallas_call x1, Pallas kernels, per_device(): call(attention_kernel, shape((2 * seq_count, 32, 128), BF16), [VMEM] * 3,...  2.66 us
    pallas_call x1, Pallas kernels, per_device(): call(latents_kernel, shape((seq_count, 64, tokens), BF16), [SMEM] + [HBM]...  2.63 us
    all_to_all x1, waiting for transfers between devices, per_device(): lax.all_to_all(send, ('dp', 'mp'), 0, 0, axis_index_groups=[LAST_ORDER])  2.56 us
  transfers between devices with their start and end apart: 3, of which 3 were waited for; matrix products, arithmetic and copies ran while one was open for 0% of the time, Pallas kernels for 8%

profile of v6, /device:TPU:32, one launch (start us, length us, event | category | flops | bytes accessed | tf_op | source)
XLA Modules:
  0.0 59.6 jit_solution(1305675650602976242)
XLA Ops:
  1.3 2.6 %latents.1 = bf16[16,64,128]{2,1,0:T(8,128)(2,1)} custom-call(s32[1]{0:T(128)S(6)} %copy.12.steps_ref, bf16[128,3072]{1,0:T(8,128)(2,1)} %bitcast.12, bf16[3072]{0:T(1024)(128)(2,1)} %gain_hbm.5, bf16[64,3072]{1,0:T(8,128)(2,1)} %bitcast.14, bf16[64,128]{1,0:T(8,128)(2,1)} %bitcast.17), custom_call_target="tpu_custom_call" | custom-call | flops 50331648 | bytes 786432 | tf_op jit(solution)/shard_map/latents/pallas_call | solution.py:356
  3.9 5.6 %all-to-all-start = ((bf16[16,64,128]{2,1,0:T(8,128)(2,1)}), bf16[16,64,128]{2,1,0:T(8,128)(2,1)S(1)}, u32[]{:S(2)}, u32[]{:S(2)}) async-start(bf16[16,64,128]{2,1,0:T(8,128)(2,1)} %latents.1), calls=%async_computation | async-start | bytes 524288 | tf_op jit(solution)/shard_map/all_to_all | solution.py:365
  9.6 2.0 %own.1 = (bf16[1536,128]{1,0:T(8,128)(2,1)S(1)}, f32[72,128]{1,0:T(8,128)S(1)}) custom-call(s32[1]{0:T(128)S(6)} %copy.12.steps_ref, bf16[128,3072]{1,0:T(8,128)(2,1)} %bitcast.13, bf16[3072]{0:T(1024)(128)(2,1)} %gain_hbm.5, bf16[64,3072]{1,0:T(8,128)(2,1)} %bitcast.15, bf16[64,128]{1,0:T(8,128)(2,1)} %bitcast.18), custom_call_target="tpu_custom_call" | custom-call | flops 50331648 | bytes 786432 | tf_op jit(solution)/shard_map/own/pallas_call | solution.py:386
  11.6 2.5 %fold.1 = (bf16[384,256]{1,0:T(8,128)(2,1)S(1)}, f32[136,128]{1,0:T(8,128)S(1)}) custom-call(s32[1]{0:T(128)S(6)} %copy.12.steps_ref, bf16[2,64,3072]{2,1,0:T(8,128)(2,1)} %embed_hbm.1, bf16[2,3072]{1,0:T(2,128)(2,1)} %gain_hbm.4, bf16[2,3,3072,128]{3,2,1,0:T(8,128)(2,1)} %bitcast.11, bf16[2,2,128]{2,1,0:T(2,128)(2,1)} %qk_hbm.1, bf16[2,64,2048]{2,1,0:T(8,128)(2,1)} %bitcast.16), custom_call_target="tpu_custom_call" | custom-call | flops 603979776 | bytes 2359296 | tf_op jit(solution)/shard_map/fold/pallas_call | solution.py:367
  14.1 1.1 %all-to-all-done.latent_ref = bf16[16,64,128]{2,1,0:T(8,128)(2,1)S(1)} async-done(((bf16[16,64,128]{2,1,0:T(8,128)(2,1)}), bf16[16,64,128]{2,1,0:T(8,128)(2,1)S(1)}, u32[]{:S(2)}, u32[]{:S(2)}) %all-to-all-start) | async-done | bytes 262176 | tf_op jit(solution)/shard_map/all_to_all | solution.py:365
  15.2 2.7 %attention.1 = bf16[32,32,128]{2,1,0:T(8,128)(2,1)S(1)} custom-call(bf16[16,64,128]{2,1,0:T(8,128)(2,1)S(1)} %all-to-all-done.latent_ref, bf16[384,256]{1,0:T(8,128)(2,1)S(1)} %get-tuple-element.18.fold_ref, f32[136,128]{1,0:T(8,128)S(1)} %get-tuple-element.19.scale_ref), custom_call_target="tpu_custom_call" | custom-call | flops 1073741824 | bytes 262144 | tf_op jit(solution)/shard_map/attention/pallas_call | solution.py:397
  17.9 10.7 %all_to_all.20.velocity_ref = bf16[32,32,128]{2,1,0:T(8,128)(2,1)S(1)} all-to-all(bf16[32,32,128]{2,1,0:T(8,128)(2,1)S(1)} %attention.1), channel_id=1, replica_groups={{124,120,116,112,108,104,100,96,92,88,84,80,76,72,68,64,60,56,52,48,44,..., dimensions={0} | all-to-all | bytes 524288 | tf_op jit(solution)/shard_map/all_to_all | solution.py:410
  28.6 0.4 gap.1
  28.9 10.3 %all_to_all.21.grad_ref = bf16[16,56,128]{2,1,0:T(8,128)(2,1)S(1)} all-to-all(bf16[16,56,128]{2,1,0:T(8,128)(2,1)S(1)} %get-tuple-element.22), channel_id=1, replica_groups={{60,56,52,48,44,40,36,32,28,24,20,16,12,8,4,0},{61,57,53,49,45,41,37,33..., dimensions={0} | all-to-all | bytes 458752 | tf_op jit(solution)/shard_map/all_to_all | solution.py:420
  39.3 0.7 %total.1 = bf16[16,56,128]{2,1,0:T(8,128)(2,1)} custom-call(bf16[16,56,128]{2,1,0:T(8,128)(2,1)S(1)} %all_to_all.21.grad_ref), custom_call_target="tpu_custom_call" | custom-call | flops 114688 | bytes 229376 | tf_op jit(solution)/shard_map/total/pallas_call | solution.py:421
  40.0 11.3 %all-to-all-start.3 = ((bf16[16,56,128]{2,1,0:T(8,128)(2,1)}), bf16[16,56,128]{2,1,0:T(8,128)(2,1)S(1)}, u32[]{:S(2)}, u32[]{:S(2)}) async-start(bf16[16,56,128]{2,1,0:T(8,128)(2,1)} %total.1), calls=%async_computation.3 | async-start | bytes 458752 | tf_op jit(solution)/shard_map/all_to_all | solution.py:429
  51.3 0.6 collective-permute-start
  51.9 4.4 %collective-permute-done.other_ref = f32[32,128]{1,0:T(8,128)S(1)} collective-permute-done((f32[32,128]{1,0:T(8,128)S(1)}, f32[32,128]{1,0:T(8,128)S(1)}, u32[]{:S(2)}, u32[]{:S(2)}) %collective-permute-start) | collective-permute-done | bytes 16416 | tf_op jit(solution)/shard_map/ppermute | solution.py:419
  56.2 2.6 %all-to-all-done.3.all_ref = bf16[16,56,128]{2,1,0:T(8,128)(2,1)S(1)} async-done(((bf16[16,56,128]{2,1,0:T(8,128)(2,1)}), bf16[16,56,128]{2,1,0:T(8,128)(2,1)S(1)}, u32[]{:S(2)}, u32[]{:S(2)}) %all-to-all-start.3) | async-done | bytes 229408 | tf_op jit(solution)/shard_map/all_to_all | solution.py:429
  58.8 0.8 %result.1 = (f32[64,128]{1,0:T(8,128)}, f32[64,192]{1,0:T(8,128)}) custom-call(bf16[16,56,128]{2,1,0:T(8,128)(2,1)S(1)} %all-to-all-done.3.all_ref, f32[32,128]{1,0:T(8,128)S(1)} %get-tuple-element.23.gap_ref, f32[32,128]{1,0:T(8,128)S(1)} %collective-permute-done.other_ref), custom_call_target="tpu_custom_call" | custom-call | flops 49152 | bytes 98304 | tf_op jit(solution)/shard_map/result/pallas_call | solution.py:430
Async XLA Ops:
  3.9 11.3 %all-to-all-start = ((bf16[16,64,128]{2,1,0:T(8,128)(2,1)}), bf16[16,64,128]{2,1,0:T(8,128)(2,1)S(1)}, u32[]{:S(2)}, u32[]{:S(2)}) async-start(bf16[16,64,128]{2,1,0:T(8,128)(2,1)} %latents.1), calls=%async_computation | async-start | bytes 524288 | tf_op jit(solution)/shard_map/all_to_all | solution.py:365
  40.0 18.8 %all-to-all-start.3 = ((bf16[16,56,128]{2,1,0:T(8,128)(2,1)}), bf16[16,56,128]{2,1,0:T(8,128)(2,1)S(1)}, u32[]{:S(2)}, u32[]{:S(2)}) async-start(bf16[16,56,128]{2,1,0:T(8,128)(2,1)} %total.1), calls=%async_computation.3 | async-start | bytes 458752 | tf_op jit(solution)/shard_map/all_to_all | solution.py:429
  51.3 4.9 %collective-permute-start = (f32[32,128]{1,0:T(8,128)S(1)}, f32[32,128]{1,0:T(8,128)S(1)}, u32[]{:S(2)}, u32[]{:S(2)}) collective-permute-start(f32[32,128]{1,0:T(8,128)S(1)} %get-tuple-element.23.gap_ref), channel_id=1, source_target_pairs={{0,192},{192,0},{64,128},{128,64},{1,193},{193,1},{65,129},{129,65... | collective-permute-start | bytes 49160 | tf_op jit(solution)/shard_map/ppermute | solution.py:419

commit v7 on v6

--- a/solution.py
+++ b/solution.py
@@ -40,7 +40,7 @@
 
 
 SEQ_ORDER = list(range(15, -1, -1))
-LAST_ORDER = list(range(15, -1, -1))
+LAST_ORDER = [4 * d + m for d in (2, 3, 0, 1) for m in (3, 2, 1, 0)]
 MODEL_ORDER = [1, 0]
 
 
@@ -183,8 +183,12 @@
     mixed = dot(out[...], value_high, NT) + dot(out[...], value_low, NT)
     linear = inner[:, 64:65] + inner[:, 65:66] + inner[:, 66:67]
     inner = jnp.where(lane < 64, inner, jnp.where(lane == 64, 2.0 * linear, 0.0))
-    high, low = split_two(jnp.concatenate([stacked(1).T, mixed, inner, stacked(0).T], axis=0))
-    fold_ref[...] = jnp.concatenate([high, low], axis=1)
+    high, low = split_two(jnp.concatenate([stacked(1).T, mixed, inner, inner, stacked(0).T], axis=0))
+    whole = jnp.concatenate([high, low], axis=1)
+    rest = (inner - high[192:256].astype(F32) - low[192:256].astype(F32)).astype(BF16)
+    fold_ref[0:192, :] = whole[0:192]
+    fold_ref[192:256, :] = jnp.concatenate([rest, jnp.zeros((64, 128), BF16)], axis=1)
+    fold_ref[256:448, :] = whole[256:448]
     gains = qk[0:1, :].astype(F32) * qk[1:2, :].astype(F32) * (math.log2(math.e) / math.sqrt(128.0))
     scale_ref[0:128, :] = jnp.broadcast_to(gains, (128, 128)).T
     scale_ref[128:136, :] = jnp.broadcast_to(squares, (8, 128))
@@ -218,14 +222,14 @@
         total = jnp.sum(inner * rows.astype(F32), axis=0, keepdims=True) + squares
         return jnp.maximum(total, 0.0) / 3072.0 + 1e-06
 
-    projected = dot(fold_ref[0:256], latents[...])
-    hidden = hidden_square(projected[192:256], latents[0:64])
+    projected = dot(fold_ref[0:320], latents[...])
+    hidden = hidden_square(projected[192:256] + projected[256:320], latents[0:64])
     key = projected[0:128]
     key_scale = lax.rsqrt(jnp.mean(key * key, axis=0, keepdims=True) + 1e-06 * hidden)
     key = (key * key_scale).astype(BF16).T
     value = (projected[128:192] * lax.rsqrt(hidden)).astype(BF16)
     value = jnp.concatenate([value, jnp.ones((16, keys), BF16)], axis=0)
-    projected = dot(fold_ref[192:384], queries[...])
+    projected = dot(fold_ref[256:448], queries[...])
     hidden = hidden_square(projected[0:64], queries[0:64])
     query = projected[64:192]
     query_scale = lax.rsqrt(jnp.mean(query * query, axis=0, keepdims=True) + 1e-06 * hidden)
@@ -366,7 +370,7 @@
 
     fold, scale = call(
         fold_kernel,
-        (shape((384, 256), BF16), shape((136, 128), F32)),
+        (shape((448, 256), BF16), shape((136, 128), F32)),
         [SMEM] + [HBM] * 5,
         "fold",
         flops=2 * width * 384 * 256,

time: 60.7 us -> 60.2 us (level)
  waiting for transfers between devices: 8.04 us -> 6.51 us
  starting transfers between devices: 17.5 us -> 18.4 us
    all_to_all x1, waiting for transfers between devices: 2.56 us -> 0.52 us  [per_device(): lax.all_to_all(send, ('dp', 'mp'), 0, 0, axis_index_groups=[LAST_ORDER])]
    all_to_all x1, starting transfers between devices: 11.3 us -> 12.2 us  [per_device(): lax.all_to_all(send, ('dp', 'mp'), 0, 0, axis_index_groups=[LAST_ORDER])]
where the time goes in v7:
time: 60.2 us; the launch traced here: 59.1 us
  blocking collectives  21 us (35%)
  starting transfers between devices  18.4 us (31%)
  Pallas kernels  11.8 us (20%)
  waiting for transfers between devices  6.51 us (11%)
  between operations  1.32 us (2%)
    all_to_all x1, starting transfers between devices, per_device(): lax.all_to_all(send, ('dp', 'mp'), 0, 0, axis_index_groups=[LAST_ORDER])  12.2 us
    all_to_all x1, blocking collectives, per_device(): lax.all_to_all(send, whole, 0, 0, axis_index_groups=pairs_of(seq_count))  10.7 us
    all_to_all x1, blocking collectives, per_device(): partials = lax.all_to_all(send, 'seq', 0, 0, axis_index_groups=[SEQ_ORDER])  10.3 us
    all_to_all x1, starting transfers between devices, per_device(): lax.all_to_all(send, 'seq', 0, 0, axis_index_groups=[SEQ_ORDER])  5.64 us
    ppermute x1, waiting for transfers between devices, per_device(): lax.ppermute(gap, 'mp', [(slot_of(m, h), slot_of(m, 1 - h)) for m in rang...  4.9 us
    pallas_call x1, Pallas kernels, per_device(): call(attention_kernel, shape((2 * seq_count, 32, 128), BF16), [VMEM] * 3,...  2.73 us
    pallas_call x1, Pallas kernels, per_device(): call(latents_kernel, shape((seq_count, 64, tokens), BF16), [SMEM] + [HBM]...  2.63 us
    pallas_call x1, Pallas kernels, per_device(): call(fold_kernel, (shape((448, 256), BF16), shape((136, 128), F32)), [SME...  2.55 us
  transfers between devices with their start and end apart: 3, of which 3 were waited for; matrix products, arithmetic and copies ran while one was open for 0% of the time, Pallas kernels for 8%

profile of v7, /device:TPU:32, one launch (start us, length us, event | category | flops | bytes accessed | tf_op | source)
XLA Modules:
  0.0 59.1 jit_solution(4098788541145181715)
XLA Ops:
  1.3 2.6 %latents.1 = bf16[16,64,128]{2,1,0:T(8,128)(2,1)} custom-call(s32[1]{0:T(128)S(6)} %copy.12.steps_ref, bf16[128,3072]{1,0:T(8,128)(2,1)} %bitcast.12, bf16[3072]{0:T(1024)(128)(2,1)} %gain_hbm.5, bf16[64,3072]{1,0:T(8,128)(2,1)} %bitcast.14, bf16[64,128]{1,0:T(8,128)(2,1)} %bitcast.17), custom_call_target="tpu_custom_call" | custom-call | flops 50331648 | bytes 786432 | tf_op jit(solution)/shard_map/latents/pallas_call | solution.py:360
  3.9 5.6 %all-to-all-start = ((bf16[16,64,128]{2,1,0:T(8,128)(2,1)}), bf16[16,64,128]{2,1,0:T(8,128)(2,1)S(1)}, u32[]{:S(2)}, u32[]{:S(2)}) async-start(bf16[16,64,128]{2,1,0:T(8,128)(2,1)} %latents.1), calls=%async_computation | async-start | bytes 524288 | tf_op jit(solution)/shard_map/all_to_all | solution.py:369
  9.6 2.0 %own.1 = (bf16[1536,128]{1,0:T(8,128)(2,1)S(1)}, f32[72,128]{1,0:T(8,128)S(1)}) custom-call(s32[1]{0:T(128)S(6)} %copy.12.steps_ref, bf16[128,3072]{1,0:T(8,128)(2,1)} %bitcast.13, bf16[3072]{0:T(1024)(128)(2,1)} %gain_hbm.5, bf16[64,3072]{1,0:T(8,128)(2,1)} %bitcast.15, bf16[64,128]{1,0:T(8,128)(2,1)} %bitcast.18), custom_call_target="tpu_custom_call" | custom-call | flops 50331648 | bytes 786432 | tf_op jit(solution)/shard_map/own/pallas_call | solution.py:390
  11.6 2.5 %fold.1 = (bf16[448,256]{1,0:T(8,128)(2,1)S(1)}, f32[136,128]{1,0:T(8,128)S(1)}) custom-call(s32[1]{0:T(128)S(6)} %copy.12.steps_ref, bf16[2,64,3072]{2,1,0:T(8,128)(2,1)} %embed_hbm.1, bf16[2,3072]{1,0:T(2,128)(2,1)} %gain_hbm.4, bf16[2,3,3072,128]{3,2,1,0:T(8,128)(2,1)} %bitcast.11, bf16[2,2,128]{2,1,0:T(2,128)(2,1)} %qk_hbm.1, bf16[2,64,2048]{2,1,0:T(8,128)(2,1)} %bitcast.16), custom_call_target="tpu_custom_call" | custom-call | flops 603979776 | bytes 2359296 | tf_op jit(solution)/shard_map/fold/pallas_call | solution.py:371
  14.1 1.1 %all-to-all-done.latent_ref = bf16[16,64,128]{2,1,0:T(8,128)(2,1)S(1)} async-done(((bf16[16,64,128]{2,1,0:T(8,128)(2,1)}), bf16[16,64,128]{2,1,0:T(8,128)(2,1)S(1)}, u32[]{:S(2)}, u32[]{:S(2)}) %all-to-all-start) | async-done | bytes 262176 | tf_op jit(solution)/shard_map/all_to_all | solution.py:369
  15.2 2.7 %attention.1 = bf16[32,32,128]{2,1,0:T(8,128)(2,1)S(1)} custom-call(bf16[16,64,128]{2,1,0:T(8,128)(2,1)S(1)} %all-to-all-done.latent_ref, bf16[448,256]{1,0:T(8,128)(2,1)S(1)} %get-tuple-element.18.fold_ref, f32[136,128]{1,0:T(8,128)S(1)} %get-tuple-element.19.scale_ref), custom_call_target="tpu_custom_call" | custom-call | flops 1073741824 | bytes 262144 | tf_op jit(solution)/shard_map/attention/pallas_call | solution.py:401
  18.0 10.7 %all_to_all.20.velocity_ref = bf16[32,32,128]{2,1,0:T(8,128)(2,1)S(1)} all-to-all(bf16[32,32,128]{2,1,0:T(8,128)(2,1)S(1)} %attention.1), channel_id=1, replica_groups={{124,120,116,112,108,104,100,96,92,88,84,80,76,72,68,64,60,56,52,48,44,..., dimensions={0} | all-to-all | bytes 524288 | tf_op jit(solution)/shard_map/all_to_all | solution.py:414
  28.6 0.4 gap.1
  29.0 10.3 %all_to_all.21.grad_ref = bf16[16,56,128]{2,1,0:T(8,128)(2,1)S(1)} all-to-all(bf16[16,56,128]{2,1,0:T(8,128)(2,1)S(1)} %get-tuple-element.22), channel_id=1, replica_groups={{60,56,52,48,44,40,36,32,28,24,20,16,12,8,4,0},{61,57,53,49,45,41,37,33..., dimensions={0} | all-to-all | bytes 458752 | tf_op jit(solution)/shard_map/all_to_all | solution.py:424
  39.4 0.7 %total.1 = bf16[16,56,128]{2,1,0:T(8,128)(2,1)} custom-call(bf16[16,56,128]{2,1,0:T(8,128)(2,1)S(1)} %all_to_all.21.grad_ref), custom_call_target="tpu_custom_call" | custom-call | flops 114688 | bytes 229376 | tf_op jit(solution)/shard_map/total/pallas_call | solution.py:425
  40.1 12.2 %all-to-all-start.3 = ((bf16[16,56,128]{2,1,0:T(8,128)(2,1)}), bf16[16,56,128]{2,1,0:T(8,128)(2,1)S(1)}, u32[]{:S(2)}, u32[]{:S(2)}) async-start(bf16[16,56,128]{2,1,0:T(8,128)(2,1)} %total.1), calls=%async_computation.3 | async-start | bytes 458752 | tf_op jit(solution)/shard_map/all_to_all | solution.py:433
  52.3 0.6 collective-permute-start
  52.8 4.9 %collective-permute-done.other_ref = f32[32,128]{1,0:T(8,128)S(1)} collective-permute-done((f32[32,128]{1,0:T(8,128)S(1)}, f32[32,128]{1,0:T(8,128)S(1)}, u32[]{:S(2)}, u32[]{:S(2)}) %collective-permute-start) | collective-permute-done | bytes 16416 | tf_op jit(solution)/shard_map/ppermute | solution.py:423
  57.7 0.5 all-to-all-done.3.all_ref
  58.3 0.8 %result.1 = (f32[64,128]{1,0:T(8,128)}, f32[64,192]{1,0:T(8,128)}) custom-call(bf16[16,56,128]{2,1,0:T(8,128)(2,1)S(1)} %all-to-all-done.3.all_ref, f32[32,128]{1,0:T(8,128)S(1)} %get-tuple-element.23.gap_ref, f32[32,128]{1,0:T(8,128)S(1)} %collective-permute-done.other_ref), custom_call_target="tpu_custom_call" | custom-call | flops 49152 | bytes 98304 | tf_op jit(solution)/shard_map/result/pallas_call | solution.py:434
Async XLA Ops:
  3.9 11.3 %all-to-all-start = ((bf16[16,64,128]{2,1,0:T(8,128)(2,1)}), bf16[16,64,128]{2,1,0:T(8,128)(2,1)S(1)}, u32[]{:S(2)}, u32[]{:S(2)}) async-start(bf16[16,64,128]{2,1,0:T(8,128)(2,1)} %latents.1), calls=%async_computation | async-start | bytes 524288 | tf_op jit(solution)/shard_map/all_to_all | solution.py:369
  40.1 18.2 %all-to-all-start.3 = ((bf16[16,56,128]{2,1,0:T(8,128)(2,1)}), bf16[16,56,128]{2,1,0:T(8,128)(2,1)S(1)}, u32[]{:S(2)}, u32[]{:S(2)}) async-start(bf16[16,56,128]{2,1,0:T(8,128)(2,1)} %total.1), calls=%async_computation.3 | async-start | bytes 458752 | tf_op jit(solution)/shard_map/all_to_all | solution.py:433
  52.3 5.5 %collective-permute-start = (f32[32,128]{1,0:T(8,128)S(1)}, f32[32,128]{1,0:T(8,128)S(1)}, u32[]{:S(2)}, u32[]{:S(2)}) collective-permute-start(f32[32,128]{1,0:T(8,128)S(1)} %get-tuple-element.23.gap_ref), channel_id=1, source_target_pairs={{0,192},{192,0},{64,128},{128,64},{1,193},{193,1},{65,129},{129,65... | collective-permute-start | bytes 49160 | tf_op jit(solution)/shard_map/ppermute | solution.py:423
